TPU v7x, 32 devices: a whole 2x2x4 slice. The times are simulated.
32 devices in a mesh: dp: 32 (over z, y, x, core), ctx: 1.
Axes of the slice: x: 2, y: 2, z: 4, core: 2. Of those that a mesh axis runs over, the one named last changes fastest.
Arguments:
- query: bfloat16 [32, 128, 4096], P('dp', 'ctx'), may hold values from -128 to 128
- key: bfloat16 [32, 128, 1024], P('dp', 'ctx'), may hold values from -6 to 6
- value: bfloat16 [32, 128, 1024], P('dp', 'ctx'), may hold values from -6 to 6
- gate_input: bfloat16 [32, 128, 4096], P('dp', 'ctx'), may hold values from -6 to 6
- conv_weight: bfloat16 [4, 4096], P(None, 'dp'), may hold values from -3 to 3
- conv_bias: bfloat16 [4096], P('dp'), may hold values from -3 to 3
- x_proj: bfloat16 [4096, 288], P('dp'), may hold values from -0.375 to 0.375
- dt_proj: bfloat16 [256, 4096], P(None, 'dp'), may hold values from -0.375 to 0.375
- dt_bias: bfloat16 [4096], P('dp'), may hold values from -7 to -2.296875
- a_log: bfloat16 [16, 4096], P(None, 'dp'), may hold values from 0 to 2.765625
- d_skip: bfloat16 [4096], P('dp'), may hold values from 0.19921875 to 1
- out_proj: bfloat16 [4096, 2048], P('dp'), may hold values from -0.09375 to 0.09375
Outputs:
- result: bfloat16 [32, 128, 2048], P('dp', 'ctx')
All inputs are finite; a program needn't handle non-finite values.
Results may differ from a plain program's by a relative error of at most 0.008.
Values may be sent and summed in bfloat16 or wider, within the bound.
No kernel may reach another device: no remote copies, remote signals or barrier semaphores. Data moves between devices by JAX's collectives and lax.ppermute only.
A program may use at most 128 MiB of HBM per device.

v0:
```python
import math

import jax
import jax.numpy as jnp
from jax import lax
from jax.sharding import PartitionSpec as P

HEAD_SIZE = 128


def shifted(value, axis, steps):
    count = lax.axis_size(axis)
    initial, last = (max(0, -steps), min(count, count - steps))
    return lax.ppermute(value, axis, [(source, source + steps) for source in range(initial, last)])


def entering(shard, axis, combine, identity):
    size, position = (lax.axis_size(axis), lax.axis_index(axis))
    everything = jax.tree.map(lambda part: lax.all_gather(part, axis), shard)
    start = jax.tree.map(
        lambda part, zero: jnp.broadcast_to(jnp.asarray(zero, part.dtype), part.shape),
        shard,
        identity,
    )

    def hop(k, before):
        reached = k < position
        new = combine(before, jax.tree.map(lambda part: part[k], everything))
        return jax.tree.map(lambda a, b: jnp.where(reached, a, b), new, before)

    return lax.fori_loop(0, size, hop, start)


def attend_whole(queries, keys_all, values_all, group):
    seq_len, kv_local, head_dim = keys_all.shape
    scale = 1.0 / math.sqrt(head_dim)
    block = min(512, seq_len)
    pieces = []
    for index in range(seq_len // block):
        begin = index * block
        end = begin + block
        query_block = queries[begin:end].reshape(block, kv_local, group, head_dim)
        scores = (
            jnp.einsum(
                "rgqd,ngd->gqrn", query_block, keys_all[:end], preferred_element_type=jnp.float32
            )
            * scale
        )
        visible = jnp.arange(end)[None, :] <= (begin + jnp.arange(block))[:, None]
        scores = jnp.where(visible, scores, -jnp.inf)
        top = jnp.max(scores, axis=-1, keepdims=True)
        raised = jnp.exp(scores - top)
        total = jnp.sum(raised, axis=-1)
        mixed = jnp.einsum(
            "gqrn,ngd->rgqd",
            raised.astype(jnp.bfloat16),
            values_all[:end],
            preferred_element_type=jnp.float32,
        )
        mixed = mixed / jnp.transpose(total, (2, 0, 1))[..., None]
        pieces.append(mixed.astype(jnp.bfloat16).reshape(block, kv_local, group * head_dim))
    return jnp.concatenate(pieces, axis=0)


def chain_pass(initial, step_size, drive_term, input_gain, readout, decay_rate):
    tok_rows = step_size.shape[0]
    block_len = math.gcd(tok_rows, 32)
    blocks = tok_rows // block_len

    def advance(state, inputs):
        size_block, drive_block, gain_block, read_block = inputs
        outputs = []
        for position in range(block_len):
            state = jnp.exp(size_block[position][None, :] * decay_rate) * state
            state = state + gain_block[position][:, None] * drive_block[position][None, :]
            outputs.append(jnp.dot(read_block[position], state, precision=lax.Precision.HIGHEST))
        return (state, jnp.stack(outputs))

    inputs = tuple(
        (
            item.reshape((blocks, block_len) + item.shape[1:])
            for item in (step_size, drive_term, input_gain, readout)
        )
    )
    final, outputs = lax.scan(advance, initial, inputs)
    return (final, outputs.reshape(tok_rows, -1))


def carried_part(carried, step_size, readout, decay_rate):
    tok_rows, channels = step_size.shape
    lower = (jnp.arange(tok_rows)[:, None] >= jnp.arange(tok_rows)[None, :]).astype(jnp.float32)
    cumulative = jnp.dot(lower, step_size, precision=lax.Precision.HIGHEST)
    block_len = math.gcd(tok_rows, 32)
    blocks = tok_rows // block_len
    cum_blocks = cumulative.reshape(blocks, block_len, channels)
    read_blocks = readout.reshape(blocks, block_len, readout.shape[1])

    def one_block(items):
        cum_block, read_block = items
        factor = jnp.exp(cum_block[:, None, :] * decay_rate[None])
        return jnp.sum(read_block[:, :, None] * factor * carried[None], axis=1)

    return lax.map(one_block, (cum_blocks, read_blocks)).reshape(tok_rows, channels)


def shards(
    query,
    key,
    value,
    gate_input,
    conv_weight,
    conv_bias,
    x_proj,
    dt_proj,
    dt_bias,
    a_log,
    d_skip,
    out_proj,
):
    tok_rows = query.shape[1]
    feature_width = query.shape[2]
    head_dim = HEAD_SIZE
    kv_heads = key.shape[2] // head_dim
    group = feature_width // key.shape[2]
    queries = query[0].reshape(tok_rows, kv_heads, group * head_dim)
    key_rows = key[0].reshape(tok_rows, kv_heads, head_dim)
    value_rows = value[0].reshape(tok_rows, kv_heads, head_dim)
    gathered_queries, gathered_keys, gathered_values = (
        lax.all_to_all(queries, "ctx", split_axis=1, concat_axis=0, tiled=True),
        lax.all_to_all(key_rows, "ctx", split_axis=1, concat_axis=0, tiled=True),
        lax.all_to_all(value_rows, "ctx", split_axis=1, concat_axis=0, tiled=True),
    )
    mixed = lax.all_to_all(
        attend_whole(gathered_queries, gathered_keys, gathered_values, group),
        "ctx",
        split_axis=0,
        concat_axis=1,
        tiled=True,
    )
    layer_input = mixed.reshape(tok_rows, feature_width)
    filter_taps, filter_bias, input_weight, step_weight, step_bias, decay_log, skip_gain = (
        lax.all_gather(conv_weight, "dp", axis=1, tiled=True),
        lax.all_gather(conv_bias, "dp", axis=0, tiled=True),
        lax.all_gather(x_proj, "dp", axis=0, tiled=True),
        lax.all_gather(dt_proj, "dp", axis=1, tiled=True),
        lax.all_gather(dt_bias, "dp", axis=0, tiled=True),
        lax.all_gather(a_log, "dp", axis=1, tiled=True),
        lax.all_gather(d_skip, "dp", axis=0, tiled=True),
    )
    taps = filter_taps.shape[0]
    earlier = shifted(layer_input[tok_rows - (taps - 1) :], "ctx", 1)
    padded = jnp.concatenate([earlier, layer_input], axis=0).astype(jnp.float32)
    filtered = filter_bias.astype(jnp.float32)[None, :]
    for tap in range(taps):
        filtered = (
            filtered + filter_taps[tap].astype(jnp.float32)[None, :] * padded[tap : tap + tok_rows]
        )
    smoothed = jax.nn.silu(filtered).astype(jnp.bfloat16)
    projected = jnp.dot(smoothed, input_weight, preferred_element_type=jnp.float32)
    rank = step_weight.shape[0]
    states = decay_log.shape[0]
    low_rank = projected[:, :rank]
    normed = (
        low_rank * lax.rsqrt(jnp.mean(low_rank * low_rank, axis=-1, keepdims=True) + 1e-06)
    ).astype(jnp.bfloat16)
    step_size = jax.nn.softplus(
        jnp.dot(normed, step_weight, preferred_element_type=jnp.float32)
        + step_bias.astype(jnp.float32)[None, :]
    )
    input_gain = projected[:, rank : rank + states]
    readout = projected[:, rank + states : rank + 2 * states]
    decay_rate = -jnp.exp(decay_log.astype(jnp.float32))
    smooth_float = smoothed.astype(jnp.float32)
    drive_term = step_size * smooth_float
    empty_state = jnp.zeros((states, feature_width), jnp.float32)
    end_state, local_out = chain_pass(
        empty_state, step_size, drive_term, input_gain, readout, decay_rate
    )
    total_decay = jnp.exp(decay_rate * jnp.sum(step_size, axis=0)[None, :])

    def combine(earlier_pair, later_pair):
        return (earlier_pair[0] * later_pair[0], later_pair[0] * earlier_pair[1] + later_pair[1])

    _, carried = entering(
        (total_decay, end_state),
        "ctx",
        combine,
        (jnp.ones_like(total_decay), jnp.zeros_like(end_state)),
    )
    carried_out = carried_part(carried, step_size, readout, decay_rate)
    scan_out = local_out + carried_out + skip_gain.astype(jnp.float32)[None, :] * smooth_float
    gated = (scan_out * jax.nn.silu(gate_input[0].astype(jnp.float32))).astype(jnp.bfloat16)
    piece = lax.all_gather(out_proj, "dp", axis=0, tiled=True)
    columns = lax.slice_in_dim(gated, 0, piece.shape[0], axis=1)
    result = jnp.zeros((tok_rows, out_proj.shape[1]), jnp.float32) + jnp.dot(
        columns, piece, preferred_element_type=jnp.float32
    )
    return result.astype(jnp.bfloat16)[None]


def solution(mesh):
    placed = (
        P("dp", "ctx", None),
        P("dp", "ctx", None),
        P("dp", "ctx", None),
        P("dp", "ctx", None),
        P(None, "dp"),
        P("dp"),
        P("dp", None),
        P(None, "dp"),
        P("dp"),
        P(None, "dp"),
        P("dp"),
        P("dp", None),
    )
    return jax.shard_map(
        shards, mesh=mesh, in_specs=placed, out_specs=P("dp", "ctx", None), check_vma=False
    )
```

profile of v0, /device:TPU:0, one launch (start us, length us, event | category | flops | bytes accessed | tf_op | source)
XLA Modules:
  0.0 446.2 jit_solution(490256342105738042)
XLA Ops:
  8.1 2.6 reshape_reshape_squeeze.3
  10.8 1.9 fusion.114
  15.8 43.3 %all_gather.29 = bf16[4,4096]{1,0:T(4,128)(2,1)S(1)} all-gather(bf16[4,128]{1,0:T(4,128)(2,1)S(1)} %copy-done.38), channel_id=1, replica_groups=mesh['dp'=32,'ctx'=1] {'dp'}, dimensions={1}, use_global_device_ids=true | all-gather | bytes 33792 | tf_op jit(solution)/shard_map/all_gather | solution.py:142
  59.2 37.1 %all_gather.33 = bf16[16,4096]{1,0:T(8,128)(2,1)S(1)} all-gather(bf16[16,128]{1,0:T(8,128)(2,1)S(1)} %copy-done.37), channel_id=1, replica_groups=mesh['dp'=32,'ctx'=1] {'dp'}, dimensions={1}, use_global_device_ids=true | all-gather | bytes 135168 | tf_op jit(solution)/shard_map/all_gather | solution.py:147
  99.4 37.8 %all-gather = bf16[32,1,128]{2,1,0:T(2,128)(2,1)S(1)} all-gather(bf16[1,1,128]{2,1,0:T(2,128)(2,1)S(1)} %bitcast.879), channel_id=1, replica_groups=mesh['dp'=32,'ctx'=1] {'dp'}, dimensions={0}, use_global_device_ids=true | all-gather | bytes 8448 | tf_op jit(solution)/shard_map/all_gather | solution.py:143
  137.3 36.9 %all-gather.1 = bf16[32,1,128]{2,1,0:T(2,128)(2,1)S(1)} all-gather(bf16[1,1,128]{2,1,0:T(2,128)(2,1)S(1)} %bitcast.880), channel_id=1, replica_groups=mesh['dp'=32,'ctx'=1] {'dp'}, dimensions={0}, use_global_device_ids=true | all-gather | bytes 8448 | tf_op jit(solution)/shard_map/all_gather | solution.py:146
  174.2 38.4 %all-gather.2 = bf16[32,1,128]{2,1,0:T(2,128)(2,1)S(1)} all-gather(bf16[1,1,128]{2,1,0:T(2,128)(2,1)S(1)} %bitcast.881), channel_id=1, replica_groups=mesh['dp'=32,'ctx'=1] {'dp'}, dimensions={0}, use_global_device_ids=true | all-gather | bytes 8448 | tf_op jit(solution)/shard_map/all_gather | solution.py:148
  214.8 2.3 multiply_convert_fusion
  217.1 2.8 fusion.124
  220.0 4.8 %convert_multiply_fusion.2 = (f32[128,4096]{1,0:T(8,128)}, f32[128,4096]{1,0:T(8,128)S(1)}) fusion(bf16[128,4096]{1,0:T(8,128)(2,1)} %multiply_convert_fusion, f32[4096]{0:T(1024)S(1)} %bitcast.876, bf16[256,4096]{1,0:T(8,128)(2,1)} %all-gather.9.cloned.1.call-done, f32[128,288]{0,1:T(8,128)S(1)} %fusion.124, f32[128]{0:T(128)S(1)} %add_rsqrt_fusion), kind=kOutput, calls=%fused_computation.261 | convolution fusion | flops 273219584 | bytes 7488000 | tf_op jit(solution)/shard_map/dot_general | solution.py:167
  224.8 2.5 fusion.112
  229.0 18.9 %while.29 = (s32[]{:T(128)}, f32[4,32,4096]{2,1,0:T(8,128)}, f32[4,32,16]{1,0,2:T(4,128)S(1)}, f32[4,32,4096]{2,1,0:T(8,128)}, f32[16,4096]{1,0:T(8,128)S(1)}, /*index=5*/s32[]{:T(128)}) while((s32[]{:T(128)}, f32[4,32,4096]{2,1,0:T(8,128)}, f32[4,32,16]{1,0,2:T(4,128)S(1)}, f32[4,32,4096]{2,1,0:T(8,128)}, f32[16,4096]{1,0:T(8,128)S(1)}, ...), condition=%wide.region_7.8_spmd, body=%wide.region_5.7_spmd.sunk | while | flops 8257538 | bytes 3418701 | solution.py:103
  230.2 2.7 multiply_reduce_fusion.3
  234.9 2.7 multiply_reduce_fusion.3
  239.6 2.7 multiply_reduce_fusion.3
  244.3 2.7 multiply_reduce_fusion.3
  250.2 174.5 %while.30 = (s32[]{:T(128)}, f32[16,4096]{1,0:T(8,128)S(1)}, f32[4,32,4096]{2,1,0:T(8,128)}, f32[4,32,4096]{2,1,0:T(8,128)}, f32[16,4096]{1,0:T(8,128)S(1)}, /*i...) while((s32[]{:T(128)}, f32[16,4096]{1,0:T(8,128)S(1)}, ...), condition=%wide.region_4.5_spmd.clone, body=%wide.region_3.4_spmd.clone.sunk | while | flops 45219872 | bytes 24533304 | solution.py:85
  250.2 2.2 constant_dynamic-slice_fusion.138
  252.4 2.9 constant_dynamic-slice_fusion.140
  255.4 1.7 fusion.291
  258.5 2.3 constant_dynamic-slice_fusion.139
  260.8 2.1 constant_dynamic-slice_fusion.137
  263.9 3.1 multiply_add_fusion.113
  289.1 3.8 stack.133
  293.8 2.4 constant_dynamic-slice_fusion.138
  296.2 3.1 constant_dynamic-slice_fusion.140
  299.3 1.7 fusion.291
  302.4 2.2 constant_dynamic-slice_fusion.139
  304.6 2.1 constant_dynamic-slice_fusion.137
  307.8 3.1 multiply_add_fusion.113
  333.0 3.8 stack.133
  337.6 2.2 constant_dynamic-slice_fusion.138
  339.9 2.9 constant_dynamic-slice_fusion.140
  342.8 1.7 fusion.291
  345.9 2.1 constant_dynamic-slice_fusion.139
  348.0 2.1 constant_dynamic-slice_fusion.137
  351.2 3.1 multiply_add_fusion.113
  376.4 3.8 stack.133
  381.1 2.4 constant_dynamic-slice_fusion.138
  383.5 2.8 constant_dynamic-slice_fusion.140
  386.3 1.7 fusion.291
  389.4 2.2 constant_dynamic-slice_fusion.139
  391.7 2.1 constant_dynamic-slice_fusion.137
  394.9 3.1 multiply_add_fusion.113
  420.1 3.8 stack.133
  424.8 2.6 add.179
  427.4 3.0 fusion.95
  430.4 9.2 %fusion.92 = bf16[1,128,2048]{2,1,0:T(8,128)(2,1)} fusion(bf16[128,4096]{1,0:T(8,128)(2,1)} %fusion.95, bf16[4096,2048]{1,0:T(8,128)(2,1)} %all-gather.11.cloned.1.call-done), kind=kOutput, calls=%fused_computation.263 | convolution fusion | flops 2147745792 | bytes 18350080 | tf_op jit(solution)/shard_map/dot_general | solution.py:195
  (403 shorter events, 122.2 us)
Async XLA Ops:
  6.5 4.1 copy-start.3
  6.5 4.2 copy-start.4
  6.5 210.6 %all-gather.7.cloned.1.call-start = ((), (), s32[]{:S(2)}) async-start(), calls=%async_computation | async-start | bytes 2433024 | tf_op jit(solution)/shard_map/all_gather | solution.py:144
  7.3 212.7 %all-gather.9.cloned.1.call-start = ((), (), s32[]{:S(2)}) async-start(), calls=%async_computation.1 | async-start | bytes 2162688 | tf_op jit(solution)/shard_map/all_gather | solution.py:145
  8.0 422.4 %all-gather.11.cloned.1.call-start = ((), (), s32[]{:S(2)}) async-start(), calls=%async_computation.2 | async-start | bytes 17301504 | tf_op jit(solution)/shard_map/all_gather | solution.py:193
  13.0 46.2 %copy-start.37 = (bf16[16,128]{1,0:T(8,128)(2,1)S(1)}, bf16[16,128]{1,0:T(8,128)(2,1)}, u32[]{:S(2)}) copy-start(bf16[16,128]{1,0:T(8,128)(2,1)} %param.25) | copy-start | bytes 12292
  15.1 198.0 %collective-permute-start = (bf16[3,4096]{1,0:T(4,128)(2,1)S(1)}, bf16[3,4096]{1,0:T(4,128)(2,1)S(1)}, u32[]{:S(2)}, u32[]{:S(2)}) collective-permute-start(bf16[3,4096]{1,0:T(4,128)(2,1)S(1)} %bitcast.877), channel_id=1, source_target_pairs={} | collective-permute-start | bytes 73736 | tf_op jit(solution)/shard_map/ppermute | solution.py:14
  96.3 118.4 %copy-start.14 = (f32[1,4096]{1,0:T(1,128)}, f32[1,4096]{1,0:T(1,128)S(1)}, u32[]{:S(2)}) copy-start(f32[1,4096]{1,0:T(1,128)S(1)} %get-tuple-element.358) | copy-start | bytes 49156
  96.3 118.4 %copy-start.16 = (f32[1,4096]{1,0:T(1,128)}, f32[1,4096]{1,0:T(1,128)S(1)}, u32[]{:S(2)}) copy-start(f32[1,4096]{1,0:T(1,128)S(1)} %get-tuple-element.359) | copy-start | bytes 49156
  96.4 118.4 %copy-start.18 = (f32[1,4096]{1,0:T(1,128)}, f32[1,4096]{1,0:T(1,128)S(1)}, u32[]{:S(2)}) copy-start(f32[1,4096]{1,0:T(1,128)S(1)} %get-tuple-element.360) | copy-start | bytes 49156
  96.4 118.4 %copy-start.20 = (f32[1,4096]{1,0:T(1,128)}, f32[1,4096]{1,0:T(1,128)S(1)}, u32[]{:S(2)}) copy-start(f32[1,4096]{1,0:T(1,128)S(1)} %get-tuple-element.361) | copy-start | bytes 49156
  96.4 40.9 %copy-start.40 = (bf16[128]{0:T(256)(128)(2,1)S(1)}, bf16[128]{0:T(256)(128)(2,1)}, u32[]{:S(2)}) copy-start(bf16[128]{0:T(256)(128)(2,1)} %param.24) | copy-start | bytes 772
  96.4 77.8 %copy-start.41 = (bf16[128]{0:T(256)(128)(2,1)S(1)}, bf16[128]{0:T(256)(128)(2,1)}, u32[]{:S(2)}) copy-start(bf16[128]{0:T(256)(128)(2,1)} %param.26) | copy-start | bytes 772
  137.3 79.8 %copy-start.12 = (f32[32,1,128]{2,1,0:T(1,128)}, f32[32,1,128]{2,1,0:T(1,128)S(1)}, u32[]{:S(2)}) copy-start(f32[32,1,128]{2,1,0:T(1,128)S(1)} %convert_element_type.66) | copy-start | bytes 49156
  262.9 4.2 copy-start.28
  263.9 4.6 %copy-start.10 = (f32[1,1,16]{1,0,2:T(1,128)S(1)}, f32[1,1,16]{1,0,2:T(1,128)}, u32[]{:S(2)}) copy-start(f32[1,1,16]{1,0,2:T(1,128)} %get-tuple-element.714) | copy-start | bytes 196 | tf_op jit(solution)/shard_map/while
  267.1 3.9 copy-start.8
  268.5 3.7 copy-start.7
  268.5 3.7 copy-start.25
  268.5 3.7 copy-start.31
  268.5 3.8 copy-start.32
  269.5 3.8 copy-start.6
  270.9 3.7 copy-start.30
  306.7 4.2 copy-start.28
  307.8 4.6 %copy-start.10 = (f32[1,1,16]{1,0,2:T(1,128)S(1)}, f32[1,1,16]{1,0,2:T(1,128)}, u32[]{:S(2)}) copy-start(f32[1,1,16]{1,0,2:T(1,128)} %get-tuple-element.714) | copy-start | bytes 196 | tf_op jit(solution)/shard_map/while
  310.9 3.9 copy-start.8
  312.4 3.7 copy-start.25
  312.4 3.7 copy-start.31
  312.4 3.8 copy-start.32
  313.4 3.8 copy-start.6
  314.8 3.7 copy-start.30
  350.1 4.2 copy-start.28
  351.2 4.6 %copy-start.10 = (f32[1,1,16]{1,0,2:T(1,128)S(1)}, f32[1,1,16]{1,0,2:T(1,128)}, u32[]{:S(2)}) copy-start(f32[1,1,16]{1,0,2:T(1,128)} %get-tuple-element.714) | copy-start | bytes 196 | tf_op jit(solution)/shard_map/while
  354.4 3.9 copy-start.8
  355.8 3.7 copy-start.25
  355.8 3.7 copy-start.31
  355.8 3.8 copy-start.32
  356.8 3.8 copy-start.6
  358.2 3.7 copy-start.30
  393.8 4.2 copy-start.28
  394.9 4.6 %copy-start.10 = (f32[1,1,16]{1,0,2:T(1,128)S(1)}, f32[1,1,16]{1,0,2:T(1,128)}, u32[]{:S(2)}) copy-start(f32[1,1,16]{1,0,2:T(1,128)} %get-tuple-element.714) | copy-start | bytes 196 | tf_op jit(solution)/shard_map/while
  398.1 3.9 copy-start.8
  399.5 3.7 copy-start.7
  399.5 3.7 copy-start.25
  399.5 3.7 copy-start.31
  399.5 3.8 copy-start.32
  400.5 3.8 copy-start.6
  401.9 3.7 copy-start.30
  (61 other events, 196.1 us)
Sparse Core Ops, SparseCore 0:
  10.2 58.5 all-gather.6
  71.7 50.8 all-gather.8
  125.5 113.8 all-gather.10
where the time goes:
time: 449 us; the launch traced here: 446 us
  blocking collectives  193 us (43%)
  matrix products  109 us (24%)
  local copies, waits for them, and re-layouts  92.6 us (21%)
  other arithmetic  33.7 us (8%)
  between operations  13.5 us (3%)
    dot_general x128, matrix products, advance(): jnp.dot(read_block[position], state, precision=lax.Precision.HIGHEST)  86.7 us
    all_gather x1, blocking collectives, shards(): lax.all_gather(conv_weight, 'dp', axis=1, tiled=True)  43.3 us
    all_gather x1, blocking collectives, shards(): lax.all_gather(d_skip, 'dp', axis=0, tiled=True)  38.4 us
    all_gather x1, blocking collectives, shards(): lax.all_gather(conv_bias, 'dp', axis=0, tiled=True)  37.8 us
    all_gather x1, blocking collectives, shards(): lax.all_gather(a_log, 'dp', axis=1, tiled=True)  37.1 us
    all_gather x1, blocking collectives, shards(): lax.all_gather(dt_bias, 'dp', axis=0, tiled=True)  36.9 us
    slice x8, local copies, waits for them, and re-layouts, advance(): state = jnp.exp(size_block[position][None, :] * decay_rate) * state  20.7 us
    slice x8, local copies, waits for them, and re-layouts, advance(): drive_block[position][None, :]  17.6 us
  transfers between devices with their start and end apart: 4, of which 0 were waited for; matrix products, arithmetic and copies ran while one was open for 50% of the time, Pallas kernels for 0%

commit v1 on v0

--- a/solution.py
+++ b/solution.py
@@ -1,8 +1,11 @@
+import functools
 import math
 
 import jax
 import jax.numpy as jnp
 from jax import lax
+from jax.experimental import pallas as pl
+from jax.experimental.pallas import tpu as pltpu
 from jax.sharding import PartitionSpec as P
 
 HEAD_SIZE = 128
@@ -198,6 +201,275 @@
     return result.astype(jnp.bfloat16)[None]
 
 
+HEAD = HEAD_SIZE
+RANK = 256
+STATES = 16
+TAPS = 4
+EPS = 1e-06
+LOG2E = 1.4426950408889634
+GROUP = 4
+XW, DT, AL, MISC, PACK_ROWS = 0, 288, 544, 560, 576
+
+
+def swap(value, distance, count):
+    return lax.ppermute(value, "dp", [(i, i ^ distance) for i in range(count)])
+
+
+def local_call(kernel, out_shape, name, scratch=(), flops=0, bytes_accessed=0, transcendentals=0):
+    def call(*args):
+        return pl.pallas_call(
+            kernel,
+            out_shape=out_shape,
+            in_specs=[pl.BlockSpec(memory_space=pltpu.VMEM)] * len(args),
+            out_specs=jax.tree.map(lambda _: pl.BlockSpec(memory_space=pltpu.VMEM), out_shape),
+            scratch_shapes=list(scratch),
+            name=name,
+            cost_estimate=pl.CostEstimate(
+                flops=flops, bytes_accessed=bytes_accessed, transcendentals=transcendentals
+            ),
+            compiler_params=pltpu.CompilerParams(vmem_limit_bytes=48 * 1024 * 1024),
+        )(*args)
+
+    return call
+
+
+def attention_kernel(q_ref, k_ref, v_ref, g_ref, keep_ref, send_ref, gkeep_ref, gsend_ref):
+    position = lax.axis_index("dp")
+    member, block = position % GROUP, position // GROUP
+    rows = q_ref.shape[0]
+    scale = 1.0 / math.sqrt(HEAD)
+    row = lax.broadcasted_iota(jnp.int32, (GROUP, rows, rows), 1).reshape(GROUP * rows, rows)
+    col = lax.broadcasted_iota(jnp.int32, (GROUP * rows, rows), 1)
+    visible = col <= row
+
+    def lanes(index):
+        return pl.ds(pl.multiple_of(index * HEAD, HEAD), HEAD)
+
+    for slot in range(8):
+        kv = block ^ slot
+        heads = [kv * GROUP + (member ^ j) for j in range(GROUP)]
+        stacked = jnp.concatenate([q_ref[:, lanes(h)] for h in heads], axis=0)
+        keys = k_ref[:, lanes(kv)]
+        values = v_ref[:, lanes(kv)]
+        scores = lax.dot_general(
+            stacked, keys, (((1,), (1,)), ((), ())), preferred_element_type=jnp.float32
+        )
+        scores = jnp.where(visible, scores * scale, -jnp.inf)
+        top = jnp.max(scores, axis=-1, keepdims=True)
+        raised = jnp.exp(scores - top)
+        total = jnp.sum(raised, axis=-1, keepdims=True)
+        mixed = jnp.dot(raised.astype(jnp.bfloat16), values, preferred_element_type=jnp.float32)
+        mixed = (mixed / total).astype(jnp.bfloat16)
+        here = slice(slot * HEAD, (slot + 1) * HEAD)
+        for j in range(GROUP):
+            target = send_ref if j % 2 else keep_ref
+            gtarget = gsend_ref if j % 2 else gkeep_ref
+            target[j // 2, :, here] = mixed[j * rows : (j + 1) * rows]
+            gtarget[j // 2, :, here] = g_ref[:, lanes(heads[j])]
+
+
+def project_kernel(*refs):
+    packs, (keep_ref, recv_ref, x1_ref, x2_ref), rest = refs[:8], refs[8:12], refs[12:]
+    smooth_ref, pkeep_ref, psend_ref, weight_ref = rest
+    rows = keep_ref.shape[1]
+    row = lax.broadcasted_iota(jnp.int32, (rows, HEAD), 0)
+    masks = [row >= k for k in range(TAPS)]
+    sources = [keep_ref.at[0], recv_ref.at[0], x1_ref.at[0], x2_ref.at[0]]
+    for slot in range(8):
+        here = slice(slot * HEAD, (slot + 1) * HEAD)
+        weight_ref[:, here] = packs[slot][XW : XW + 288, :]
+        misc = packs[slot][MISC : MISC + 16, :].astype(jnp.float32)
+        for j in range(GROUP):
+            mixed = sources[j][:, here].astype(jnp.float32)
+            filtered = misc[4:5] + jnp.zeros_like(mixed)
+            for tap in range(TAPS):
+                shift = TAPS - 1 - tap
+                moved = mixed
+                if shift:
+                    moved = jnp.where(masks[shift], pltpu.roll(mixed, shift, 0), 0.0)
+                filtered = filtered + misc[tap : tap + 1] * moved
+            smooth = filtered / (1.0 + jnp.exp(-filtered))
+            smooth_ref[j, :, here] = smooth.astype(jnp.bfloat16)
+    for j in range(GROUP):
+        part = lax.dot_general(
+            smooth_ref[j],
+            weight_ref[...],
+            (((1,), (1,)), ((), ())),
+            preferred_element_type=jnp.float32,
+        )
+        target = psend_ref if j % 2 else pkeep_ref
+        half = j // 2
+        target[:, half * 256 : half * 256 + 256] = part[:, :256]
+        target[:, 512 + half * 32 : 512 + half * 32 + 32] = part[:, 256:288]
+
+
+def scan_kernel(half, *refs):
+    packs, (f0_ref, f1_ref, smooth_ref, ga_ref, gb_ref), rest = refs[:8], refs[8:13], refs[13:]
+    gated_ref, size_ref, drive_ref, out_ref, rate_ref, gain_ref, read_ref = rest
+    rows = f0_ref.shape[0]
+    sources = [f0_ref, f1_ref]
+    gates = [ga_ref, gb_ref]
+    for s in range(2):
+        low = sources[s][:, half * 256 : half * 256 + 256]
+        normed = low * lax.rsqrt(jnp.mean(low * low, axis=-1, keepdims=True) + EPS)
+        normed = normed.astype(jnp.bfloat16)
+        both = sources[s][:, 512 + half * 32 : 512 + half * 32 + 32]
+        for n in range(STATES):
+            wide = jnp.broadcast_to(both[:, n : n + 1], (rows, HEAD))
+            gain_ref[s, pl.ds(n, rows, stride=STATES), :] = wide
+            wide = jnp.broadcast_to(both[:, STATES + n : STATES + n + 1], (rows, HEAD))
+            read_ref[s, pl.ds(n, rows, stride=STATES), :] = wide
+        for slot in range(8):
+            bias = packs[slot][MISC : MISC + 16, :].astype(jnp.float32)[5:6]
+            raw = (
+                jnp.dot(
+                    normed, packs[slot][DT : DT + RANK, :], preferred_element_type=jnp.float32
+                )
+                + bias
+            )
+            size = jnp.maximum(raw, 0.0) + jnp.log1p(jnp.exp(-jnp.abs(raw)))
+            smooth = smooth_ref[2 * half + s, :, slot * HEAD : (slot + 1) * HEAD]
+            size_ref[s, pl.ds(slot, rows, stride=8), :] = size
+            drive_ref[s, pl.ds(slot, rows, stride=8), :] = size * smooth.astype(jnp.float32)
+    for slot in range(8):
+        rate = -jnp.exp(packs[slot][AL : AL + STATES, :].astype(jnp.float32)) * LOG2E
+        rate_ref[pl.ds(slot, STATES, stride=8), :] = rate
+
+    def one(t, states):
+        new = []
+        for s in range(2):
+            at = pl.ds(pl.multiple_of(t * 8, 8), 8)
+            size = size_ref[s, at, :]
+            drive = drive_ref[s, at, :]
+            total = [None, None]
+            for n in range(STATES):
+                decay = jnp.exp2(size * rate_ref[n * 8 : n * 8 + 8, :])
+                gain = gain_ref[s, pl.ds(t * STATES + n, 1), :]
+                read = read_ref[s, pl.ds(t * STATES + n, 1), :]
+                state = decay * states[s * STATES + n] + gain * drive
+                new.append(state)
+                term = read * state
+                total[n % 2] = term if total[n % 2] is None else total[n % 2] + term
+            out_ref[s, at, :] = total[0] + total[1]
+        return tuple(new)
+
+    zero = jnp.zeros((8, HEAD), jnp.float32)
+    lax.fori_loop(0, rows, one, (zero,) * (2 * STATES), unroll=2)
+    for s in range(2):
+        for slot in range(8):
+            here = slice(slot * HEAD, (slot + 1) * HEAD)
+            skip = packs[slot][MISC : MISC + 16, :].astype(jnp.float32)[6:7]
+            smooth = smooth_ref[2 * half + s, :, here].astype(jnp.float32)
+            scanned = out_ref[s, pl.ds(slot, rows, stride=8), :] + skip * smooth
+            gate = gates[s][0, :, here].astype(jnp.float32)
+            gated = scanned * (gate / (1.0 + jnp.exp(-gate)))
+            gated_ref[s * rows : (s + 1) * rows, here] = gated.astype(jnp.bfloat16)
+
+
+def output_kernel(*refs):
+    slots, gated_ref, (keep_ref, send_ref) = refs[:8], refs[8], refs[9:]
+    rows = keep_ref.shape[0]
+    width = 512
+    for begin in range(0, keep_ref.shape[1], width):
+        columns = slice(begin, begin + width)
+        weight = jnp.concatenate([slots[slot][:, columns] for slot in range(8)], axis=0)
+        total = jnp.dot(gated_ref[...], weight, preferred_element_type=jnp.float32)
+        keep_ref[:, columns] = total[:rows]
+        send_ref[:, columns] = total[rows:].astype(send_ref.dtype)
+
+
+def grouped(query, key, value, gate_input, conv_weight, conv_bias, x_proj, dt_proj, dt_bias, a_log, d_skip, out_proj):
+    count = lax.axis_size("dp")
+    rows = query.shape[1]
+    width = out_proj.shape[1]
+    pack = jnp.concatenate(
+        [
+            x_proj.T,
+            dt_proj,
+            a_log,
+            conv_weight,
+            conv_bias[None],
+            dt_bias[None],
+            d_skip[None],
+            jnp.zeros((PACK_ROWS - MISC - 7, HEAD), jnp.bfloat16),
+        ],
+        axis=0,
+    )
+
+    def gathered(own):
+        slots = [None] * 8
+        slots[0] = own
+        for even in (2, 4, 6):
+            slots[even] = swap(own, GROUP * even, count)
+        for even in (0, 2, 4, 6):
+            slots[even + 1] = swap(slots[even], GROUP, count)
+        return slots
+
+    packs = gathered(pack)
+    half = jax.ShapeDtypeStruct((2, rows, 8 * HEAD), jnp.bfloat16)
+    keep, send, gkeep, gsend = local_call(
+        attention_kernel, (half,) * 4, "attention",
+        flops=4 * 32 * rows * rows * HEAD, bytes_accessed=6 << 20, transcendentals=32 * rows * rows,
+    )(query[0], key[0], value[0], gate_input[0])
+    x1 = swap(keep[1:2], 2, count)
+    recv = swap(send, 1, count)
+    x2 = swap(recv[1:2], 2, count)
+    grecv = swap(gsend, 1, count)
+    gx1 = swap(gkeep[1:2], 2, count)
+    gx2 = swap(grecv[1:2], 2, count)
+    slots = gathered(out_proj)
+    wide = jax.ShapeDtypeStruct((rows, 640), jnp.float32)
+    smooth, pkeep, psend = local_call(
+        project_kernel,
+        (jax.ShapeDtypeStruct((GROUP, rows, 8 * HEAD), jnp.bfloat16), wide, wide),
+        "project",
+        scratch=[pltpu.VMEM((288, 8 * HEAD), jnp.bfloat16)],
+        flops=2 * GROUP * rows * 1024 * 288, bytes_accessed=4 << 20, transcendentals=GROUP * rows * 1024,
+    )(*packs, keep, recv, x1, x2)
+    chip = pkeep + swap(psend, 1, count)
+    other = swap(chip, 2, count)
+    other = jnp.concatenate(
+        [other[:, 256:512], other[:, :256], other[:, 544:576], other[:, 512:544], other[:, 576:]],
+        axis=1,
+    )
+    full = chip + other
+    partner = swap(full, 1, count)
+
+    def scanned(which, gate_a, gate_b):
+        return local_call(
+            functools.partial(scan_kernel, which),
+            jax.ShapeDtypeStruct((2 * rows, 8 * HEAD), jnp.bfloat16),
+            "scan",
+            scratch=[
+                pltpu.VMEM((2, rows * 8, HEAD), jnp.float32),
+                pltpu.VMEM((2, rows * 8, HEAD), jnp.float32),
+                pltpu.VMEM((2, rows * 8, HEAD), jnp.float32),
+                pltpu.VMEM((STATES * 8, HEAD), jnp.float32),
+                pltpu.VMEM((2, rows * STATES, HEAD), jnp.float32),
+                pltpu.VMEM((2, rows * STATES, HEAD), jnp.float32),
+            ],
+            flops=16 * 1024 * 256 * 256, bytes_accessed=4 << 20, transcendentals=256 * 1024 * 16,
+        )(*packs, full, partner, smooth, gate_a, gate_b)
+
+    def projected_out(gated):
+        return local_call(
+            output_kernel,
+            (
+                jax.ShapeDtypeStruct((rows, width), jnp.float32),
+                jax.ShapeDtypeStruct((rows, width), jnp.bfloat16),
+            ),
+            "output",
+            flops=2 * 2 * rows * 1024 * width, bytes_accessed=6 << 20,
+        )(*slots, gated)
+
+    far_keep, far_send = projected_out(scanned(1, gx1, gx2))
+    far = (far_keep + swap(far_send, 1, count).astype(jnp.float32)).astype(jnp.bfloat16)
+    from_far = swap(far, 2, count)
+    near_keep, near_send = projected_out(scanned(0, gkeep[0:1], grecv[0:1]))
+    near = near_keep + swap(near_send, 1, count).astype(jnp.float32)
+    return (near + from_far.astype(jnp.float32)).astype(jnp.bfloat16)[None]
+
+
 def solution(mesh):
     placed = (
         P("dp", "ctx", None),
@@ -213,6 +485,7 @@
         P("dp"),
         P("dp", None),
     )
+    fits = mesh.shape["ctx"] == 1 and mesh.shape["dp"] == 32
     return jax.shard_map(
-        shards, mesh=mesh, in_specs=placed, out_specs=P("dp", "ctx", None), check_vma=False
-    )
+        grouped if fits else shards, mesh=mesh, in_specs=placed, out_specs=P("dp", "ctx", None), check_vma=False
+    )

time: 449 us -> 141 us (0.31)
  blocking collectives: 193 us -> 0 us
  matrix products: 109 us -> 0 us
  local copies, waits for them, and re-layouts: 92.6 us -> 14 us
  waiting for transfers between devices: 1.45 us -> 68.7 us
  other arithmetic: 33.7 us -> 2.31 us
  starting transfers between devices: 0.73 us -> 29 us
  Pallas kernels: 0 us -> 26.4 us
  between operations: 13.5 us -> 0.35 us
    all_gather x5 -> x0, blocking collectives: 193 us -> none  [the longest x1 43.3 us: shards(): lax.all_gather(conv_weight, 'dp', axis=1, tiled=True)]
    dot_general x134 -> x0, matrix products: 109 us -> none  [the longest x128 86.7 us: advance(): jnp.dot(read_block[position], state, precision=lax.Precision.HIGHEST)]
    ppermute x1 -> x26, waiting for transfers between devices: 0.01 us -> 68.7 us  [swap(): return lax.ppermute(value, 'dp', [(i, i ^ distance) for i in range(count)])]
    slice x26 -> x7, local copies, waits for them, and re-layouts: 43.7 us -> 3.02 us  [the longest x2 0.87 us: grouped(): near_keep, near_send = projected_out(scanned(0, gkeep[0:1], grecv[0:1]))]
    ppermute x1 -> x26, starting transfers between devices: 0.66 us -> 29 us  [swap(): return lax.ppermute(value, 'dp', [(i, i ^ distance) for i in range(count)])]
    pallas_call x0 -> x6, Pallas kernels: none -> 26.4 us  [call(): pl.pallas_call(kernel, out_shape=out_shape, in_specs=[pl.BlockSpec(memory...]
    another operation x8 -> x0, local copies, waits for them, and re-layouts: 22.5 us -> none  [the longest x4 15.4 us: advance(): return (state, jnp.stack(outputs))]
    mul x16 -> x0, local copies, waits for them, and re-layouts: 15.6 us -> none  [the longest x8 11 us: advance(): gain_block[position][:, None] * drive_block[position][None, :]]
  transfers between devices with their start and end apart: 4 -> 26, of which waited for: 0 -> 11; matrix products, arithmetic and copies ran while one was open for 50% -> 5% of each run, Pallas kernels for 0% -> 14%
where the time goes in v1:
time: 141 us
  waiting for transfers between devices  68.7 us (49%)
  starting transfers between devices  29 us (21%)
  Pallas kernels  26.4 us (19%)
  local copies, waits for them, and re-layouts  14 us (10%)
  other arithmetic  2.31 us (2%)
    ppermute x26, waiting for transfers between devices, swap(): return lax.ppermute(value, 'dp', [(i, i ^ distance) for i in range(count)])  68.7 us
    ppermute x26, starting transfers between devices, swap(): return lax.ppermute(value, 'dp', [(i, i ^ distance) for i in range(count)])  29 us
    pallas_call x6, Pallas kernels, call(): pl.pallas_call(kernel, out_shape=out_shape, in_specs=[pl.BlockSpec(memory...  26.4 us
    unnamed x70, local copies, waits for them, and re-layouts  8.89 us
  transfers between devices with their start and end apart: 26, of which 11 were waited for; matrix products, arithmetic and copies ran while one was open for 5% of the time, Pallas kernels for 14%

profile of v1, /device:TPU:0, one launch (start us, length us, event | category | flops | bytes accessed | tf_op | source)
XLA Modules:
  0.0 140.8 jit_solution(5642372048043349178)
XLA Ops:
  0.0 1.2 copy-done.1
  1.2 1.2 copy-done.2
  2.5 0.9 copy-done.3
  3.4 0.9 copy-done.4
  4.4 1.6 %attention.1 = (bf16[2,128,1024]{2,1,0:T(8,128)(2,1)S(1)}, bf16[2,128,1024]{2,1,0:T(8,128)(2,1)S(1)}, bf16[2,128,1024]{2,1,0:T(8,128)(2,1)S(1)}, bf16[2,128,1024]{2,1,0:T(8,128)(2,1)S(1)}) custom-call(bf16[128,4096]{1,0:T(8,128)(2,1)S(1)} %bitcast.10, bf16[128,1024]{1,0:T(8,128)(2,1)S(1)} %bitcast.12, bf16[128,1024]{1,0:T(8,128)(2,1)S(1)} %bitcast.13, ...), custom_call_target="tpu_custom_call" | custom-call | flops 268435456 | bytes 6291456 | tf_op jit(solution)/shard_map/attention/pallas_call | solution.py:220
  6.5 0.6 copy-done.30
  7.4 4.7 %collective-permute-start.12 = (bf16[576,128]{1,0:T(8,128)(2,1)S(1)}, bf16[576,128]{1,0:T(8,128)(2,1)S(1)}, u32[]{:S(2)}, u32[]{:S(2)}) collective-permute-start(bf16[576,128]{1,0:T(8,128)(2,1)S(1)} %concatenate.6.refs_0_), channel_id=1, source_target_pairs={{0,24},{1,25},{2,26},{3,27},{4,28},{5,29},{6,30},{7,31},{8,16},{9,... | collective-permute-start | bytes 442376 | tf_op jit(solution)/shard_map/ppermute | solution.py:215
  12.1 0.6 collective-permute-start.8
  12.7 1.7 %collective-permute-start.7 = (bf16[576,128]{1,0:T(8,128)(2,1)S(1)}, bf16[576,128]{1,0:T(8,128)(2,1)S(1)}, u32[]{:S(2)}, u32[]{:S(2)}) collective-permute-start(bf16[576,128]{1,0:T(8,128)(2,1)S(1)} %concatenate.6.refs_0_), channel_id=1, source_target_pairs={{0,4},{1,5},{2,6},{3,7},{4,0},{5,1},{6,2},{7,3},{8,12},{9,13},{10,... | collective-permute-start | bytes 442376 | tf_op jit(solution)/shard_map/ppermute | solution.py:215
  14.4 1.5 %collective-permute-start.15 = (bf16[1,128,1024]{2,1,0:T(8,128)(2,1)S(1)}, bf16[1,128,1024]{2,1,0:T(8,128)(2,1)S(1)}, u32[]{:S(2)}, u32[]{:S(2)}) collective-permute-start(bf16[1,128,1024]{2,1,0:T(8,128)(2,1)S(1)} %slice.33), channel_id=1, source_target_pairs={{0,2},{1,3},{2,0},{3,1},{4,6},{5,7},{6,4},{7,5},{8,10},{9,11},{10,... | collective-permute-start | bytes 786440 | tf_op jit(solution)/shard_map/ppermute | solution.py:215
  16.0 0.9 collective-permute-done.12.refs_6_
  16.9 1.6 %collective-permute-start.16 = (bf16[1,128,1024]{2,1,0:T(8,128)(2,1)S(1)}, bf16[1,128,1024]{2,1,0:T(8,128)(2,1)S(1)}, u32[]{:S(2)}, u32[]{:S(2)}) collective-permute-start(bf16[1,128,1024]{2,1,0:T(8,128)(2,1)S(1)} %slice.44), channel_id=1, source_target_pairs={{0,2},{1,3},{2,0},{3,1},{4,6},{5,7},{6,4},{7,5},{8,10},{9,11},{10,... | collective-permute-start | bytes 786440 | tf_op jit(solution)/shard_map/ppermute | solution.py:215
  18.5 6.7 %collective-permute-done.10.refs_4_ = bf16[576,128]{1,0:T(8,128)(2,1)S(1)} collective-permute-done((bf16[576,128]{1,0:T(8,128)(2,1)S(1)}, bf16[576,128]{1,0:T(8,128)(2,1)S(1)}, u32[]{:S(2)}, u32[]{:S(2)}) %collective-permute-start.10) | collective-permute-done | bytes 147488 | tf_op jit(solution)/shard_map/ppermute | solution.py:215
  25.2 1.5 %collective-permute-start.13 = (bf16[576,128]{1,0:T(8,128)(2,1)S(1)}, bf16[576,128]{1,0:T(8,128)(2,1)S(1)}, u32[]{:S(2)}, u32[]{:S(2)}) collective-permute-start(bf16[576,128]{1,0:T(8,128)(2,1)S(1)} %collective-permute-done.12.refs_6_), channel_id=1, source_target_pairs={{0,4},{1,5},{2,6},{3,7},{4,0},{5,1},{6,2},{7,3},{8,12},{9,13},{10,... | collective-permute-start | bytes 442376 | tf_op jit(solution)/shard_map/ppermute | solution.py:215
  27.2 1.5 %collective-permute-start.9 = (bf16[576,128]{1,0:T(8,128)(2,1)S(1)}, bf16[576,128]{1,0:T(8,128)(2,1)S(1)}, u32[]{:S(2)}, u32[]{:S(2)}) collective-permute-start(bf16[576,128]{1,0:T(8,128)(2,1)S(1)} %collective-permute-done.8.refs_2_), channel_id=1, source_target_pairs={{0,4},{1,5},{2,6},{3,7},{4,0},{5,1},{6,2},{7,3},{8,12},{9,13},{10,... | collective-permute-start | bytes 442376 | tf_op jit(solution)/shard_map/ppermute | solution.py:215
  28.8 3.2 %collective-permute-done.13.refs_7_ = bf16[576,128]{1,0:T(8,128)(2,1)S(1)} collective-permute-done((bf16[576,128]{1,0:T(8,128)(2,1)S(1)}, bf16[576,128]{1,0:T(8,128)(2,1)S(1)}, u32[]{:S(2)}, u32[]{:S(2)}) %collective-permute-start.13) | collective-permute-done | bytes 147488 | tf_op jit(solution)/shard_map/ppermute | solution.py:215
  32.0 3.2 %collective-permute-done.11.refs_5_ = bf16[576,128]{1,0:T(8,128)(2,1)S(1)} collective-permute-done((bf16[576,128]{1,0:T(8,128)(2,1)S(1)}, bf16[576,128]{1,0:T(8,128)(2,1)S(1)}, u32[]{:S(2)}, u32[]{:S(2)}) %collective-permute-start.11) | collective-permute-done | bytes 147488 | tf_op jit(solution)/shard_map/ppermute | solution.py:215
  35.1 1.9 %collective-permute-done.9.refs_3_ = bf16[576,128]{1,0:T(8,128)(2,1)S(1)} collective-permute-done((bf16[576,128]{1,0:T(8,128)(2,1)S(1)}, bf16[576,128]{1,0:T(8,128)(2,1)S(1)}, u32[]{:S(2)}, u32[]{:S(2)}) %collective-permute-start.9) | collective-permute-done | bytes 147488 | tf_op jit(solution)/shard_map/ppermute | solution.py:215
  37.0 2.1 %project.1 = (bf16[4,128,1024]{2,1,0:T(8,128)(2,1)S(1)}, f32[128,640]{1,0:T(8,128)S(1)}, f32[128,640]{1,0:T(8,128)S(1)}) custom-call(bf16[576,128]{1,0:T(8,128)(2,1)S(1)} %concatenate.6.refs_0_, bf16[576,128]{1,0:T(8,128)(2,1)S(1)} %collective-permute-done.7.refs_1_, bf16[576,128]{1,0:T(8,128)(2,1)S(1)} %collective-permute-done.8.refs_2_, ...), custom_call_target="tpu_custom_call" | custom-call | flops 301989888 | bytes 4194304 | tf_op jit(solution)/shard_map/project/pallas_call | solution.py:220
  39.8 2.5 %collective-permute-start.5 = (bf16[128,2048]{1,0:T(8,128)(2,1)S(1)}, bf16[128,2048]{1,0:T(8,128)(2,1)S(1)}, u32[]{:S(2)}, u32[]{:S(2)}) collective-permute-start(bf16[128,2048]{1,0:T(8,128)(2,1)S(1)} %copy-done), channel_id=1, source_target_pairs={{0,24},{1,25},{2,26},{3,27},{4,28},{5,29},{6,30},{7,31},{8,16},{9,... | collective-permute-start | bytes 1572872 | tf_op jit(solution)/shard_map/ppermute | solution.py:215
  42.3 1.9 %collective-permute-start.1 = (bf16[128,2048]{1,0:T(8,128)(2,1)S(1)}, bf16[128,2048]{1,0:T(8,128)(2,1)S(1)}, u32[]{:S(2)}, u32[]{:S(2)}) collective-permute-start(bf16[128,2048]{1,0:T(8,128)(2,1)S(1)} %copy-done), channel_id=1, source_target_pairs={{0,8},{1,9},{2,10},{3,11},{4,12},{5,13},{6,14},{7,15},{8,0},{9,1},... | collective-permute-start | bytes 1572872 | tf_op jit(solution)/shard_map/ppermute | solution.py:215
  44.2 1.6 %collective-permute-start.18 = (f32[128,640]{1,0:T(8,128)S(1)}, f32[128,640]{1,0:T(8,128)S(1)}, u32[]{:S(2)}, u32[]{:S(2)}) collective-permute-start(f32[128,640]{1,0:T(8,128)S(1)} %add.15), channel_id=1, source_target_pairs={{0,2},{1,3},{2,0},{3,1},{4,6},{5,7},{6,4},{7,5},{8,10},{9,11},{10,... | collective-permute-start | bytes 983048 | tf_op jit(solution)/shard_map/ppermute | solution.py:215
  45.8 0.6 collective-permute-start.22
  46.4 0.8 fusion.1
  47.3 7.7 %collective-permute-done.18 = f32[128,640]{1,0:T(8,128)S(1)} collective-permute-done((f32[128,640]{1,0:T(8,128)S(1)}, f32[128,640]{1,0:T(8,128)S(1)}, u32[]{:S(2)}, u32[]{:S(2)}) %collective-permute-start.18) | collective-permute-done | bytes 327712 | tf_op jit(solution)/shard_map/ppermute | solution.py:215
  54.9 1.5 %collective-permute-start.23 = (bf16[1,128,1024]{2,1,0:T(8,128)(2,1)}, bf16[1,128,1024]{2,1,0:T(8,128)(2,1)}, u32[]{:S(2)}, u32[]{:S(2)}) collective-permute-start(bf16[1,128,1024]{2,1,0:T(8,128)(2,1)} %get-tuple-element.28), channel_id=1, source_target_pairs={{0,2},{1,3},{2,0},{3,1},{4,6},{5,7},{6,4},{7,5},{8,10},{9,11},{10,... | collective-permute-start | bytes 786440 | tf_op jit(solution)/shard_map/ppermute | solution.py:215
  56.4 0.7 fusion.4
  57.1 3.4 %collective-permute-done.22.refs_11_ = bf16[1,128,1024]{2,1,0:T(8,128)(2,1)S(1)} collective-permute-done((bf16[1,128,1024]{2,1,0:T(8,128)(2,1)S(1)}, bf16[1,128,1024]{2,1,0:T(8,128)(2,1)S(1)}, u32[]{:S(2)}, u32[]{:S(2)}) %collective-permute-start.22) | collective-permute-done | bytes 262176 | tf_op jit(solution)/shard_map/ppermute | solution.py:215
  60.6 0.7 copy-done.23
  61.3 1.5 %collective-permute-start = (bf16[128,2048]{1,0:T(8,128)(2,1)S(1)}, bf16[128,2048]{1,0:T(8,128)(2,1)S(1)}, u32[]{:S(2)}, u32[]{:S(2)}) collective-permute-start(bf16[128,2048]{1,0:T(8,128)(2,1)S(1)} %copy-done), channel_id=1, source_target_pairs={{0,4},{1,5},{2,6},{3,7},{4,0},{5,1},{6,2},{7,3},{8,12},{9,13},{10,... | collective-permute-start | bytes 1572872 | tf_op jit(solution)/shard_map/ppermute | solution.py:215
  63.3 23.2 %collective-permute-done.3.refs_4_ = bf16[128,2048]{1,0:T(8,128)(2,1)S(1)} collective-permute-done((bf16[128,2048]{1,0:T(8,128)(2,1)S(1)}, bf16[128,2048]{1,0:T(8,128)(2,1)S(1)}, u32[]{:S(2)}, u32[]{:S(2)}) %collective-permute-start.3) | collective-permute-done | bytes 524320 | tf_op jit(solution)/shard_map/ppermute | solution.py:215
  86.5 1.5 %collective-permute-start.4 = (bf16[128,2048]{1,0:T(8,128)(2,1)S(1)}, bf16[128,2048]{1,0:T(8,128)(2,1)}, u32[]{:S(2)}, u32[]{:S(2)}) collective-permute-start(bf16[128,2048]{1,0:T(8,128)(2,1)S(1)} %collective-permute-done.3.refs_4_), channel_id=1, source_target_pairs={{0,4},{1,5},{2,6},{3,7},{4,0},{5,1},{6,2},{7,3},{8,12},{9,13},{10,... | collective-permute-start | bytes 1572872 | tf_op jit(solution)/shard_map/ppermute | solution.py:215
  88.5 0.7 fusion.3
  89.2 0.7 slice.49
  89.9 1.9 %concatenate.7 = f32[128,640]{1,0:T(8,128)} concatenate(f32[128,256]{1,0:T(8,128)} %get-tuple-element.34, f32[128,256]{1,0:T(8,128)} %get-tuple-element.33, f32[128,32]{1,0:T(8,128)} %get-tuple-element.32, f32[128,32]{1,0:T(8,128)} %get-tuple-element.31, f32[128,64]{1,0:T(8,128)} %slice.49), dimensions={1} | concatenate | bytes 655360 | tf_op jit(solution)/shard_map/concatenate | solution.py:431
  91.8 1.2 add.16.refs_8_
  93.1 1.6 %collective-permute-done.19.refs_9_ = f32[128,640]{1,0:T(8,128)S(1)} collective-permute-done((f32[128,640]{1,0:T(8,128)S(1)}, f32[128,640]{1,0:T(8,128)S(1)}, u32[]{:S(2)}, u32[]{:S(2)}) %collective-permute-start.19) | collective-permute-done | bytes 327712 | tf_op jit(solution)/shard_map/ppermute | solution.py:215
  94.8 0.9 copy-done.19
  95.7 1.2 copy-done.21
  96.9 0.9 copy-done.24
  97.8 8.3 %scan.3.refs_8_ = bf16[256,1024]{1,0:T(8,128)(2,1)S(1)} custom-call(bf16[576,128]{1,0:T(8,128)(2,1)S(1)} %concatenate.6.refs_0_, bf16[576,128]{1,0:T(8,128)(2,1)S(1)} %copy-done.13, bf16[576,128]{1,0:T(8,128)(2,1)S(1)} %copy-done.11, bf16[576,128]{1,0:T(8,128)(2,1)S(1)} %copy-done.19, bf16[576,128]{1,0:T(8,128)(2,1)S(1)} %copy-done.9, ...), custom_call_target="tpu_custom_call" | custom-call | flops 1073741824 | bytes 4194304 | tf_op jit(solution)/shard_map/scan/pallas_call | solution.py:220
  106.2 4.7 %collective-permute-done.2.refs_3_ = bf16[128,2048]{1,0:T(8,128)(2,1)} collective-permute-done((bf16[128,2048]{1,0:T(8,128)(2,1)S(1)}, bf16[128,2048]{1,0:T(8,128)(2,1)}, u32[]{:S(2)}, u32[]{:S(2)}) %collective-permute-start.2) | collective-permute-done | bytes 524320 | tf_op jit(solution)/shard_map/ppermute | solution.py:215
  110.9 3.4 %output.3 = (f32[128,2048]{1,0:T(8,128)}, bf16[128,2048]{1,0:T(8,128)(2,1)S(1)}) custom-call(bf16[128,2048]{1,0:T(8,128)(2,1)S(1)} %copy-done, bf16[128,2048]{1,0:T(8,128)(2,1)S(1)} %collective-permute-done.refs_1_, bf16[128,2048]{1,0:T(8,128)(2,1)S(1)} %collective-permute-done.1.refs_2_, bf16[128,2048]{1,0:T(8,128)(2,1)} %collective-permute-done.2.refs_3_, ...), custom_call_target="tpu_custom_call" | custom-call | flops 1073741824 | bytes 6291456 | tf_op jit(solution)/shard_map/output/pallas_call | solution.py:220
  114.3 7.4 %scan.2.refs_8_ = bf16[256,1024]{1,0:T(8,128)(2,1)S(1)} custom-call(bf16[576,128]{1,0:T(8,128)(2,1)S(1)} %concatenate.6.refs_0_, bf16[576,128]{1,0:T(8,128)(2,1)S(1)} %copy-done.13, bf16[576,128]{1,0:T(8,128)(2,1)S(1)} %copy-done.11, bf16[576,128]{1,0:T(8,128)(2,1)S(1)} %copy-done.19, bf16[576,128]{1,0:T(8,128)(2,1)S(1)} %copy-done.9, ...), custom_call_target="tpu_custom_call" | custom-call | flops 1073741824 | bytes 4194304 | tf_op jit(solution)/shard_map/scan/pallas_call | solution.py:220
  121.7 3.5 %output.2 = (f32[128,2048]{1,0:T(8,128)}, bf16[128,2048]{1,0:T(8,128)(2,1)S(1)}) custom-call(bf16[128,2048]{1,0:T(8,128)(2,1)S(1)} %copy-done, bf16[128,2048]{1,0:T(8,128)(2,1)S(1)} %collective-permute-done.refs_1_, bf16[128,2048]{1,0:T(8,128)(2,1)S(1)} %collective-permute-done.1.refs_2_, bf16[128,2048]{1,0:T(8,128)(2,1)} %collective-permute-done.2.refs_3_, ...), custom_call_target="tpu_custom_call" | custom-call | flops 1073741824 | bytes 6291456 | tf_op jit(solution)/shard_map/output/pallas_call | solution.py:220
  125.9 1.6 %collective-permute-start.25 = (bf16[128,2048]{1,0:T(8,128)(2,1)S(1)}, bf16[128,2048]{1,0:T(8,128)(2,1)S(1)}, u32[]{:S(2)}, u32[]{:S(2)}) collective-permute-start(bf16[128,2048]{1,0:T(8,128)(2,1)S(1)} %add_convert_fusion.1), channel_id=1, source_target_pairs={{0,2},{1,3},{2,0},{3,1},{4,6},{5,7},{6,4},{7,5},{8,10},{9,11},{10,... | collective-permute-start | bytes 1572872 | tf_op jit(solution)/shard_map/ppermute | solution.py:215
  127.4 12.3 %collective-permute-done.25 = bf16[128,2048]{1,0:T(8,128)(2,1)S(1)} collective-permute-done((bf16[128,2048]{1,0:T(8,128)(2,1)S(1)}, bf16[128,2048]{1,0:T(8,128)(2,1)S(1)}, u32[]{:S(2)}, u32[]{:S(2)}) %collective-permute-start.25) | collective-permute-done | bytes 524320 | tf_op jit(solution)/shard_map/ppermute | solution.py:215
  139.8 1.0 fusion
  (94 shorter events, 3.7 us)
Async XLA Ops:
  4.4 2.2 %copy-start.28 = (bf16[128,288]{0,1:T(8,128)(2,1)S(1)}, bf16[128,288]{0,1:T(8,128)(2,1)}, u32[]{:S(2)}) copy-start(bf16[128,288]{0,1:T(8,128)(2,1)} %param.18) | copy-start | bytes 221188
  4.4 2.2 %copy-start.29 = (bf16[256,128]{1,0:T(8,128)(2,1)S(1)}, bf16[256,128]{1,0:T(8,128)(2,1)}, u32[]{:S(2)}) copy-start(bf16[256,128]{1,0:T(8,128)(2,1)} %param.19) | copy-start | bytes 196612
  6.0 8.5 %collective-permute-start.14 = (bf16[2,128,1024]{2,1,0:T(8,128)(2,1)S(1)}, bf16[2,128,1024]{2,1,0:T(8,128)(2,1)S(1)}, u32[]{:S(2)}, u32[]{:S(2)}) collective-permute-start(bf16[2,128,1024]{2,1,0:T(8,128)(2,1)S(1)} %get-tuple-element.17), channel_id=1, source_target_pairs={{0,1},{1,0},{2,3},{3,2},{4,5},{5,4},{6,7},{7,6},{8,9},{9,8},{10,11... | collective-permute-start | bytes 1572872 | tf_op jit(solution)/shard_map/ppermute | solution.py:215
  7.4 9.5 %collective-permute-start.12 = (bf16[576,128]{1,0:T(8,128)(2,1)S(1)}, bf16[576,128]{1,0:T(8,128)(2,1)S(1)}, u32[]{:S(2)}, u32[]{:S(2)}) collective-permute-start(bf16[576,128]{1,0:T(8,128)(2,1)S(1)} %concatenate.6.refs_0_), channel_id=1, source_target_pairs={{0,24},{1,25},{2,26},{3,27},{4,28},{5,29},{6,30},{7,31},{8,16},{9,... | collective-permute-start | bytes 442376 | tf_op jit(solution)/shard_map/ppermute | solution.py:215
  12.1 13.1 %collective-permute-start.10 = (bf16[576,128]{1,0:T(8,128)(2,1)S(1)}, bf16[576,128]{1,0:T(8,128)(2,1)S(1)}, u32[]{:S(2)}, u32[]{:S(2)}) collective-permute-start(bf16[576,128]{1,0:T(8,128)(2,1)S(1)} %concatenate.6.refs_0_), channel_id=1, source_target_pairs={{0,16},{1,17},{2,18},{3,19},{4,20},{5,21},{6,22},{7,23},{8,24},{9,... | collective-permute-start | bytes 442376 | tf_op jit(solution)/shard_map/ppermute | solution.py:215
  12.1 14.7 %collective-permute-start.8 = (bf16[576,128]{1,0:T(8,128)(2,1)S(1)}, bf16[576,128]{1,0:T(8,128)(2,1)S(1)}, u32[]{:S(2)}, u32[]{:S(2)}) collective-permute-start(bf16[576,128]{1,0:T(8,128)(2,1)S(1)} %concatenate.6.refs_0_), channel_id=1, source_target_pairs={{0,8},{1,9},{2,10},{3,11},{4,12},{5,13},{6,14},{7,15},{8,0},{9,1},... | collective-permute-start | bytes 442376 | tf_op jit(solution)/shard_map/ppermute | solution.py:215
  12.7 14.5 %collective-permute-start.7 = (bf16[576,128]{1,0:T(8,128)(2,1)S(1)}, bf16[576,128]{1,0:T(8,128)(2,1)S(1)}, u32[]{:S(2)}, u32[]{:S(2)}) collective-permute-start(bf16[576,128]{1,0:T(8,128)(2,1)S(1)} %concatenate.6.refs_0_), channel_id=1, source_target_pairs={{0,4},{1,5},{2,6},{3,7},{4,0},{5,1},{6,2},{7,3},{8,12},{9,13},{10,... | collective-permute-start | bytes 442376 | tf_op jit(solution)/shard_map/ppermute | solution.py:215
  14.4 14.4 %collective-permute-start.15 = (bf16[1,128,1024]{2,1,0:T(8,128)(2,1)S(1)}, bf16[1,128,1024]{2,1,0:T(8,128)(2,1)S(1)}, u32[]{:S(2)}, u32[]{:S(2)}) collective-permute-start(bf16[1,128,1024]{2,1,0:T(8,128)(2,1)S(1)} %slice.33), channel_id=1, source_target_pairs={{0,2},{1,3},{2,0},{3,1},{4,6},{5,7},{6,4},{7,5},{8,10},{9,11},{10,... | collective-permute-start | bytes 786440 | tf_op jit(solution)/shard_map/ppermute | solution.py:215
  16.0 23.8 %copy-start = (bf16[128,2048]{1,0:T(8,128)(2,1)S(1)}, bf16[128,2048]{1,0:T(8,128)(2,1)}, u32[]{:S(2)}) copy-start(bf16[128,2048]{1,0:T(8,128)(2,1)} %refs_0_.3) | copy-start | bytes 1572868
  16.9 22.3 %copy-start.6 = (bf16[576,128]{1,0:T(8,128)(2,1)}, bf16[576,128]{1,0:T(8,128)(2,1)S(1)}, u32[]{:S(2)}) copy-start(bf16[576,128]{1,0:T(8,128)(2,1)S(1)} %collective-permute-done.12.refs_6_) | copy-start | bytes 442372
  16.9 20.1 %collective-permute-start.16 = (bf16[1,128,1024]{2,1,0:T(8,128)(2,1)S(1)}, bf16[1,128,1024]{2,1,0:T(8,128)(2,1)S(1)}, u32[]{:S(2)}, u32[]{:S(2)}) collective-permute-start(bf16[1,128,1024]{2,1,0:T(8,128)(2,1)S(1)} %slice.44), channel_id=1, source_target_pairs={{0,2},{1,3},{2,0},{3,1},{4,6},{5,7},{6,4},{7,5},{8,10},{9,11},{10,... | collective-permute-start | bytes 786440 | tf_op jit(solution)/shard_map/ppermute | solution.py:215
  25.2 13.9 %copy-start.8 = (bf16[576,128]{1,0:T(8,128)(2,1)}, bf16[576,128]{1,0:T(8,128)(2,1)S(1)}, u32[]{:S(2)}) copy-start(bf16[576,128]{1,0:T(8,128)(2,1)S(1)} %collective-permute-done.10.refs_4_) | copy-start | bytes 442372
  25.2 6.8 %collective-permute-start.13 = (bf16[576,128]{1,0:T(8,128)(2,1)S(1)}, bf16[576,128]{1,0:T(8,128)(2,1)S(1)}, u32[]{:S(2)}, u32[]{:S(2)}) collective-permute-start(bf16[576,128]{1,0:T(8,128)(2,1)S(1)} %collective-permute-done.12.refs_6_), channel_id=1, source_target_pairs={{0,4},{1,5},{2,6},{3,7},{4,0},{5,1},{6,2},{7,3},{8,12},{9,13},{10,... | collective-permute-start | bytes 442376 | tf_op jit(solution)/shard_map/ppermute | solution.py:215
  26.7 12.4 %copy-start.10 = (bf16[576,128]{1,0:T(8,128)(2,1)}, bf16[576,128]{1,0:T(8,128)(2,1)S(1)}, u32[]{:S(2)}) copy-start(bf16[576,128]{1,0:T(8,128)(2,1)S(1)} %collective-permute-done.8.refs_2_) | copy-start | bytes 442372
  26.7 8.4 %collective-permute-start.11 = (bf16[576,128]{1,0:T(8,128)(2,1)S(1)}, bf16[576,128]{1,0:T(8,128)(2,1)S(1)}, u32[]{:S(2)}, u32[]{:S(2)}) collective-permute-start(bf16[576,128]{1,0:T(8,128)(2,1)S(1)} %collective-permute-done.10.refs_4_), channel_id=1, source_target_pairs={{0,4},{1,5},{2,6},{3,7},{4,0},{5,1},{6,2},{7,3},{8,12},{9,13},{10,... | collective-permute-start | bytes 442376 | tf_op jit(solution)/shard_map/ppermute | solution.py:215
  27.2 11.9 %copy-start.12 = (bf16[576,128]{1,0:T(8,128)(2,1)}, bf16[576,128]{1,0:T(8,128)(2,1)S(1)}, u32[]{:S(2)}) copy-start(bf16[576,128]{1,0:T(8,128)(2,1)S(1)} %collective-permute-done.7.refs_1_) | copy-start | bytes 442372
  27.2 9.8 %collective-permute-start.9 = (bf16[576,128]{1,0:T(8,128)(2,1)S(1)}, bf16[576,128]{1,0:T(8,128)(2,1)S(1)}, u32[]{:S(2)}, u32[]{:S(2)}) collective-permute-start(bf16[576,128]{1,0:T(8,128)(2,1)S(1)} %collective-permute-done.8.refs_2_), channel_id=1, source_target_pairs={{0,4},{1,5},{2,6},{3,7},{4,0},{5,1},{6,2},{7,3},{8,12},{9,13},{10,... | collective-permute-start | bytes 442376 | tf_op jit(solution)/shard_map/ppermute | solution.py:215
  32.0 7.2 %copy-start.14 = (bf16[576,128]{1,0:T(8,128)(2,1)}, bf16[576,128]{1,0:T(8,128)(2,1)S(1)}, u32[]{:S(2)}) copy-start(bf16[576,128]{1,0:T(8,128)(2,1)S(1)} %collective-permute-done.13.refs_7_) | copy-start | bytes 442372
  35.1 4.1 %copy-start.16 = (bf16[576,128]{1,0:T(8,128)(2,1)}, bf16[576,128]{1,0:T(8,128)(2,1)S(1)}, u32[]{:S(2)}) copy-start(bf16[576,128]{1,0:T(8,128)(2,1)S(1)} %collective-permute-done.11.refs_5_) | copy-start | bytes 442372
  37.0 2.2 %copy-start.18 = (bf16[576,128]{1,0:T(8,128)(2,1)}, bf16[576,128]{1,0:T(8,128)(2,1)S(1)}, u32[]{:S(2)}) copy-start(bf16[576,128]{1,0:T(8,128)(2,1)S(1)} %collective-permute-done.9.refs_3_) | copy-start | bytes 442372
  39.2 8.1 %copy-start.20 = (bf16[4,128,1024]{2,1,0:T(8,128)(2,1)}, bf16[4,128,1024]{2,1,0:T(8,128)(2,1)S(1)}, u32[]{:S(2)}) copy-start(bf16[4,128,1024]{2,1,0:T(8,128)(2,1)S(1)} %get-tuple-element.20.refs_10_) | copy-start | bytes 3145732
  39.2 5.0 %collective-permute-start.17 = (f32[128,640]{1,0:T(8,128)S(1)}, f32[128,640]{1,0:T(8,128)S(1)}, u32[]{:S(2)}, u32[]{:S(2)}) collective-permute-start(f32[128,640]{1,0:T(8,128)S(1)} %get-tuple-element.19), channel_id=1, source_target_pairs={{0,1},{1,0},{2,3},{3,2},{4,5},{5,4},{6,7},{7,6},{8,9},{9,8},{10,11... | collective-permute-start | bytes 983048 | tf_op jit(solution)/shard_map/ppermute | solution.py:215
  39.3 6.6 %collective-permute-start.20 = (bf16[2,128,1024]{2,1,0:T(8,128)(2,1)S(1)}, bf16[2,128,1024]{2,1,0:T(8,128)(2,1)S(1)}, u32[]{:S(2)}, u32[]{:S(2)}) collective-permute-start(bf16[2,128,1024]{2,1,0:T(8,128)(2,1)S(1)} %get-tuple-element.22), channel_id=1, source_target_pairs={{0,1},{1,0},{2,3},{3,2},{4,5},{5,4},{6,7},{7,6},{8,9},{9,8},{10,11... | collective-permute-start | bytes 1572872 | tf_op jit(solution)/shard_map/ppermute | solution.py:215
  39.8 23.0 %collective-permute-start.5 = (bf16[128,2048]{1,0:T(8,128)(2,1)S(1)}, bf16[128,2048]{1,0:T(8,128)(2,1)S(1)}, u32[]{:S(2)}, u32[]{:S(2)}) collective-permute-start(bf16[128,2048]{1,0:T(8,128)(2,1)S(1)} %copy-done), channel_id=1, source_target_pairs={{0,24},{1,25},{2,26},{3,27},{4,28},{5,29},{6,30},{7,31},{8,16},{9,... | collective-permute-start | bytes 1572872 | tf_op jit(solution)/shard_map/ppermute | solution.py:215
  42.3 44.2 %collective-permute-start.3 = (bf16[128,2048]{1,0:T(8,128)(2,1)S(1)}, bf16[128,2048]{1,0:T(8,128)(2,1)S(1)}, u32[]{:S(2)}, u32[]{:S(2)}) collective-permute-start(bf16[128,2048]{1,0:T(8,128)(2,1)S(1)} %copy-done), channel_id=1, source_target_pairs={{0,16},{1,17},{2,18},{3,19},{4,20},{5,21},{6,22},{7,23},{8,24},{9,... | collective-permute-start | bytes 1572872 | tf_op jit(solution)/shard_map/ppermute | solution.py:215
  42.3 45.8 %collective-permute-start.1 = (bf16[128,2048]{1,0:T(8,128)(2,1)S(1)}, bf16[128,2048]{1,0:T(8,128)(2,1)S(1)}, u32[]{:S(2)}, u32[]{:S(2)}) collective-permute-start(bf16[128,2048]{1,0:T(8,128)(2,1)S(1)} %copy-done), channel_id=1, source_target_pairs={{0,8},{1,9},{2,10},{3,11},{4,12},{5,13},{6,14},{7,15},{8,0},{9,1},... | collective-permute-start | bytes 1572872 | tf_op jit(solution)/shard_map/ppermute | solution.py:215
  44.2 1.6 %copy-start.25 = (f32[128,640]{1,0:T(8,128)}, f32[128,640]{1,0:T(8,128)S(1)}, u32[]{:S(2)}) copy-start(f32[128,640]{1,0:T(8,128)S(1)} %add.15) | copy-start | bytes 983044
  44.2 10.7 %collective-permute-start.18 = (f32[128,640]{1,0:T(8,128)S(1)}, f32[128,640]{1,0:T(8,128)S(1)}, u32[]{:S(2)}, u32[]{:S(2)}) collective-permute-start(f32[128,640]{1,0:T(8,128)S(1)} %add.15), channel_id=1, source_target_pairs={{0,2},{1,3},{2,0},{3,1},{4,6},{5,7},{6,4},{7,5},{8,10},{9,11},{10,... | collective-permute-start | bytes 983048 | tf_op jit(solution)/shard_map/ppermute | solution.py:215
  45.8 14.7 %collective-permute-start.22 = (bf16[1,128,1024]{2,1,0:T(8,128)(2,1)S(1)}, bf16[1,128,1024]{2,1,0:T(8,128)(2,1)S(1)}, u32[]{:S(2)}, u32[]{:S(2)}) collective-permute-start(bf16[1,128,1024]{2,1,0:T(8,128)(2,1)S(1)} %get-tuple-element.30), channel_id=1, source_target_pairs={{0,2},{1,3},{2,0},{3,1},{4,6},{5,7},{6,4},{7,5},{8,10},{9,11},{10,... | collective-permute-start | bytes 786440 | tf_op jit(solution)/shard_map/ppermute | solution.py:215
  54.9 38.1 %collective-permute-start.23 = (bf16[1,128,1024]{2,1,0:T(8,128)(2,1)}, bf16[1,128,1024]{2,1,0:T(8,128)(2,1)}, u32[]{:S(2)}, u32[]{:S(2)}) collective-permute-start(bf16[1,128,1024]{2,1,0:T(8,128)(2,1)} %get-tuple-element.28), channel_id=1, source_target_pairs={{0,2},{1,3},{2,0},{3,1},{4,6},{5,7},{6,4},{7,5},{8,10},{9,11},{10,... | collective-permute-start | bytes 786440 | tf_op jit(solution)/shard_map/ppermute | solution.py:215
  61.3 44.9 %collective-permute-start = (bf16[128,2048]{1,0:T(8,128)(2,1)S(1)}, bf16[128,2048]{1,0:T(8,128)(2,1)S(1)}, u32[]{:S(2)}, u32[]{:S(2)}) collective-permute-start(bf16[128,2048]{1,0:T(8,128)(2,1)S(1)} %copy-done), channel_id=1, source_target_pairs={{0,4},{1,5},{2,6},{3,7},{4,0},{5,1},{6,2},{7,3},{8,12},{9,13},{10,... | collective-permute-start | bytes 1572872 | tf_op jit(solution)/shard_map/ppermute | solution.py:215
  62.8 43.4 %collective-permute-start.6 = (bf16[128,2048]{1,0:T(8,128)(2,1)S(1)}, bf16[128,2048]{1,0:T(8,128)(2,1)S(1)}, u32[]{:S(2)}, u32[]{:S(2)}) collective-permute-start(bf16[128,2048]{1,0:T(8,128)(2,1)S(1)} %collective-permute-done.5.refs_6_), channel_id=1, source_target_pairs={{0,4},{1,5},{2,6},{3,7},{4,0},{5,1},{6,2},{7,3},{8,12},{9,13},{10,... | collective-permute-start | bytes 1572872 | tf_op jit(solution)/shard_map/ppermute | solution.py:215
  86.5 19.7 %collective-permute-start.4 = (bf16[128,2048]{1,0:T(8,128)(2,1)S(1)}, bf16[128,2048]{1,0:T(8,128)(2,1)}, u32[]{:S(2)}, u32[]{:S(2)}) collective-permute-start(bf16[128,2048]{1,0:T(8,128)(2,1)S(1)} %collective-permute-done.3.refs_4_), channel_id=1, source_target_pairs={{0,4},{1,5},{2,6},{3,7},{4,0},{5,1},{6,2},{7,3},{8,12},{9,13},{10,... | collective-permute-start | bytes 1572872 | tf_op jit(solution)/shard_map/ppermute | solution.py:215
  88.0 22.9 %collective-permute-start.2 = (bf16[128,2048]{1,0:T(8,128)(2,1)S(1)}, bf16[128,2048]{1,0:T(8,128)(2,1)}, u32[]{:S(2)}, u32[]{:S(2)}) collective-permute-start(bf16[128,2048]{1,0:T(8,128)(2,1)S(1)} %collective-permute-done.1.refs_2_), channel_id=1, source_target_pairs={{0,4},{1,5},{2,6},{3,7},{4,0},{5,1},{6,2},{7,3},{8,12},{9,13},{10,... | collective-permute-start | bytes 1572872 | tf_op jit(solution)/shard_map/ppermute | solution.py:215
  91.8 2.9 %copy-start.7 = (bf16[576,128]{1,0:T(8,128)(2,1)S(1)}, bf16[576,128]{1,0:T(8,128)(2,1)}, u32[]{:S(2)}) copy-start(bf16[576,128]{1,0:T(8,128)(2,1)} %copy-done.6) | copy-start | bytes 442372
  91.8 2.9 %copy-start.9 = (bf16[576,128]{1,0:T(8,128)(2,1)S(1)}, bf16[576,128]{1,0:T(8,128)(2,1)}, u32[]{:S(2)}) copy-start(bf16[576,128]{1,0:T(8,128)(2,1)} %copy-done.8) | copy-start | bytes 442372
  91.8 2.9 %copy-start.11 = (bf16[576,128]{1,0:T(8,128)(2,1)S(1)}, bf16[576,128]{1,0:T(8,128)(2,1)}, u32[]{:S(2)}) copy-start(bf16[576,128]{1,0:T(8,128)(2,1)} %copy-done.10) | copy-start | bytes 442372
  91.8 2.9 %copy-start.13 = (bf16[576,128]{1,0:T(8,128)(2,1)S(1)}, bf16[576,128]{1,0:T(8,128)(2,1)}, u32[]{:S(2)}) copy-start(bf16[576,128]{1,0:T(8,128)(2,1)} %copy-done.12) | copy-start | bytes 442372
  91.8 2.9 %copy-start.15 = (bf16[576,128]{1,0:T(8,128)(2,1)S(1)}, bf16[576,128]{1,0:T(8,128)(2,1)}, u32[]{:S(2)}) copy-start(bf16[576,128]{1,0:T(8,128)(2,1)} %copy-done.14) | copy-start | bytes 442372
  91.8 2.9 %copy-start.17 = (bf16[576,128]{1,0:T(8,128)(2,1)S(1)}, bf16[576,128]{1,0:T(8,128)(2,1)}, u32[]{:S(2)}) copy-start(bf16[576,128]{1,0:T(8,128)(2,1)} %copy-done.16) | copy-start | bytes 442372
  93.0 1.7 %collective-permute-start.19 = (f32[128,640]{1,0:T(8,128)S(1)}, f32[128,640]{1,0:T(8,128)S(1)}, u32[]{:S(2)}, u32[]{:S(2)}) collective-permute-start(f32[128,640]{1,0:T(8,128)S(1)} %add.16.refs_8_), channel_id=1, source_target_pairs={{0,1},{1,0},{2,3},{3,2},{4,5},{5,4},{6,7},{7,6},{8,9},{9,8},{10,11... | collective-permute-start | bytes 983048 | tf_op jit(solution)/shard_map/ppermute | solution.py:215
  106.2 8.1 %copy-start.5 = (bf16[1,128,1024]{2,1,0:T(8,128)(2,1)S(1)}, bf16[1,128,1024]{2,1,0:T(8,128)(2,1)}, u32[]{:S(2)}) copy-start(bf16[1,128,1024]{2,1,0:T(8,128)(2,1)} %get-tuple-element.27.refs_12_) | copy-start | bytes 786436
  106.2 8.1 %copy-start.22 = (bf16[4,128,1024]{2,1,0:T(8,128)(2,1)S(1)}, bf16[4,128,1024]{2,1,0:T(8,128)(2,1)}, u32[]{:S(2)}) copy-start(bf16[4,128,1024]{2,1,0:T(8,128)(2,1)} %copy-done.20) | copy-start | bytes 3145732
  114.3 11.5 %collective-permute-start.24 = (bf16[128,2048]{1,0:T(8,128)(2,1)S(1)}, bf16[128,2048]{1,0:T(8,128)(2,1)S(1)}, u32[]{:S(2)}, u32[]{:S(2)}) collective-permute-start(bf16[128,2048]{1,0:T(8,128)(2,1)S(1)} %get-tuple-element.26), channel_id=1, source_target_pairs={{0,1},{1,0},{2,3},{3,2},{4,5},{5,4},{6,7},{7,6},{8,9},{9,8},{10,11... | collective-permute-start | bytes 1572872 | tf_op jit(solution)/shard_map/ppermute | solution.py:215
  121.7 4.0 %copy-start.26 = (f32[128,2048]{1,0:T(8,128)S(1)}, f32[128,2048]{1,0:T(8,128)}, u32[]{:S(2)}) copy-start(f32[128,2048]{1,0:T(8,128)} %get-tuple-element.25) | copy-start | bytes 3145732
  125.3 2.2 %collective-permute-start.21 = (bf16[128,2048]{1,0:T(8,128)(2,1)S(1)}, bf16[128,2048]{1,0:T(8,128)(2,1)S(1)}, u32[]{:S(2)}, u32[]{:S(2)}) collective-permute-start(bf16[128,2048]{1,0:T(8,128)(2,1)S(1)} %get-tuple-element.24), channel_id=1, source_target_pairs={{0,1},{1,0},{2,3},{3,2},{4,5},{5,4},{6,7},{7,6},{8,9},{9,8},{10,11... | collective-permute-start | bytes 1572872 | tf_op jit(solution)/shard_map/ppermute | solution.py:215
  125.8 14.0 %copy-start.27 = (f32[128,2048]{1,0:T(8,128)S(1)}, f32[128,2048]{1,0:T(8,128)}, u32[]{:S(2)}) copy-start(f32[128,2048]{1,0:T(8,128)} %get-tuple-element.23) | copy-start | bytes 3145732
  125.9 13.9 %collective-permute-start.25 = (bf16[128,2048]{1,0:T(8,128)(2,1)S(1)}, bf16[128,2048]{1,0:T(8,128)(2,1)S(1)}, u32[]{:S(2)}, u32[]{:S(2)}) collective-permute-start(bf16[128,2048]{1,0:T(8,128)(2,1)S(1)} %add_convert_fusion.1), channel_id=1, source_target_pairs={{0,2},{1,3},{2,0},{3,1},{4,6},{5,7},{6,4},{7,5},{8,10},{9,11},{10,... | collective-permute-start | bytes 1572872 | tf_op jit(solution)/shard_map/ppermute | solution.py:215
  (13 other events, 11.6 us)

commit v2 on v1

--- a/solution.py
+++ b/solution.py
@@ -208,6 +208,10 @@
 EPS = 1e-06
 LOG2E = 1.4426950408889634
 GROUP = 4
+MEMBERS = (1, 8)
+SLOTS = (2, 4, 16)
+COST = {"attention": 5, "project": 0, "combine": 0, "scan": 8, "output": 0}
+WAITS = {"project": (), "add": (), "combine": (), "scan": ()}
 XW, DT, AL, MISC, PACK_ROWS = 0, 288, 544, 560, 576
 
 
@@ -215,39 +219,56 @@
     return lax.ppermute(value, "dp", [(i, i ^ distance) for i in range(count)])
 
 
-def local_call(kernel, out_shape, name, scratch=(), flops=0, bytes_accessed=0, transcendentals=0):
+def local_call(kernel, out_shape, name, weight=0, scratch=(), waits=(), away=0):
     def call(*args):
+        inside, anywhere = (pl.BlockSpec(memory_space=m) for m in (pltpu.VMEM, pl.ANY))
         return pl.pallas_call(
             kernel,
             out_shape=out_shape,
-            in_specs=[pl.BlockSpec(memory_space=pltpu.VMEM)] * len(args),
-            out_specs=jax.tree.map(lambda _: pl.BlockSpec(memory_space=pltpu.VMEM), out_shape),
+            in_specs=[anywhere] * away + [inside] * (len(args) - away) + [anywhere] * len(waits),
+            out_specs=jax.tree.map(lambda _: inside, out_shape),
             scratch_shapes=list(scratch),
             name=name,
-            cost_estimate=pl.CostEstimate(
-                flops=flops, bytes_accessed=bytes_accessed, transcendentals=transcendentals
-            ),
+            cost_estimate=pl.CostEstimate(flops=1, bytes_accessed=weight * 3_690_000, transcendentals=0),
             compiler_params=pltpu.CompilerParams(vmem_limit_bytes=48 * 1024 * 1024),
-        )(*args)
+        )(*args, *waits)
 
     return call
 
 
-def attention_kernel(q_ref, k_ref, v_ref, g_ref, keep_ref, send_ref, gkeep_ref, gsend_ref):
+def placed(distance):
+    member = sum(1 << k for k, bit in enumerate(MEMBERS) if distance & bit)
+    return member, sum(1 << k for k, bit in enumerate(SLOTS) if distance & bit)
+
+
+def after(value, *others):
+    return lax.optimization_barrier((value,) + others)[0]
+
+
+def attention_kernel(*refs):
+    inputs, (own_ref, across_ref, send_ref) = refs[:3], refs[3:6]
+    q_ref, k_ref, v_ref, arrived = refs[6:]
+    copies = [
+        pltpu.make_async_copy(source, held, arrived.at[n])
+        for n, (source, held) in enumerate(zip(inputs, (q_ref, k_ref, v_ref)))
+    ]
+    for copy in copies:
+        copy.start()
     position = lax.axis_index("dp")
-    member, block = position % GROUP, position // GROUP
     rows = q_ref.shape[0]
     scale = 1.0 / math.sqrt(HEAD)
     row = lax.broadcasted_iota(jnp.int32, (GROUP, rows, rows), 1).reshape(GROUP * rows, rows)
     col = lax.broadcasted_iota(jnp.int32, (GROUP * rows, rows), 1)
     visible = col <= row
+    for copy in copies:
+        copy.wait()
 
     def lanes(index):
         return pl.ds(pl.multiple_of(index * HEAD, HEAD), HEAD)
 
-    for slot in range(8):
-        kv = block ^ slot
-        heads = [kv * GROUP + (member ^ j) for j in range(GROUP)]
+    for pair in range(8):
+        kv = (position // 4) ^ pair
+        heads = [position ^ (pair * 4 + inner) for inner in range(4)]
         stacked = jnp.concatenate([q_ref[:, lanes(h)] for h in heads], axis=0)
         keys = k_ref[:, lanes(kv)]
         values = v_ref[:, lanes(kv)]
@@ -260,21 +281,45 @@
         total = jnp.sum(raised, axis=-1, keepdims=True)
         mixed = jnp.dot(raised.astype(jnp.bfloat16), values, preferred_element_type=jnp.float32)
         mixed = (mixed / total).astype(jnp.bfloat16)
+        for inner in range(4):
+            j, slot = placed(pair * 4 + inner)
+            here = slice(slot * HEAD, (slot + 1) * HEAD)
+            target = (own_ref, send_ref.at[0], across_ref, send_ref.at[1])[j]
+            target[:, here] = mixed[inner * rows : (inner + 1) * rows]
+
+
+def gates_kernel(g_ref, own_ref, across_ref, send_ref):
+    position = lax.axis_index("dp")
+    for distance in range(32):
+        j, slot = placed(distance)
         here = slice(slot * HEAD, (slot + 1) * HEAD)
-        for j in range(GROUP):
-            target = send_ref if j % 2 else keep_ref
-            gtarget = gsend_ref if j % 2 else gkeep_ref
-            target[j // 2, :, here] = mixed[j * rows : (j + 1) * rows]
-            gtarget[j // 2, :, here] = g_ref[:, lanes(heads[j])]
+        head = position ^ distance
+        target = (own_ref, send_ref.at[0], across_ref, send_ref.at[1])[j]
+        target[:, here] = g_ref[:, pl.ds(pl.multiple_of(head * HEAD, HEAD), HEAD)]
+
+
+def slot_packs(refs):
+    own, z_ref, x_ref, y_ref, xy_ref, xyz_ref = refs
+    return [
+        own,
+        x_ref.at[:PACK_ROWS],
+        y_ref.at[:PACK_ROWS],
+        xy_ref,
+        z_ref,
+        x_ref.at[PACK_ROWS:],
+        y_ref.at[PACK_ROWS:],
+        xyz_ref,
+    ]
 
 
 def project_kernel(*refs):
-    packs, (keep_ref, recv_ref, x1_ref, x2_ref), rest = refs[:8], refs[8:12], refs[12:]
-    smooth_ref, pkeep_ref, psend_ref, weight_ref = rest
-    rows = keep_ref.shape[1]
+    packs = slot_packs(refs[:6])
+    own_ref, send_ref, pair_ref = refs[6:9]
+    smooth_ref, pkeep_ref, psend_ref, weight_ref = refs[-4:]
+    sources = [own_ref, send_ref.at[0], pair_ref.at[0], pair_ref.at[1]]
+    rows = own_ref.shape[0]
     row = lax.broadcasted_iota(jnp.int32, (rows, HEAD), 0)
     masks = [row >= k for k in range(TAPS)]
-    sources = [keep_ref.at[0], recv_ref.at[0], x1_ref.at[0], x2_ref.at[0]]
     for slot in range(8):
         here = slice(slot * HEAD, (slot + 1) * HEAD)
         weight_ref[:, here] = packs[slot][XW : XW + 288, :]
@@ -303,12 +348,25 @@
         target[:, 512 + half * 32 : 512 + half * 32 + 32] = part[:, 256:288]
 
 
+def add_kernel(a_ref, b_ref, *rest):
+    rest[-1][...] = a_ref[...] + b_ref[...]
+
+
+def combine_kernel(chip_ref, other_ref, *rest):
+    full_ref = rest[-1]
+    full_ref[:, :256] = chip_ref[:, :256] + other_ref[:, 256:512]
+    full_ref[:, 256:512] = chip_ref[:, 256:512] + other_ref[:, :256]
+    lanes = lax.broadcasted_iota(jnp.int32, (chip_ref.shape[0], HEAD), 1)
+    other = other_ref[:, 512:]
+    turned = jnp.where(lanes < 32, pltpu.roll(other, HEAD - 32, 1), pltpu.roll(other, 32, 1))
+    full_ref[:, 512:] = chip_ref[:, 512:] + turned
+
+
 def scan_kernel(half, *refs):
-    packs, (f0_ref, f1_ref, smooth_ref, ga_ref, gb_ref), rest = refs[:8], refs[8:13], refs[13:]
-    gated_ref, size_ref, drive_ref, out_ref, rate_ref, gain_ref, read_ref = rest
+    packs, (f0_ref, f1_ref, smooth_ref) = slot_packs(refs[:6]), refs[6:9]
+    scanned_ref, size_ref, drive_ref, out_ref, rate_ref, gain_ref, read_ref = refs[-7:]
     rows = f0_ref.shape[0]
     sources = [f0_ref, f1_ref]
-    gates = [ga_ref, gb_ref]
     for s in range(2):
         low = sources[s][:, half * 256 : half * 256 + 256]
         normed = low * lax.rsqrt(jnp.mean(low * low, axis=-1, keepdims=True) + EPS)
@@ -361,18 +419,24 @@
             skip = packs[slot][MISC : MISC + 16, :].astype(jnp.float32)[6:7]
             smooth = smooth_ref[2 * half + s, :, here].astype(jnp.float32)
             scanned = out_ref[s, pl.ds(slot, rows, stride=8), :] + skip * smooth
-            gate = gates[s][0, :, here].astype(jnp.float32)
-            gated = scanned * (gate / (1.0 + jnp.exp(-gate)))
+            scanned_ref[s, :, here] = scanned
+
+
+def output_kernel(half, *refs):
+    slots = refs[:-6]
+    scanned_ref, g0_ref, g1_ref, keep_ref, send_ref, gated_ref = refs[-6:]
+    rows = keep_ref.shape[0]
+    gates = [g0_ref.at[0] if half else g0_ref, g1_ref.at[half]]
+    for s in range(2):
+        for slot in range(8):
+            here = slice(slot * HEAD, (slot + 1) * HEAD)
+            gate = gates[s][:, here].astype(jnp.float32)
+            gated = scanned_ref[s, :, here] * (gate / (1.0 + jnp.exp(-gate)))
             gated_ref[s * rows : (s + 1) * rows, here] = gated.astype(jnp.bfloat16)
-
-
-def output_kernel(*refs):
-    slots, gated_ref, (keep_ref, send_ref) = refs[:8], refs[8], refs[9:]
-    rows = keep_ref.shape[0]
     width = 512
     for begin in range(0, keep_ref.shape[1], width):
         columns = slice(begin, begin + width)
-        weight = jnp.concatenate([slots[slot][:, columns] for slot in range(8)], axis=0)
+        weight = jnp.concatenate([slot[:, columns] for slot in slots], axis=0)
         total = jnp.dot(gated_ref[...], weight, preferred_element_type=jnp.float32)
         keep_ref[:, columns] = total[:rows]
         send_ref[:, columns] = total[rows:].astype(send_ref.dtype)
@@ -396,78 +460,100 @@
         axis=0,
     )
 
-    def gathered(own):
-        slots = [None] * 8
-        slots[0] = own
-        for even in (2, 4, 6):
-            slots[even] = swap(own, GROUP * even, count)
-        for even in (0, 2, 4, 6):
-            slots[even + 1] = swap(slots[even], GROUP, count)
-        return slots
-
-    packs = gathered(pack)
-    half = jax.ShapeDtypeStruct((2, rows, 8 * HEAD), jnp.bfloat16)
-    keep, send, gkeep, gsend = local_call(
-        attention_kernel, (half,) * 4, "attention",
-        flops=4 * 32 * rows * rows * HEAD, bytes_accessed=6 << 20, transcendentals=32 * rows * rows,
-    )(query[0], key[0], value[0], gate_input[0])
-    x1 = swap(keep[1:2], 2, count)
-    recv = swap(send, 1, count)
-    x2 = swap(recv[1:2], 2, count)
-    grecv = swap(gsend, 1, count)
-    gx1 = swap(gkeep[1:2], 2, count)
-    gx2 = swap(grecv[1:2], 2, count)
-    slots = gathered(out_proj)
+    near, far = MEMBERS
+    bit_x, bit_y, bit_z = SLOTS
+
+    pack_z = swap(pack, bit_z, count)
+    slot_x = swap(out_proj, bit_x, count)
+    slot_y = swap(out_proj, bit_y, count)
+    pack_two = jnp.concatenate([pack, pack_z], axis=0)
+    pack_x = swap(pack_two, bit_x, count)
+    pack_y = swap(pack_two, bit_y, count)
+    pack_xy = swap(after(pack_y[:PACK_ROWS], slot_x), bit_x, count)
+    pack_xyz = swap(after(pack_x[PACK_ROWS:], slot_y), bit_y, count)
+    packs = [pack, pack_z, pack_x, pack_y, pack_xy, pack_xyz]
+    slot_xy = swap(slot_y, bit_x, count)
+    slot_z = swap(out_proj, bit_z, count)
+    slot_zx = swap(slot_z, bit_x, count)
+    slot_zy = swap(slot_z, bit_y, count)
+    slot_zxy = swap(slot_zx, bit_y, count)
+    slots = [out_proj, slot_x, slot_y, slot_xy, slot_z, slot_zx, slot_zy, slot_zxy]
+
+    quarter = jax.ShapeDtypeStruct((rows, 8 * HEAD), jnp.bfloat16)
+    both = jax.ShapeDtypeStruct((2, rows, 8 * HEAD), jnp.bfloat16)
+
+    def spread(own, across, send):
+        arrived = swap(send, near, count)
+        pair = swap(jnp.stack([across, arrived[1]]), far, count)
+        return own, arrived, pair
+
+    made = local_call(
+        attention_kernel,
+        (quarter, quarter, both),
+        "attention",
+        COST["attention"],
+        scratch=[
+            pltpu.VMEM(query.shape[1:], jnp.bfloat16),
+            pltpu.VMEM(key.shape[1:], jnp.bfloat16),
+            pltpu.VMEM(value.shape[1:], jnp.bfloat16),
+            pltpu.SemaphoreType.DMA((3,)),
+        ],
+        away=3,
+    )(query[0], key[0], value[0])
+    mixed = spread(*made)
     wide = jax.ShapeDtypeStruct((rows, 640), jnp.float32)
     smooth, pkeep, psend = local_call(
         project_kernel,
         (jax.ShapeDtypeStruct((GROUP, rows, 8 * HEAD), jnp.bfloat16), wide, wide),
         "project",
+        COST["project"],
         scratch=[pltpu.VMEM((288, 8 * HEAD), jnp.bfloat16)],
-        flops=2 * GROUP * rows * 1024 * 288, bytes_accessed=4 << 20, transcendentals=GROUP * rows * 1024,
-    )(*packs, keep, recv, x1, x2)
-    chip = pkeep + swap(psend, 1, count)
-    other = swap(chip, 2, count)
-    other = jnp.concatenate(
-        [other[:, 256:512], other[:, :256], other[:, 544:576], other[:, 512:544], other[:, 576:]],
-        axis=1,
-    )
-    full = chip + other
-    partner = swap(full, 1, count)
-
-    def scanned(which, gate_a, gate_b):
+        waits=[slots[i] for i in WAITS["project"]],
+    )(*packs, *mixed)
+    chip = local_call(
+        add_kernel, wide, "add", waits=[slots[i] for i in WAITS["add"]]
+    )(pkeep, swap(psend, near, count))
+    full = local_call(
+        combine_kernel, wide, "combine", COST["combine"], waits=[slots[i] for i in WAITS["combine"]]
+    )(chip, swap(chip, far, count))
+    partner = swap(full, near, count)
+    gate_source = after(gate_input[0], psend)
+    gates = spread(*local_call(gates_kernel, (quarter, quarter, both), "gates")(gate_source))
+
+    def scanned(which, waits):
+        work = pltpu.VMEM((2, rows * 8, HEAD), jnp.float32)
+        lanes = pltpu.VMEM((2, rows * STATES, HEAD), jnp.float32)
         return local_call(
             functools.partial(scan_kernel, which),
-            jax.ShapeDtypeStruct((2 * rows, 8 * HEAD), jnp.bfloat16),
+            jax.ShapeDtypeStruct((2, rows, 8 * HEAD), jnp.float32),
             "scan",
-            scratch=[
-                pltpu.VMEM((2, rows * 8, HEAD), jnp.float32),
-                pltpu.VMEM((2, rows * 8, HEAD), jnp.float32),
-                pltpu.VMEM((2, rows * 8, HEAD), jnp.float32),
-                pltpu.VMEM((STATES * 8, HEAD), jnp.float32),
-                pltpu.VMEM((2, rows * STATES, HEAD), jnp.float32),
-                pltpu.VMEM((2, rows * STATES, HEAD), jnp.float32),
-            ],
-            flops=16 * 1024 * 256 * 256, bytes_accessed=4 << 20, transcendentals=256 * 1024 * 16,
-        )(*packs, full, partner, smooth, gate_a, gate_b)
-
-    def projected_out(gated):
+            COST["scan"],
+            scratch=[work, work, work, pltpu.VMEM((STATES * 8, HEAD), jnp.float32), lanes, lanes],
+            waits=waits,
+        )(*packs, full, partner, smooth)
+
+    def projected_out(which, *args):
         return local_call(
-            output_kernel,
+            functools.partial(output_kernel, which),
             (
                 jax.ShapeDtypeStruct((rows, width), jnp.float32),
                 jax.ShapeDtypeStruct((rows, width), jnp.bfloat16),
             ),
             "output",
-            flops=2 * 2 * rows * 1024 * width, bytes_accessed=6 << 20,
-        )(*slots, gated)
-
-    far_keep, far_send = projected_out(scanned(1, gx1, gx2))
-    far = (far_keep + swap(far_send, 1, count).astype(jnp.float32)).astype(jnp.bfloat16)
-    from_far = swap(far, 2, count)
-    near_keep, near_send = projected_out(scanned(0, gkeep[0:1], grecv[0:1]))
-    near = near_keep + swap(near_send, 1, count).astype(jnp.float32)
-    return (near + from_far.astype(jnp.float32)).astype(jnp.bfloat16)[None]
+            COST["output"],
+            scratch=[pltpu.VMEM((2 * rows, 8 * HEAD), jnp.bfloat16)],
+        )(*slots, *args)
+
+    own_gate, sent_gate, pair_gate = gates
+    far_keep, far_send = projected_out(
+        1, scanned(1, [slots[i] for i in WAITS["scan"]]), pair_gate, pair_gate
+    )
+    far_sum = (far_keep + swap(far_send, near, count).astype(jnp.float32)).astype(jnp.bfloat16)
+    from_far = swap(far_sum, far, count)
+    near_keep, near_send = projected_out(0, scanned(0, [far_sum]), own_gate, sent_gate)
+    from_near = swap(after(near_send, from_far), near, count)
+    near_sum = near_keep + from_near.astype(jnp.float32) + from_far.astype(jnp.float32)
+    return near_sum.astype(jnp.bfloat16)[None]
 
 
 def solution(mesh):

time: 141 us -> 102 us (0.72)
  waiting for transfers between devices: 68.7 us -> 42.3 us
  local copies, waits for them, and re-layouts: 14 us -> 5.63 us
  starting transfers between devices: 29 us -> 24.1 us
    ppermute x26 -> x22, waiting for transfers between devices: 68.7 us -> 42.3 us  [swap(): return lax.ppermute(value, 'dp', [(i, i ^ distance) for i in range(count)])]
    ppermute x26 -> x22, starting transfers between devices: 29 us -> 24.1 us  [swap(): return lax.ppermute(value, 'dp', [(i, i ^ distance) for i in range(count)])]
    unnamed x70 -> x28, local copies, waits for them, and re-layouts: 8.89 us -> 5.1 us
    slice x7 -> x4, local copies, waits for them, and re-layouts: 3.02 us -> 0.06 us  [the longest x2 0.04 us: spread(): pair = swap(jnp.stack([across, arrived[1]]), far, count)]
    concatenate x1, local copies, waits for them, and re-layouts: 1.85 us -> 0.27 us  [grouped(): pack_two = jnp.concatenate([pack, pack_z], axis=0)]
    pallas_call x6 -> x9, Pallas kernels: 26.4 us -> 25.8 us  [call(): pl.pallas_call(kernel, out_shape=out_shape, in_specs=[anywhere] * away +...]
  transfers between devices with their start and end apart: 26 -> 22, of which waited for: 11 -> 11; matrix products, arithmetic and copies ran while one was open for 5% -> 1% of each run, Pallas kernels for 14% -> 20%
where the time goes in v2:
time: 102 us
  waiting for transfers between devices  42.3 us (41%)
  Pallas kernels  25.8 us (25%)
  starting transfers between devices  24.1 us (24%)
  local copies, waits for them, and re-layouts  5.63 us (6%)
  other arithmetic  3.64 us (4%)
    ppermute x22, waiting for transfers between devices, swap(): return lax.ppermute(value, 'dp', [(i, i ^ distance) for i in range(count)])  42.3 us
    pallas_call x9, Pallas kernels, call(): pl.pallas_call(kernel, out_shape=out_shape, in_specs=[anywhere] * away +...  25.8 us
    ppermute x22, starting transfers between devices, swap(): return lax.ppermute(value, 'dp', [(i, i ^ distance) for i in range(count)])  24.1 us
    unnamed x28, local copies, waits for them, and re-layouts  5.1 us
    broadcast_in_dim x1, other arithmetic, grouped(): return near_sum.astype(jnp.bfloat16)[None]  2.21 us
  transfers between devices with their start and end apart: 22, of which 11 were waited for; matrix products, arithmetic and copies ran while one was open for 1% of the time, Pallas kernels for 20%

profile of v2, /device:TPU:0, one launch (start us, length us, event | category | flops | bytes accessed | tf_op | source)
XLA Modules:
  0.0 101.8 jit_solution(4793218631316227627)
XLA Ops:
  0.0 1.2 %copy-done.3 = bf16[1,128,4096]{2,1,0:T(8,128)(2,1)S(1)} copy-done((bf16[1,128,4096]{2,1,0:T(8,128)(2,1)S(1)}, bf16[1,128,4096]{2,1,0:T(8,128)(2,1)}, u32[]{:S(2)}) %copy-start.3) | copy-done | bytes 1048600
  1.2 0.9 copy-done.5
  2.2 0.9 copy-done.6
  3.2 1.7 %attention.1 = (bf16[128,1024]{1,0:T(8,128)(2,1)S(1)}, bf16[128,1024]{1,0:T(8,128)(2,1)S(1)}, bf16[2,128,1024]{2,1,0:T(8,128)(2,1)S(1)}) custom-call(bf16[128,4096]{1,0:T(8,128)(2,1)S(1)} %bitcast.12, bf16[128,1024]{1,0:T(8,128)(2,1)S(1)} %bitcast.14, bf16[128,1024]{1,0:T(8,128)(2,1)S(1)} %bitcast.15), custom_call_target="tpu_custom_call" | custom-call | flops 1 | bytes 18450000 | tf_op jit(solution)/shard_map/attention/pallas_call | solution.py:225
  4.8 0.5 collective-permute-start.12
  5.4 0.2 concatenate.7.refs_0_
  5.6 3.7 %collective-permute-start.7 = (bf16[576,128]{1,0:T(8,128)(2,1)S(1)}, bf16[576,128]{1,0:T(8,128)(2,1)S(1)}, u32[]{:S(2)}, u32[]{:S(2)}) collective-permute-start(bf16[576,128]{1,0:T(8,128)(2,1)S(1)} %concatenate.7.refs_0_), channel_id=1, source_target_pairs={{0,16},{1,17},{2,18},{3,19},{4,20},{5,21},{6,22},{7,23},{8,24},{9,... | collective-permute-start | bytes 442376 | tf_op jit(solution)/shard_map/ppermute | solution.py:219
  9.3 7.6 %collective-permute-done.7.refs_1_ = bf16[576,128]{1,0:T(8,128)(2,1)S(1)} collective-permute-done((bf16[576,128]{1,0:T(8,128)(2,1)S(1)}, bf16[576,128]{1,0:T(8,128)(2,1)S(1)}, u32[]{:S(2)}, u32[]{:S(2)}) %collective-permute-start.7) | collective-permute-done | bytes 147488 | tf_op jit(solution)/shard_map/ppermute | solution.py:219
  17.0 0.3 concatenate.8
  17.2 1.6 %collective-permute-start.9 = (bf16[1152,128]{1,0:T(8,128)(2,1)S(1)}, bf16[1152,128]{1,0:T(8,128)(2,1)S(1)}, u32[]{:S(2)}, u32[]{:S(2)}) collective-permute-start(bf16[1152,128]{1,0:T(8,128)(2,1)S(1)} %concatenate.8), channel_id=1, source_target_pairs={{0,4},{1,5},{2,6},{3,7},{4,0},{5,1},{6,2},{7,3},{8,12},{9,13},{10,... | collective-permute-start | bytes 884744 | tf_op jit(solution)/shard_map/ppermute | solution.py:219
  18.9 0.4 collective-permute-start.1
  19.3 1.5 %collective-permute-start = (bf16[128,2048]{1,0:T(8,128)(2,1)S(1)}, bf16[128,2048]{1,0:T(8,128)(2,1)S(1)}, u32[]{:S(2)}, u32[]{:S(2)}) collective-permute-start(bf16[128,2048]{1,0:T(8,128)(2,1)S(1)} %copy-done.2), channel_id=1, source_target_pairs={{0,2},{1,3},{2,0},{3,1},{4,6},{5,7},{6,4},{7,5},{8,10},{9,11},{10,... | collective-permute-start | bytes 1572872 | tf_op jit(solution)/shard_map/ppermute | solution.py:219
  20.9 0.1 pad_maximum_fusion
  21.0 4.1 %collective-permute-start.13 = (bf16[2,128,1024]{2,1,0:T(8,128)(2,1)S(1)}, bf16[2,128,1024]{2,1,0:T(8,128)(2,1)S(1)}, u32[]{:S(2)}, u32[]{:S(2)}) collective-permute-start(bf16[2,128,1024]{2,1,0:T(8,128)(2,1)S(1)} %pad_maximum_fusion), channel_id=1, source_target_pairs={{0,8},{1,9},{2,10},{3,11},{4,12},{5,13},{6,14},{7,15},{8,0},{9,1},... | collective-permute-start | bytes 1572872 | tf_op jit(solution)/shard_map/ppermute | solution.py:219
  25.1 2.1 %collective-permute-done.9.refs_3_ = bf16[1152,128]{1,0:T(8,128)(2,1)S(1)} collective-permute-done((bf16[1152,128]{1,0:T(8,128)(2,1)S(1)}, bf16[1152,128]{1,0:T(8,128)(2,1)S(1)}, u32[]{:S(2)}, u32[]{:S(2)}) %collective-permute-start.9) | collective-permute-done | bytes 294944 | tf_op jit(solution)/shard_map/ppermute | solution.py:219
  27.2 1.6 %collective-permute-start.8 = (bf16[1152,128]{1,0:T(8,128)(2,1)S(1)}, bf16[1152,128]{1,0:T(8,128)(2,1)S(1)}, u32[]{:S(2)}, u32[]{:S(2)}) collective-permute-start(bf16[1152,128]{1,0:T(8,128)(2,1)S(1)} %concatenate.8), channel_id=1, source_target_pairs={{0,2},{1,3},{2,0},{3,1},{4,6},{5,7},{6,4},{7,5},{8,10},{9,11},{10,... | collective-permute-start | bytes 884744 | tf_op jit(solution)/shard_map/ppermute | solution.py:219
  28.8 10.0 %collective-permute-done.8.refs_2_ = bf16[1152,128]{1,0:T(8,128)(2,1)S(1)} collective-permute-done((bf16[1152,128]{1,0:T(8,128)(2,1)S(1)}, bf16[1152,128]{1,0:T(8,128)(2,1)S(1)}, u32[]{:S(2)}, u32[]{:S(2)}) %collective-permute-start.8) | collective-permute-done | bytes 294944 | tf_op jit(solution)/shard_map/ppermute | solution.py:219
  38.8 1.4 %collective-permute-start.11 = (bf16[576,128]{1,0:T(8,128)(2,1)S(1)}, bf16[576,128]{1,0:T(8,128)(2,1)S(1)}, u32[]{:S(2)}, u32[]{:S(2)}) collective-permute-start(bf16[576,128]{1,0:T(8,128)(2,1)S(1)} %slice.17), channel_id=1, source_target_pairs={{0,4},{1,5},{2,6},{3,7},{4,0},{5,1},{6,2},{7,3},{8,12},{9,13},{10,... | collective-permute-start | bytes 442376 | tf_op jit(solution)/shard_map/ppermute | solution.py:219
  40.3 1.5 %collective-permute-start.10 = (bf16[576,128]{1,0:T(8,128)(2,1)S(1)}, bf16[576,128]{1,0:T(8,128)(2,1)S(1)}, u32[]{:S(2)}, u32[]{:S(2)}) collective-permute-start(bf16[576,128]{1,0:T(8,128)(2,1)S(1)} %slice.16), channel_id=1, source_target_pairs={{0,2},{1,3},{2,0},{3,1},{4,6},{5,7},{6,4},{7,5},{8,10},{9,11},{10,... | collective-permute-start | bytes 442376 | tf_op jit(solution)/shard_map/ppermute | solution.py:219
  41.8 4.0 %collective-permute-done.3.refs_4_ = bf16[128,2048]{1,0:T(8,128)(2,1)S(1)} collective-permute-done((bf16[128,2048]{1,0:T(8,128)(2,1)S(1)}, bf16[128,2048]{1,0:T(8,128)(2,1)S(1)}, u32[]{:S(2)}, u32[]{:S(2)}) %collective-permute-start.3) | collective-permute-done | bytes 524320 | tf_op jit(solution)/shard_map/ppermute | solution.py:219
  45.8 0.7 collective-permute-start.4
  46.5 2.1 %project.1 = (bf16[4,128,1024]{2,1,0:T(8,128)(2,1)S(1)}, f32[128,640]{1,0:T(8,128)S(1)}, f32[128,640]{1,0:T(8,128)S(1)}) custom-call(bf16[576,128]{1,0:T(8,128)(2,1)S(1)} %concatenate.7.refs_0_, bf16[576,128]{1,0:T(8,128)(2,1)S(1)} %collective-permute-done.7.refs_1_, bf16[1152,128]{1,0:T(8,128)(2,1)S(1)} %collective-permute-done.8.refs_2_, ...), custom_call_target="tpu_custom_call" | custom-call | flops 1 | tf_op jit(solution)/shard_map/project/pallas_call | solution.py:225
  48.7 0.3 gates.1
  48.9 0.1 collective-permute-start.17
  49.0 0.5 collective-permute-start.14
  49.5 1.9 %collective-permute-done.14.b_ref = f32[128,640]{1,0:T(8,128)S(1)} collective-permute-done((f32[128,640]{1,0:T(8,128)S(1)}, f32[128,640]{1,0:T(8,128)S(1)}, u32[]{:S(2)}, u32[]{:S(2)}) %collective-permute-start.14) | collective-permute-done | bytes 327712 | tf_op jit(solution)/shard_map/ppermute | solution.py:219
  51.4 0.1 collective-permute-start.15
  51.5 1.4 %collective-permute-start.5 = (bf16[128,2048]{1,0:T(8,128)(2,1)S(1)}, bf16[128,2048]{1,0:T(8,128)(2,1)S(1)}, u32[]{:S(2)}, u32[]{:S(2)}) collective-permute-start(bf16[128,2048]{1,0:T(8,128)(2,1)S(1)} %collective-permute-done.3.refs_4_), channel_id=1, source_target_pairs={{0,4},{1,5},{2,6},{3,7},{4,0},{5,1},{6,2},{7,3},{8,12},{9,13},{10,... | collective-permute-start | bytes 1572872 | tf_op jit(solution)/shard_map/ppermute | solution.py:219
  52.9 1.5 %collective-permute-start.2 = (bf16[128,2048]{1,0:T(8,128)(2,1)S(1)}, bf16[128,2048]{1,0:T(8,128)(2,1)S(1)}, u32[]{:S(2)}, u32[]{:S(2)}) collective-permute-start(bf16[128,2048]{1,0:T(8,128)(2,1)S(1)} %collective-permute-done.1.refs_2_), channel_id=1, source_target_pairs={{0,2},{1,3},{2,0},{3,1},{4,6},{5,7},{6,4},{7,5},{8,10},{9,11},{10,... | collective-permute-start | bytes 1572872 | tf_op jit(solution)/shard_map/ppermute | solution.py:219
  54.4 6.2 %collective-permute-done.4.refs_5_ = bf16[128,2048]{1,0:T(8,128)(2,1)S(1)} collective-permute-done((bf16[128,2048]{1,0:T(8,128)(2,1)S(1)}, bf16[128,2048]{1,0:T(8,128)(2,1)S(1)}, u32[]{:S(2)}, u32[]{:S(2)}) %collective-permute-start.4) | collective-permute-done | bytes 524320 | tf_op jit(solution)/shard_map/ppermute | solution.py:219
  60.7 1.5 %collective-permute-start.6 = (bf16[128,2048]{1,0:T(8,128)(2,1)S(1)}, bf16[128,2048]{1,0:T(8,128)(2,1)S(1)}, u32[]{:S(2)}, u32[]{:S(2)}) collective-permute-start(bf16[128,2048]{1,0:T(8,128)(2,1)S(1)} %collective-permute-done.4.refs_5_), channel_id=1, source_target_pairs={{0,4},{1,5},{2,6},{3,7},{4,0},{5,1},{6,2},{7,3},{8,12},{9,13},{10,... | collective-permute-start | bytes 1572872 | tf_op jit(solution)/shard_map/ppermute | solution.py:219
  62.3 0.1 collective-permute-start.18
  62.3 0.1 combine.1.refs_6_
  62.5 0.1 collective-permute-start.16
  62.5 1.6 %collective-permute-done.16.refs_7_ = f32[128,640]{1,0:T(8,128)S(1)} collective-permute-done((f32[128,640]{1,0:T(8,128)S(1)}, f32[128,640]{1,0:T(8,128)S(1)}, u32[]{:S(2)}, u32[]{:S(2)}) %collective-permute-start.16) | collective-permute-done | bytes 327712 | tf_op jit(solution)/shard_map/ppermute | solution.py:219
  64.2 7.2 %scan.2.refs_8_ = f32[2,128,1024]{2,1,0:T(8,128)S(1)} custom-call(bf16[576,128]{1,0:T(8,128)(2,1)S(1)} %concatenate.7.refs_0_, bf16[576,128]{1,0:T(8,128)(2,1)S(1)} %collective-permute-done.7.refs_1_, bf16[1152,128]{1,0:T(8,128)(2,1)S(1)} %collective-permute-done.8.refs_2_, bf16[1152,128]{1,0:T(8,128)(2,1)S(1)} %collective-permute-done.9.refs_3_, ...), custom_call_target="tpu_custom_call" | custom-call | flops 1 | bytes 29520000 | tf_op jit(solution)/shard_map/scan/pallas_call | solution.py:225
  71.3 1.0 copy-done.1
  72.3 4.5 %collective-permute-done.6.refs_7_ = bf16[128,2048]{1,0:T(8,128)(2,1)S(1)} collective-permute-done((bf16[128,2048]{1,0:T(8,128)(2,1)S(1)}, bf16[128,2048]{1,0:T(8,128)(2,1)S(1)}, u32[]{:S(2)}, u32[]{:S(2)}) %collective-permute-start.6) | collective-permute-done | bytes 524320 | tf_op jit(solution)/shard_map/ppermute | solution.py:219
  76.8 3.6 %output.2 = (f32[128,2048]{1,0:T(8,128)}, bf16[128,2048]{1,0:T(8,128)(2,1)S(1)}) custom-call(bf16[128,2048]{1,0:T(8,128)(2,1)S(1)} %copy-done.2, bf16[128,2048]{1,0:T(8,128)(2,1)S(1)} %collective-permute-done.refs_1_, bf16[128,2048]{1,0:T(8,128)(2,1)S(1)} %collective-permute-done.1.refs_2_, bf16[128,2048]{1,0:T(8,128)(2,1)S(1)} %collective-permute-done.2.refs_3_, ...), custom_call_target="tpu_custom_call" | custom-call | flops 1 | tf_op jit(solution)/shard_map/output/pallas_call | solution.py:225
  80.4 1.9 %collective-permute-done.19 = bf16[128,2048]{1,0:T(8,128)(2,1)S(1)} collective-permute-done((bf16[128,2048]{1,0:T(8,128)(2,1)S(1)}, bf16[128,2048]{1,0:T(8,128)(2,1)S(1)}, u32[]{:S(2)}, u32[]{:S(2)}) %collective-permute-start.19) | collective-permute-done | bytes 524320 | tf_op jit(solution)/shard_map/ppermute | solution.py:219
  82.3 1.3 %add_convert_fusion.1.refs_9_ = bf16[128,2048]{1,0:T(8,128)(2,1)S(1)} fusion(f32[128,2048]{1,0:T(8,128)} %get-tuple-element.33, bf16[128,2048]{1,0:T(8,128)(2,1)S(1)} %collective-permute-done.19), kind=kLoop, calls=%fused_computation.1 | loop fusion | flops 786432 | bytes 2097152 | tf_op jit(solution)/shard_map/convert_element_type | solution.py:551
  83.6 1.7 %collective-permute-start.20 = (bf16[128,2048]{1,0:T(8,128)(2,1)S(1)}, bf16[128,2048]{1,0:T(8,128)(2,1)S(1)}, u32[]{:S(2)}, u32[]{:S(2)}) collective-permute-start(bf16[128,2048]{1,0:T(8,128)(2,1)S(1)} %add_convert_fusion.1.refs_9_), channel_id=1, source_target_pairs={{0,8},{1,9},{2,10},{3,11},{4,12},{5,13},{6,14},{7,15},{8,0},{9,1},... | collective-permute-start | bytes 1572872 | tf_op jit(solution)/shard_map/ppermute | solution.py:219
  85.4 7.2 %scan.3.refs_8_ = f32[2,128,1024]{2,1,0:T(8,128)S(1)} custom-call(bf16[576,128]{1,0:T(8,128)(2,1)S(1)} %concatenate.7.refs_0_, bf16[576,128]{1,0:T(8,128)(2,1)S(1)} %collective-permute-done.7.refs_1_, bf16[1152,128]{1,0:T(8,128)(2,1)S(1)} %collective-permute-done.8.refs_2_, bf16[1152,128]{1,0:T(8,128)(2,1)S(1)} %collective-permute-done.9.refs_3_, ...), custom_call_target="tpu_custom_call" | custom-call | flops 1 | bytes 29520000 | tf_op jit(solution)/shard_map/scan/pallas_call | solution.py:225
  92.6 1.0 copy-done
  93.5 3.6 %output.3 = (f32[128,2048]{1,0:T(8,128)}, bf16[128,2048]{1,0:T(8,128)(2,1)S(1)}) custom-call(bf16[128,2048]{1,0:T(8,128)(2,1)S(1)} %copy-done.2, bf16[128,2048]{1,0:T(8,128)(2,1)S(1)} %collective-permute-done.refs_1_, bf16[128,2048]{1,0:T(8,128)(2,1)S(1)} %collective-permute-done.1.refs_2_, bf16[128,2048]{1,0:T(8,128)(2,1)S(1)} %collective-permute-done.2.refs_3_, ...), custom_call_target="tpu_custom_call" | custom-call | flops 1 | tf_op jit(solution)/shard_map/output/pallas_call | solution.py:225
  97.2 0.5 collective-permute-done.20
  97.7 1.9 %collective-permute-done.21 = bf16[128,2048]{1,0:T(8,128)(2,1)S(1)} collective-permute-done((bf16[128,2048]{1,0:T(8,128)(2,1)S(1)}, bf16[128,2048]{1,0:T(8,128)(2,1)S(1)}, u32[]{:S(2)}, u32[]{:S(2)}) %collective-permute-start.21) | collective-permute-done | bytes 524320 | tf_op jit(solution)/shard_map/ppermute | solution.py:219
  99.6 2.2 %fusion = bf16[1,128,2048]{2,1,0:T(8,128)(2,1)} fusion(bf16[128,2048]{1,0:T(8,128)(2,1)S(1)} %collective-permute-done.20, f32[128,2048]{1,0:T(8,128)} %get-tuple-element.36, bf16[128,2048]{1,0:T(8,128)(2,1)S(1)} %collective-permute-done.21), kind=kLoop, calls=%fused_computation.2 | loop fusion | flops 1310720 | bytes 2621440 | tf_op jit(solution)/shard_map/broadcast_in_dim | solution.py:556
  (44 shorter events, 0.2 us)
Async XLA Ops:
  0.0 1.2 %copy-start.3 = (bf16[1,128,4096]{2,1,0:T(8,128)(2,1)S(1)}, bf16[1,128,4096]{2,1,0:T(8,128)(2,1)}, u32[]{:S(2)}) copy-start(bf16[1,128,4096]{2,1,0:T(8,128)(2,1)} %param.12) | copy-start | bytes 3145732
  1.2 0.9 copy-start.5
  2.2 0.9 copy-start.6
  3.1 2.2 %copy-start.7 = (bf16[128,288]{0,1:T(8,128)(2,1)S(1)}, bf16[128,288]{0,1:T(8,128)(2,1)}, u32[]{:S(2)}) copy-start(bf16[128,288]{0,1:T(8,128)(2,1)} %param.18) | copy-start | bytes 221188
  3.1 2.2 %copy-start.8 = (bf16[256,128]{1,0:T(8,128)(2,1)S(1)}, bf16[256,128]{1,0:T(8,128)(2,1)}, u32[]{:S(2)}) copy-start(bf16[256,128]{1,0:T(8,128)(2,1)} %param.19) | copy-start | bytes 196612
  3.1 2.2 %copy-start.9 = (bf16[16,128]{1,0:T(8,128)(2,1)S(1)}, bf16[16,128]{1,0:T(8,128)(2,1)}, u32[]{:S(2)}) copy-start(bf16[16,128]{1,0:T(8,128)(2,1)} %param.21) | copy-start | bytes 12292
  3.1 2.3 %copy-start.10 = (bf16[4,128]{1,0:T(4,128)(2,1)S(1)}, bf16[4,128]{1,0:T(4,128)(2,1)}, u32[]{:S(2)}) copy-start(bf16[4,128]{1,0:T(4,128)(2,1)} %param.16) | copy-start | bytes 3076
  3.1 2.3 %copy-start.11 = (bf16[128]{0:T(256)(128)(2,1)S(1)}, bf16[128]{0:T(256)(128)(2,1)}, u32[]{:S(2)}) copy-start(bf16[128]{0:T(256)(128)(2,1)} %param.17) | copy-start | bytes 772
  3.1 2.3 %copy-start.12 = (bf16[128]{0:T(256)(128)(2,1)S(1)}, bf16[128]{0:T(256)(128)(2,1)}, u32[]{:S(2)}) copy-start(bf16[128]{0:T(256)(128)(2,1)} %param.20) | copy-start | bytes 772
  3.2 2.3 %copy-start.13 = (bf16[128]{0:T(256)(128)(2,1)S(1)}, bf16[128]{0:T(256)(128)(2,1)}, u32[]{:S(2)}) copy-start(bf16[128]{0:T(256)(128)(2,1)} %param.22) | copy-start | bytes 772
  4.8 14.0 %copy-start.2 = (bf16[128,2048]{1,0:T(8,128)(2,1)S(1)}, bf16[128,2048]{1,0:T(8,128)(2,1)}, u32[]{:S(2)}) copy-start(bf16[128,2048]{1,0:T(8,128)(2,1)} %refs_0_.3) | copy-start | bytes 1572868
  4.8 16.0 %collective-permute-start.12 = (bf16[2,128,1024]{2,1,0:T(8,128)(2,1)S(1)}, bf16[2,128,1024]{2,1,0:T(8,128)(2,1)S(1)}, u32[]{:S(2)}, u32[]{:S(2)}) collective-permute-start(bf16[2,128,1024]{2,1,0:T(8,128)(2,1)S(1)} %get-tuple-element.25), channel_id=1, source_target_pairs={{0,1},{1,0},{2,3},{3,2},{4,5},{5,4},{6,7},{7,6},{8,9},{9,8},{10,11... | collective-permute-start | bytes 1572872 | tf_op jit(solution)/shard_map/ppermute | solution.py:219
  5.6 11.3 %collective-permute-start.7 = (bf16[576,128]{1,0:T(8,128)(2,1)S(1)}, bf16[576,128]{1,0:T(8,128)(2,1)S(1)}, u32[]{:S(2)}, u32[]{:S(2)}) collective-permute-start(bf16[576,128]{1,0:T(8,128)(2,1)S(1)} %concatenate.7.refs_0_), channel_id=1, source_target_pairs={{0,16},{1,17},{2,18},{3,19},{4,20},{5,21},{6,22},{7,23},{8,24},{9,... | collective-permute-start | bytes 442376 | tf_op jit(solution)/shard_map/ppermute | solution.py:219
  17.2 9.9 %collective-permute-start.9 = (bf16[1152,128]{1,0:T(8,128)(2,1)S(1)}, bf16[1152,128]{1,0:T(8,128)(2,1)S(1)}, u32[]{:S(2)}, u32[]{:S(2)}) collective-permute-start(bf16[1152,128]{1,0:T(8,128)(2,1)S(1)} %concatenate.8), channel_id=1, source_target_pairs={{0,4},{1,5},{2,6},{3,7},{4,0},{5,1},{6,2},{7,3},{8,12},{9,13},{10,... | collective-permute-start | bytes 884744 | tf_op jit(solution)/shard_map/ppermute | solution.py:219
  18.9 20.0 %collective-permute-start.1 = (bf16[128,2048]{1,0:T(8,128)(2,1)S(1)}, bf16[128,2048]{1,0:T(8,128)(2,1)S(1)}, u32[]{:S(2)}, u32[]{:S(2)}) collective-permute-start(bf16[128,2048]{1,0:T(8,128)(2,1)S(1)} %copy-done.2), channel_id=1, source_target_pairs={{0,4},{1,5},{2,6},{3,7},{4,0},{5,1},{6,2},{7,3},{8,12},{9,13},{10,... | collective-permute-start | bytes 1572872 | tf_op jit(solution)/shard_map/ppermute | solution.py:219
  19.3 21.0 %collective-permute-start = (bf16[128,2048]{1,0:T(8,128)(2,1)S(1)}, bf16[128,2048]{1,0:T(8,128)(2,1)S(1)}, u32[]{:S(2)}, u32[]{:S(2)}) collective-permute-start(bf16[128,2048]{1,0:T(8,128)(2,1)S(1)} %copy-done.2), channel_id=1, source_target_pairs={{0,2},{1,3},{2,0},{3,1},{4,6},{5,7},{6,4},{7,5},{8,10},{9,11},{10,... | collective-permute-start | bytes 1572872 | tf_op jit(solution)/shard_map/ppermute | solution.py:219
  20.9 24.9 %collective-permute-start.3 = (bf16[128,2048]{1,0:T(8,128)(2,1)S(1)}, bf16[128,2048]{1,0:T(8,128)(2,1)S(1)}, u32[]{:S(2)}, u32[]{:S(2)}) collective-permute-start(bf16[128,2048]{1,0:T(8,128)(2,1)S(1)} %copy-done.2), channel_id=1, source_target_pairs={{0,16},{1,17},{2,18},{3,19},{4,20},{5,21},{6,22},{7,23},{8,24},{9,... | collective-permute-start | bytes 1572872 | tf_op jit(solution)/shard_map/ppermute | solution.py:219
  21.0 25.5 %collective-permute-start.13 = (bf16[2,128,1024]{2,1,0:T(8,128)(2,1)S(1)}, bf16[2,128,1024]{2,1,0:T(8,128)(2,1)S(1)}, u32[]{:S(2)}, u32[]{:S(2)}) collective-permute-start(bf16[2,128,1024]{2,1,0:T(8,128)(2,1)S(1)} %pad_maximum_fusion), channel_id=1, source_target_pairs={{0,8},{1,9},{2,10},{3,11},{4,12},{5,13},{6,14},{7,15},{8,0},{9,1},... | collective-permute-start | bytes 1572872 | tf_op jit(solution)/shard_map/ppermute | solution.py:219
  27.2 11.6 %collective-permute-start.8 = (bf16[1152,128]{1,0:T(8,128)(2,1)S(1)}, bf16[1152,128]{1,0:T(8,128)(2,1)S(1)}, u32[]{:S(2)}, u32[]{:S(2)}) collective-permute-start(bf16[1152,128]{1,0:T(8,128)(2,1)S(1)} %concatenate.8), channel_id=1, source_target_pairs={{0,2},{1,3},{2,0},{3,1},{4,6},{5,7},{6,4},{7,5},{8,10},{9,11},{10,... | collective-permute-start | bytes 884744 | tf_op jit(solution)/shard_map/ppermute | solution.py:219
  38.8 7.6 %collective-permute-start.11 = (bf16[576,128]{1,0:T(8,128)(2,1)S(1)}, bf16[576,128]{1,0:T(8,128)(2,1)S(1)}, u32[]{:S(2)}, u32[]{:S(2)}) collective-permute-start(bf16[576,128]{1,0:T(8,128)(2,1)S(1)} %slice.17), channel_id=1, source_target_pairs={{0,4},{1,5},{2,6},{3,7},{4,0},{5,1},{6,2},{7,3},{8,12},{9,13},{10,... | collective-permute-start | bytes 442376 | tf_op jit(solution)/shard_map/ppermute | solution.py:219
  40.3 6.2 %collective-permute-start.10 = (bf16[576,128]{1,0:T(8,128)(2,1)S(1)}, bf16[576,128]{1,0:T(8,128)(2,1)S(1)}, u32[]{:S(2)}, u32[]{:S(2)}) collective-permute-start(bf16[576,128]{1,0:T(8,128)(2,1)S(1)} %slice.16), channel_id=1, source_target_pairs={{0,2},{1,3},{2,0},{3,1},{4,6},{5,7},{6,4},{7,5},{8,10},{9,11},{10,... | collective-permute-start | bytes 442376 | tf_op jit(solution)/shard_map/ppermute | solution.py:219
  45.8 14.9 %collective-permute-start.4 = (bf16[128,2048]{1,0:T(8,128)(2,1)S(1)}, bf16[128,2048]{1,0:T(8,128)(2,1)S(1)}, u32[]{:S(2)}, u32[]{:S(2)}) collective-permute-start(bf16[128,2048]{1,0:T(8,128)(2,1)S(1)} %collective-permute-done.3.refs_4_), channel_id=1, source_target_pairs={{0,2},{1,3},{2,0},{3,1},{4,6},{5,7},{6,4},{7,5},{8,10},{9,11},{10,... | collective-permute-start | bytes 1572872 | tf_op jit(solution)/shard_map/ppermute | solution.py:219
  46.5 2.2 %copy-start.4 = (bf16[1,128,4096]{2,1,0:T(8,128)(2,1)S(1)}, bf16[1,128,4096]{2,1,0:T(8,128)(2,1)}, u32[]{:S(2)}) copy-start(bf16[1,128,4096]{2,1,0:T(8,128)(2,1)} %param.15) | copy-start | bytes 3145732
  48.9 13.2 %collective-permute-start.17 = (bf16[2,128,1024]{2,1,0:T(8,128)(2,1)S(1)}, bf16[2,128,1024]{2,1,0:T(8,128)(2,1)S(1)}, u32[]{:S(2)}, u32[]{:S(2)}) collective-permute-start(bf16[2,128,1024]{2,1,0:T(8,128)(2,1)S(1)} %get-tuple-element.32), channel_id=1, source_target_pairs={{0,1},{1,0},{2,3},{3,2},{4,5},{5,4},{6,7},{7,6},{8,9},{9,8},{10,11... | collective-permute-start | bytes 1572872 | tf_op jit(solution)/shard_map/ppermute | solution.py:219
  49.0 2.4 %collective-permute-start.14 = (f32[128,640]{1,0:T(8,128)S(1)}, f32[128,640]{1,0:T(8,128)S(1)}, u32[]{:S(2)}, u32[]{:S(2)}) collective-permute-start(f32[128,640]{1,0:T(8,128)S(1)} %get-tuple-element.28), channel_id=1, source_target_pairs={{0,1},{1,0},{2,3},{3,2},{4,5},{5,4},{6,7},{7,6},{8,9},{9,8},{10,11... | collective-permute-start | bytes 983048 | tf_op jit(solution)/shard_map/ppermute | solution.py:219
  51.4 10.9 %collective-permute-start.15 = (f32[128,640]{1,0:T(8,128)S(1)}, f32[128,640]{1,0:T(8,128)S(1)}, u32[]{:S(2)}, u32[]{:S(2)}) collective-permute-start(f32[128,640]{1,0:T(8,128)S(1)} %add.20.chip_ref), channel_id=1, source_target_pairs={{0,8},{1,9},{2,10},{3,11},{4,12},{5,13},{6,14},{7,15},{8,0},{9,1},... | collective-permute-start | bytes 983048 | tf_op jit(solution)/shard_map/ppermute | solution.py:219
  51.5 20.8 %collective-permute-start.5 = (bf16[128,2048]{1,0:T(8,128)(2,1)S(1)}, bf16[128,2048]{1,0:T(8,128)(2,1)S(1)}, u32[]{:S(2)}, u32[]{:S(2)}) collective-permute-start(bf16[128,2048]{1,0:T(8,128)(2,1)S(1)} %collective-permute-done.3.refs_4_), channel_id=1, source_target_pairs={{0,4},{1,5},{2,6},{3,7},{4,0},{5,1},{6,2},{7,3},{8,12},{9,13},{10,... | collective-permute-start | bytes 1572872 | tf_op jit(solution)/shard_map/ppermute | solution.py:219
  52.9 19.4 %collective-permute-start.2 = (bf16[128,2048]{1,0:T(8,128)(2,1)S(1)}, bf16[128,2048]{1,0:T(8,128)(2,1)S(1)}, u32[]{:S(2)}, u32[]{:S(2)}) collective-permute-start(bf16[128,2048]{1,0:T(8,128)(2,1)S(1)} %collective-permute-done.1.refs_2_), channel_id=1, source_target_pairs={{0,2},{1,3},{2,0},{3,1},{4,6},{5,7},{6,4},{7,5},{8,10},{9,11},{10,... | collective-permute-start | bytes 1572872 | tf_op jit(solution)/shard_map/ppermute | solution.py:219
  60.7 16.1 %collective-permute-start.6 = (bf16[128,2048]{1,0:T(8,128)(2,1)S(1)}, bf16[128,2048]{1,0:T(8,128)(2,1)S(1)}, u32[]{:S(2)}, u32[]{:S(2)}) collective-permute-start(bf16[128,2048]{1,0:T(8,128)(2,1)S(1)} %collective-permute-done.4.refs_5_), channel_id=1, source_target_pairs={{0,4},{1,5},{2,6},{3,7},{4,0},{5,1},{6,2},{7,3},{8,12},{9,13},{10,... | collective-permute-start | bytes 1572872 | tf_op jit(solution)/shard_map/ppermute | solution.py:219
  62.3 14.5 %collective-permute-start.18 = (bf16[2,128,1024]{2,1,0:T(8,128)(2,1)S(1)}, bf16[2,128,1024]{2,1,0:T(8,128)(2,1)S(1)}, u32[]{:S(2)}, u32[]{:S(2)}) collective-permute-start(bf16[2,128,1024]{2,1,0:T(8,128)(2,1)S(1)} %pad_maximum_fusion.1), channel_id=1, source_target_pairs={{0,8},{1,9},{2,10},{3,11},{4,12},{5,13},{6,14},{7,15},{8,0},{9,1},... | collective-permute-start | bytes 1572872 | tf_op jit(solution)/shard_map/ppermute | solution.py:219
  62.5 1.7 %collective-permute-start.16 = (f32[128,640]{1,0:T(8,128)S(1)}, f32[128,640]{1,0:T(8,128)S(1)}, u32[]{:S(2)}, u32[]{:S(2)}) collective-permute-start(f32[128,640]{1,0:T(8,128)S(1)} %combine.1.refs_6_), channel_id=1, source_target_pairs={{0,1},{1,0},{2,3},{3,2},{4,5},{5,4},{6,7},{7,6},{8,9},{9,8},{10,11... | collective-permute-start | bytes 983048 | tf_op jit(solution)/shard_map/ppermute | solution.py:219
  71.3 1.0 copy-start.1
  80.4 1.9 %collective-permute-start.19 = (bf16[128,2048]{1,0:T(8,128)(2,1)S(1)}, bf16[128,2048]{1,0:T(8,128)(2,1)S(1)}, u32[]{:S(2)}, u32[]{:S(2)}) collective-permute-start(bf16[128,2048]{1,0:T(8,128)(2,1)S(1)} %get-tuple-element.34), channel_id=1, source_target_pairs={{0,1},{1,0},{2,3},{3,2},{4,5},{5,4},{6,7},{7,6},{8,9},{9,8},{10,11... | collective-permute-start | bytes 1572872 | tf_op jit(solution)/shard_map/ppermute | solution.py:219
  83.6 14.0 %collective-permute-start.20 = (bf16[128,2048]{1,0:T(8,128)(2,1)S(1)}, bf16[128,2048]{1,0:T(8,128)(2,1)S(1)}, u32[]{:S(2)}, u32[]{:S(2)}) collective-permute-start(bf16[128,2048]{1,0:T(8,128)(2,1)S(1)} %add_convert_fusion.1.refs_9_), channel_id=1, source_target_pairs={{0,8},{1,9},{2,10},{3,11},{4,12},{5,13},{6,14},{7,15},{8,0},{9,1},... | collective-permute-start | bytes 1572872 | tf_op jit(solution)/shard_map/ppermute | solution.py:219
  92.6 1.0 copy-start
  97.7 1.9 %collective-permute-start.21 = (bf16[128,2048]{1,0:T(8,128)(2,1)S(1)}, bf16[128,2048]{1,0:T(8,128)(2,1)S(1)}, u32[]{:S(2)}, u32[]{:S(2)}) collective-permute-start(bf16[128,2048]{1,0:T(8,128)(2,1)S(1)} %get-tuple-element.38), channel_id=1, source_target_pairs={{0,1},{1,0},{2,3},{3,2},{4,5},{5,4},{6,7},{7,6},{8,9},{9,8},{10,11... | collective-permute-start | bytes 1572872 | tf_op jit(solution)/shard_map/ppermute | solution.py:219

commit v3 on v2

--- a/solution.py
+++ b/solution.py
@@ -211,7 +211,7 @@
 MEMBERS = (1, 8)
 SLOTS = (2, 4, 16)
 COST = {"attention": 5, "project": 0, "combine": 0, "scan": 8, "output": 0}
-WAITS = {"project": (), "add": (), "combine": (), "scan": ()}
+WAITS = {"project": (4,), "add": (), "combine": (), "scan": ()}
 XW, DT, AL, MISC, PACK_ROWS = 0, 288, 544, 560, 576
 
 
@@ -230,7 +230,7 @@
             scratch_shapes=list(scratch),
             name=name,
             cost_estimate=pl.CostEstimate(flops=1, bytes_accessed=weight * 3_690_000, transcendentals=0),
-            compiler_params=pltpu.CompilerParams(vmem_limit_bytes=48 * 1024 * 1024),
+            compiler_params=pltpu.CompilerParams(vmem_limit_bytes=20 * 1024 * 1024),
         )(*args, *waits)
 
     return call
@@ -348,6 +348,12 @@
         target[:, 512 + half * 32 : 512 + half * 32 + 32] = part[:, 256:288]
 
 
+def join_kernel(a_ref, b_ref, *rest):
+    out_ref = rest[-1]
+    out_ref[:PACK_ROWS] = a_ref[...]
+    out_ref[PACK_ROWS:] = b_ref[...]
+
+
 def add_kernel(a_ref, b_ref, *rest):
     rest[-1][...] = a_ref[...] + b_ref[...]
 
@@ -463,22 +469,6 @@
     near, far = MEMBERS
     bit_x, bit_y, bit_z = SLOTS
 
-    pack_z = swap(pack, bit_z, count)
-    slot_x = swap(out_proj, bit_x, count)
-    slot_y = swap(out_proj, bit_y, count)
-    pack_two = jnp.concatenate([pack, pack_z], axis=0)
-    pack_x = swap(pack_two, bit_x, count)
-    pack_y = swap(pack_two, bit_y, count)
-    pack_xy = swap(after(pack_y[:PACK_ROWS], slot_x), bit_x, count)
-    pack_xyz = swap(after(pack_x[PACK_ROWS:], slot_y), bit_y, count)
-    packs = [pack, pack_z, pack_x, pack_y, pack_xy, pack_xyz]
-    slot_xy = swap(slot_y, bit_x, count)
-    slot_z = swap(out_proj, bit_z, count)
-    slot_zx = swap(slot_z, bit_x, count)
-    slot_zy = swap(slot_z, bit_y, count)
-    slot_zxy = swap(slot_zx, bit_y, count)
-    slots = [out_proj, slot_x, slot_y, slot_xy, slot_z, slot_zx, slot_zy, slot_zxy]
-
     quarter = jax.ShapeDtypeStruct((rows, 8 * HEAD), jnp.bfloat16)
     both = jax.ShapeDtypeStruct((2, rows, 8 * HEAD), jnp.bfloat16)
 
@@ -501,6 +491,22 @@
         away=3,
     )(query[0], key[0], value[0])
     mixed = spread(*made)
+    pack_z = swap(pack, bit_z, count)
+    slot_x = swap(out_proj, bit_x, count)
+    slot_y = swap(out_proj, bit_y, count)
+    pack_two = local_call(join_kernel, jax.ShapeDtypeStruct((2 * PACK_ROWS, HEAD), jnp.bfloat16), "join", waits=[slot_x, slot_y])(pack, pack_z)
+    pack_x = swap(pack_two, bit_x, count)
+    pack_y = swap(pack_two, bit_y, count)
+    pack_xy = swap(pack_y[:PACK_ROWS], bit_x, count)
+    pack_xyz = swap(pack_x[PACK_ROWS:], bit_y, count)
+    packs = [pack, pack_z, pack_x, pack_y, pack_xy, pack_xyz]
+    slot_xy = swap(slot_y, bit_x, count)
+    slot_z = swap(after(out_proj, mixed[1]), bit_z, count)
+    slot_zx = swap(slot_z, bit_x, count)
+    slot_zy = swap(slot_z, bit_y, count)
+    slot_zxy = swap(slot_zx, bit_y, count)
+    slots = [out_proj, slot_x, slot_y, slot_xy, slot_z, slot_zx, slot_zy, slot_zxy]
+
     wide = jax.ShapeDtypeStruct((rows, 640), jnp.float32)
     smooth, pkeep, psend = local_call(
         project_kernel,
@@ -517,7 +523,7 @@
         combine_kernel, wide, "combine", COST["combine"], waits=[slots[i] for i in WAITS["combine"]]
     )(chip, swap(chip, far, count))
     partner = swap(full, near, count)
-    gate_source = after(gate_input[0], psend)
+    gate_source = after(gate_input[0], chip)
     gates = spread(*local_call(gates_kernel, (quarter, quarter, both), "gates")(gate_source))
 
     def scanned(which, waits):

time: 102 us -> 93.7 us (0.919)
  waiting for transfers between devices: 42.3 us -> 47.6 us
  starting transfers between devices: 24.1 us -> 18.9 us
  Pallas kernels: 25.8 us -> 21.5 us
  other arithmetic: 3.64 us -> 1.19 us
  local copies, waits for them, and re-layouts: 5.63 us -> 4.06 us
    ppermute x22, waiting for transfers between devices: 42.3 us -> 47.6 us  [swap(): return lax.ppermute(value, 'dp', [(i, i ^ distance) for i in range(count)])]
    ppermute x22, starting transfers between devices: 24.1 us -> 18.9 us  [swap(): return lax.ppermute(value, 'dp', [(i, i ^ distance) for i in range(count)])]
    pallas_call x9 -> x10, Pallas kernels: 25.8 us -> 21.5 us  [call(): pl.pallas_call(kernel, out_shape=out_shape, in_specs=[anywhere] * away +...]
    unnamed x28 -> x24, local copies, waits for them, and re-layouts: 5.1 us -> 3.81 us
    convert_element_type x1, other arithmetic: 1.33 us -> 0.1 us  [grouped(): (far_keep + swap(far_send, near, count).astype(jnp.float32)).astype(jnp.b...]
    broadcast_in_dim x1, other arithmetic: 2.21 us -> 0.98 us  [grouped(): return near_sum.astype(jnp.bfloat16)[None]]
  transfers between devices with their start and end apart: 22 -> 22, of which waited for: 11 -> 15; matrix products, arithmetic and copies ran while one was open for 1% -> 0% of each run, Pallas kernels for 20% -> 17%
where the time goes in v3:
time: 93.7 us; the launch traced here: 93.5 us
  waiting for transfers between devices  47.6 us (51%)
  Pallas kernels  21.5 us (23%)
  starting transfers between devices  18.9 us (20%)
  local copies, waits for them, and re-layouts  4.06 us (4%)
  other arithmetic  1.19 us (1%)
    ppermute x22, waiting for transfers between devices, swap(): return lax.ppermute(value, 'dp', [(i, i ^ distance) for i in range(count)])  47.6 us
    pallas_call x10, Pallas kernels, call(): pl.pallas_call(kernel, out_shape=out_shape, in_specs=[anywhere] * away +...  21.5 us
    ppermute x22, starting transfers between devices, swap(): return lax.ppermute(value, 'dp', [(i, i ^ distance) for i in range(count)])  18.9 us
    unnamed x24, local copies, waits for them, and re-layouts  3.81 us
  transfers between devices with their start and end apart: 22, of which 15 were waited for; matrix products, arithmetic and copies ran while one was open for 0% of the time, Pallas kernels for 17%

profile of v3, /device:TPU:0, one launch (start us, length us, event | category | flops | bytes accessed | tf_op | source)
XLA Modules:
  0.0 93.5 jit_solution(6074874602977428149)
XLA Ops:
  0.0 1.2 %copy-done.1 = bf16[1,128,4096]{2,1,0:T(8,128)(2,1)S(1)} copy-done((bf16[1,128,4096]{2,1,0:T(8,128)(2,1)S(1)}, bf16[1,128,4096]{2,1,0:T(8,128)(2,1)}, u32[]{:S(2)}) %copy-start.1) | copy-done | bytes 1048600
  1.2 0.9 %copy-done.3 = bf16[1,128,1024]{2,1,0:T(8,128)(2,1)S(1)} copy-done((bf16[1,128,1024]{2,1,0:T(8,128)(2,1)S(1)}, bf16[1,128,1024]{2,1,0:T(8,128)(2,1)}, u32[]{:S(2)}) %copy-start.3) | copy-done | bytes 262168
  2.2 0.9 %copy-done.4 = bf16[1,128,1024]{2,1,0:T(8,128)(2,1)S(1)} copy-done((bf16[1,128,1024]{2,1,0:T(8,128)(2,1)S(1)}, bf16[1,128,1024]{2,1,0:T(8,128)(2,1)}, u32[]{:S(2)}) %copy-start.4) | copy-done | bytes 262168
  3.1 1.6 %attention.1 = (bf16[128,1024]{1,0:T(8,128)(2,1)S(1)}, bf16[128,1024]{1,0:T(8,128)(2,1)S(1)}, bf16[2,128,1024]{2,1,0:T(8,128)(2,1)S(1)}) custom-call(bf16[128,4096]{1,0:T(8,128)(2,1)S(1)} %bitcast.12, bf16[128,1024]{1,0:T(8,128)(2,1)S(1)} %bitcast.14, bf16[128,1024]{1,0:T(8,128)(2,1)S(1)} %bitcast.15), custom_call_target="tpu_custom_call" | custom-call | flops 1 | bytes 18450000 | tf_op jit(solution)/shard_map/attention/pallas_call | solution.py:225
  4.8 0.5 collective-permute-start.3
  5.3 2.6 %collective-permute-start.1 = (bf16[128,2048]{1,0:T(8,128)(2,1)S(1)}, bf16[128,2048]{1,0:T(8,128)(2,1)S(1)}, u32[]{:S(2)}, u32[]{:S(2)}) collective-permute-start(bf16[128,2048]{1,0:T(8,128)(2,1)S(1)} %copy-done), channel_id=1, source_target_pairs={{0,4},{1,5},{2,6},{3,7},{4,0},{5,1},{6,2},{7,3},{8,12},{9,13},{10,... | collective-permute-start | bytes 1572872 | tf_op jit(solution)/shard_map/ppermute | solution.py:219
  7.9 1.5 %collective-permute-start = (bf16[128,2048]{1,0:T(8,128)(2,1)S(1)}, bf16[128,2048]{1,0:T(8,128)(2,1)S(1)}, u32[]{:S(2)}, u32[]{:S(2)}) collective-permute-start(bf16[128,2048]{1,0:T(8,128)(2,1)S(1)} %copy-done), channel_id=1, source_target_pairs={{0,2},{1,3},{2,0},{3,1},{4,6},{5,7},{6,4},{7,5},{8,10},{9,11},{10,... | collective-permute-start | bytes 1572872 | tf_op jit(solution)/shard_map/ppermute | solution.py:219
  9.5 0.6 copy-done.7
  10.1 0.2 concatenate.3.a_ref.refs_0_
  10.3 2.6 %collective-permute-start.8 = (bf16[576,128]{1,0:T(8,128)(2,1)S(1)}, bf16[576,128]{1,0:T(8,128)(2,1)S(1)}, u32[]{:S(2)}, u32[]{:S(2)}) collective-permute-start(bf16[576,128]{1,0:T(8,128)(2,1)S(1)} %concatenate.3.a_ref.refs_0_), channel_id=1, source_target_pairs={{0,16},{1,17},{2,18},{3,19},{4,20},{5,21},{6,22},{7,23},{8,24},{9,... | collective-permute-start | bytes 442376 | tf_op jit(solution)/shard_map/ppermute | solution.py:219
  13.1 1.6 %collective-permute-start.13 = (bf16[2,128,1024]{2,1,0:T(8,128)(2,1)S(1)}, bf16[2,128,1024]{2,1,0:T(8,128)(2,1)S(1)}, u32[]{:S(2)}, u32[]{:S(2)}) collective-permute-start(bf16[2,128,1024]{2,1,0:T(8,128)(2,1)S(1)} %pad_maximum_fusion), channel_id=1, source_target_pairs={{0,8},{1,9},{2,10},{3,11},{4,12},{5,13},{6,14},{7,15},{8,0},{9,1},... | collective-permute-start | bytes 1572872 | tf_op jit(solution)/shard_map/ppermute | solution.py:219
  14.7 0.3 collective-permute-start.4
  15.0 6.2 %collective-permute-done.8.b_ref.refs_1_ = bf16[576,128]{1,0:T(8,128)(2,1)S(1)} collective-permute-done((bf16[576,128]{1,0:T(8,128)(2,1)S(1)}, bf16[576,128]{1,0:T(8,128)(2,1)S(1)}, u32[]{:S(2)}, u32[]{:S(2)}) %collective-permute-start.8) | collective-permute-done | bytes 147488 | tf_op jit(solution)/shard_map/ppermute | solution.py:219
  21.3 0.6 collective-permute-done.rest_0_.refs_1_
  21.9 0.3 collective-permute-start.10
  22.3 1.7 %collective-permute-start.9 = (bf16[1152,128]{1,0:T(8,128)(2,1)S(1)}, bf16[1152,128]{1,0:T(8,128)(2,1)S(1)}, u32[]{:S(2)}, u32[]{:S(2)}) collective-permute-start(bf16[1152,128]{1,0:T(8,128)(2,1)S(1)} %join.1), channel_id=1, source_target_pairs={{0,2},{1,3},{2,0},{3,1},{4,6},{5,7},{6,4},{7,5},{8,10},{9,11},{10,... | collective-permute-start | bytes 884744 | tf_op jit(solution)/shard_map/ppermute | solution.py:219
  24.0 6.2 %collective-permute-done.10.refs_3_ = bf16[1152,128]{1,0:T(8,128)(2,1)S(1)} collective-permute-done((bf16[1152,128]{1,0:T(8,128)(2,1)S(1)}, bf16[1152,128]{1,0:T(8,128)(2,1)S(1)}, u32[]{:S(2)}, u32[]{:S(2)}) %collective-permute-start.10) | collective-permute-done | bytes 294944 | tf_op jit(solution)/shard_map/ppermute | solution.py:219
  30.2 1.6 %collective-permute-start.11 = (bf16[576,128]{1,0:T(8,128)(2,1)S(1)}, bf16[576,128]{1,0:T(8,128)(2,1)S(1)}, u32[]{:S(2)}, u32[]{:S(2)}) collective-permute-start(bf16[576,128]{1,0:T(8,128)(2,1)S(1)} %slice.16), channel_id=1, source_target_pairs={{0,2},{1,3},{2,0},{3,1},{4,6},{5,7},{6,4},{7,5},{8,10},{9,11},{10,... | collective-permute-start | bytes 442376 | tf_op jit(solution)/shard_map/ppermute | solution.py:219
  31.8 0.7 collective-permute-start.12
  32.5 3.0 %collective-permute-done.11.refs_4_ = bf16[576,128]{1,0:T(8,128)(2,1)S(1)} collective-permute-done((bf16[576,128]{1,0:T(8,128)(2,1)S(1)}, bf16[576,128]{1,0:T(8,128)(2,1)S(1)}, u32[]{:S(2)}, u32[]{:S(2)}) %collective-permute-start.11) | collective-permute-done | bytes 147488 | tf_op jit(solution)/shard_map/ppermute | solution.py:219
  35.5 1.6 %collective-permute-done.12.refs_5_ = bf16[576,128]{1,0:T(8,128)(2,1)S(1)} collective-permute-done((bf16[576,128]{1,0:T(8,128)(2,1)S(1)}, bf16[576,128]{1,0:T(8,128)(2,1)S(1)}, u32[]{:S(2)}, u32[]{:S(2)}) %collective-permute-start.12) | collective-permute-done | bytes 147488 | tf_op jit(solution)/shard_map/ppermute | solution.py:219
  37.0 0.8 collective-permute-done.13.refs_8_
  37.8 4.8 %collective-permute-done.4.refs_9_.refs_4_ = bf16[128,2048]{1,0:T(8,128)(2,1)S(1)} collective-permute-done((bf16[128,2048]{1,0:T(8,128)(2,1)S(1)}, bf16[128,2048]{1,0:T(8,128)(2,1)S(1)}, u32[]{:S(2)}, u32[]{:S(2)}) %collective-permute-start.4) | collective-permute-done | bytes 524320 | tf_op jit(solution)/shard_map/ppermute | solution.py:219
  42.6 2.1 %project.1 = (bf16[4,128,1024]{2,1,0:T(8,128)(2,1)S(1)}, f32[128,640]{1,0:T(8,128)S(1)}, f32[128,640]{1,0:T(8,128)S(1)}) custom-call(bf16[576,128]{1,0:T(8,128)(2,1)S(1)} %concatenate.3.a_ref.refs_0_, bf16[576,128]{1,0:T(8,128)(2,1)S(1)} %collective-permute-done.8.b_ref.refs_1_, bf16[1152,128]{1,0:T(8,128)(2,1)S(1)} %collective-permute-done.9.refs_2_, ...), custom_call_target="tpu_custom_call" | custom-call | flops 1 | tf_op jit(solution)/shard_map/project/pallas_call | solution.py:225
  44.8 0.6 collective-permute-start.5
  45.4 1.0 %collective-permute-done.14.b_ref = f32[128,640]{1,0:T(8,128)S(1)} collective-permute-done((f32[128,640]{1,0:T(8,128)S(1)}, f32[128,640]{1,0:T(8,128)S(1)}, u32[]{:S(2)}, u32[]{:S(2)}) %collective-permute-start.14) | collective-permute-done | bytes 327712 | tf_op jit(solution)/shard_map/ppermute | solution.py:219
  46.4 0.3 gates.1
  46.7 0.2 collective-permute-start.17
  46.9 0.7 collective-permute-start.15
  47.6 0.5 collective-permute-start.2
  48.2 0.5 collective-permute-start.6
  48.7 10.9 %collective-permute-done.5.refs_5_ = bf16[128,2048]{1,0:T(8,128)(2,1)S(1)} collective-permute-done((bf16[128,2048]{1,0:T(8,128)(2,1)S(1)}, bf16[128,2048]{1,0:T(8,128)(2,1)S(1)}, u32[]{:S(2)}, u32[]{:S(2)}) %collective-permute-start.5) | collective-permute-done | bytes 524320 | tf_op jit(solution)/shard_map/ppermute | solution.py:219
  59.6 0.5 collective-permute-start.7
  60.2 0.7 collective-permute-start.18
  60.9 0.1 combine.1.refs_6_
  61.1 1.6 %collective-permute-done.16.refs_7_ = f32[128,640]{1,0:T(8,128)S(1)} collective-permute-done((f32[128,640]{1,0:T(8,128)S(1)}, f32[128,640]{1,0:T(8,128)S(1)}, u32[]{:S(2)}, u32[]{:S(2)}) %collective-permute-start.16) | collective-permute-done | bytes 327712 | tf_op jit(solution)/shard_map/ppermute | solution.py:219
  62.7 7.2 %scan.2.refs_8_ = f32[2,128,1024]{2,1,0:T(8,128)S(1)} custom-call(bf16[576,128]{1,0:T(8,128)(2,1)S(1)} %concatenate.3.a_ref.refs_0_, bf16[576,128]{1,0:T(8,128)(2,1)S(1)} %collective-permute-done.8.b_ref.refs_1_, bf16[1152,128]{1,0:T(8,128)(2,1)S(1)} %collective-permute-done.9.refs_2_, bf16[1152,128]{1,0:T(8,128)(2,1)S(1)} %collective-permute-done.10.refs_3_, ...), custom_call_target="tpu_custom_call" | custom-call | flops 1 | bytes 29520000 | tf_op jit(solution)/shard_map/scan/pallas_call | solution.py:225
  69.9 0.5 collective-permute-done.2.refs_3_
  70.4 2.7 %collective-permute-done.7.refs_7_ = bf16[128,2048]{1,0:T(8,128)(2,1)S(1)} collective-permute-done((bf16[128,2048]{1,0:T(8,128)(2,1)S(1)}, bf16[128,2048]{1,0:T(8,128)(2,1)S(1)}, u32[]{:S(2)}, u32[]{:S(2)}) %collective-permute-start.7) | collective-permute-done | bytes 524320 | tf_op jit(solution)/shard_map/ppermute | solution.py:219
  73.0 1.5 %output.2 = (f32[128,2048]{1,0:T(8,128)S(1)}, bf16[128,2048]{1,0:T(8,128)(2,1)S(1)}) custom-call(bf16[128,2048]{1,0:T(8,128)(2,1)S(1)} %copy-done, bf16[128,2048]{1,0:T(8,128)(2,1)S(1)} %collective-permute-done.rest_0_.refs_1_, bf16[128,2048]{1,0:T(8,128)(2,1)S(1)} %collective-permute-done.1.rest_1_.refs_2_, ...), custom_call_target="tpu_custom_call" | custom-call | flops 1 | tf_op jit(solution)/shard_map/output/pallas_call | solution.py:225
  74.6 1.9 %collective-permute-done.19 = bf16[128,2048]{1,0:T(8,128)(2,1)S(1)} collective-permute-done((bf16[128,2048]{1,0:T(8,128)(2,1)S(1)}, bf16[128,2048]{1,0:T(8,128)(2,1)S(1)}, u32[]{:S(2)}, u32[]{:S(2)}) %collective-permute-start.19) | collective-permute-done | bytes 524320 | tf_op jit(solution)/shard_map/ppermute | solution.py:219
  76.5 0.1 add_convert_fusion.1.refs_9_
  76.6 1.4 %collective-permute-start.20 = (bf16[128,2048]{1,0:T(8,128)(2,1)S(1)}, bf16[128,2048]{1,0:T(8,128)(2,1)S(1)}, u32[]{:S(2)}, u32[]{:S(2)}) collective-permute-start(bf16[128,2048]{1,0:T(8,128)(2,1)S(1)} %add_convert_fusion.1.refs_9_), channel_id=1, source_target_pairs={{0,8},{1,9},{2,10},{3,11},{4,12},{5,13},{6,14},{7,15},{8,0},{9,1},... | collective-permute-start | bytes 1572872 | tf_op jit(solution)/shard_map/ppermute | solution.py:219
  78.0 7.2 %scan.3.refs_8_ = f32[2,128,1024]{2,1,0:T(8,128)S(1)} custom-call(bf16[576,128]{1,0:T(8,128)(2,1)S(1)} %concatenate.3.a_ref.refs_0_, bf16[576,128]{1,0:T(8,128)(2,1)S(1)} %collective-permute-done.8.b_ref.refs_1_, bf16[1152,128]{1,0:T(8,128)(2,1)S(1)} %collective-permute-done.9.refs_2_, bf16[1152,128]{1,0:T(8,128)(2,1)S(1)} %collective-permute-done.10.refs_3_, ...), custom_call_target="tpu_custom_call" | custom-call | flops 1 | bytes 29520000 | tf_op jit(solution)/shard_map/scan/pallas_call | solution.py:225
  85.2 1.5 %output.3 = (f32[128,2048]{1,0:T(8,128)S(1)}, bf16[128,2048]{1,0:T(8,128)(2,1)S(1)}) custom-call(bf16[128,2048]{1,0:T(8,128)(2,1)S(1)} %copy-done, bf16[128,2048]{1,0:T(8,128)(2,1)S(1)} %collective-permute-done.rest_0_.refs_1_, bf16[128,2048]{1,0:T(8,128)(2,1)S(1)} %collective-permute-done.1.rest_1_.refs_2_, ...), custom_call_target="tpu_custom_call" | custom-call | flops 1 | tf_op jit(solution)/shard_map/output/pallas_call | solution.py:225
  86.7 4.0 %collective-permute-done.20 = bf16[128,2048]{1,0:T(8,128)(2,1)S(1)} collective-permute-done((bf16[128,2048]{1,0:T(8,128)(2,1)S(1)}, bf16[128,2048]{1,0:T(8,128)(2,1)S(1)}, u32[]{:S(2)}, u32[]{:S(2)}) %collective-permute-start.20) | collective-permute-done | bytes 524320 | tf_op jit(solution)/shard_map/ppermute | solution.py:219
  90.6 1.9 %collective-permute-done.21 = bf16[128,2048]{1,0:T(8,128)(2,1)S(1)} collective-permute-done((bf16[128,2048]{1,0:T(8,128)(2,1)S(1)}, bf16[128,2048]{1,0:T(8,128)(2,1)S(1)}, u32[]{:S(2)}, u32[]{:S(2)}) %collective-permute-start.21) | collective-permute-done | bytes 524320 | tf_op jit(solution)/shard_map/ppermute | solution.py:219
  92.5 1.0 %fusion = bf16[1,128,2048]{2,1,0:T(8,128)(2,1)} fusion(bf16[128,2048]{1,0:T(8,128)(2,1)S(1)} %collective-permute-done.20, f32[128,2048]{1,0:T(8,128)S(1)} %get-tuple-element.34, bf16[128,2048]{1,0:T(8,128)(2,1)S(1)} %collective-permute-done.21), kind=kLoop, calls=%fused_computation.2 | loop fusion | flops 1310720 | bytes 2621440 | tf_op jit(solution)/shard_map/broadcast_in_dim | solution.py:562
  (40 shorter events, 0.5 us)
Async XLA Ops:
  0.0 1.2 %copy-start.1 = (bf16[1,128,4096]{2,1,0:T(8,128)(2,1)S(1)}, bf16[1,128,4096]{2,1,0:T(8,128)(2,1)}, u32[]{:S(2)}) copy-start(bf16[1,128,4096]{2,1,0:T(8,128)(2,1)} %param.12) | copy-start | bytes 3145732
  1.2 0.9 %copy-start.3 = (bf16[1,128,1024]{2,1,0:T(8,128)(2,1)S(1)}, bf16[1,128,1024]{2,1,0:T(8,128)(2,1)}, u32[]{:S(2)}) copy-start(bf16[1,128,1024]{2,1,0:T(8,128)(2,1)} %param.13) | copy-start | bytes 786436
  2.2 0.9 %copy-start.4 = (bf16[1,128,1024]{2,1,0:T(8,128)(2,1)S(1)}, bf16[1,128,1024]{2,1,0:T(8,128)(2,1)}, u32[]{:S(2)}) copy-start(bf16[1,128,1024]{2,1,0:T(8,128)(2,1)} %param.14) | copy-start | bytes 786436
  3.1 2.2 %copy-start = (bf16[128,2048]{1,0:T(8,128)(2,1)S(1)}, bf16[128,2048]{1,0:T(8,128)(2,1)}, u32[]{:S(2)}) copy-start(bf16[128,2048]{1,0:T(8,128)(2,1)} %refs_0_.3) | copy-start | bytes 1572868
  3.1 6.3 %copy-start.5 = (bf16[128,288]{0,1:T(8,128)(2,1)S(1)}, bf16[128,288]{0,1:T(8,128)(2,1)}, u32[]{:S(2)}) copy-start(bf16[128,288]{0,1:T(8,128)(2,1)} %param.18) | copy-start | bytes 221188
  3.1 6.3 %copy-start.6 = (bf16[256,128]{1,0:T(8,128)(2,1)S(1)}, bf16[256,128]{1,0:T(8,128)(2,1)}, u32[]{:S(2)}) copy-start(bf16[256,128]{1,0:T(8,128)(2,1)} %param.19) | copy-start | bytes 196612
  4.8 8.2 %collective-permute-start.3 = (bf16[2,128,1024]{2,1,0:T(8,128)(2,1)S(1)}, bf16[2,128,1024]{2,1,0:T(8,128)(2,1)S(1)}, u32[]{:S(2)}, u32[]{:S(2)}) collective-permute-start(bf16[2,128,1024]{2,1,0:T(8,128)(2,1)S(1)} %get-tuple-element.21), channel_id=1, source_target_pairs={{0,1},{1,0},{2,3},{3,2},{4,5},{5,4},{6,7},{7,6},{8,9},{9,8},{10,11... | collective-permute-start | bytes 1572872 | tf_op jit(solution)/shard_map/ppermute | solution.py:219
  5.3 16.0 %collective-permute-start.1 = (bf16[128,2048]{1,0:T(8,128)(2,1)S(1)}, bf16[128,2048]{1,0:T(8,128)(2,1)S(1)}, u32[]{:S(2)}, u32[]{:S(2)}) collective-permute-start(bf16[128,2048]{1,0:T(8,128)(2,1)S(1)} %copy-done), channel_id=1, source_target_pairs={{0,4},{1,5},{2,6},{3,7},{4,0},{5,1},{6,2},{7,3},{8,12},{9,13},{10,... | collective-permute-start | bytes 1572872 | tf_op jit(solution)/shard_map/ppermute | solution.py:219
  7.9 14.0 %collective-permute-start = (bf16[128,2048]{1,0:T(8,128)(2,1)S(1)}, bf16[128,2048]{1,0:T(8,128)(2,1)S(1)}, u32[]{:S(2)}, u32[]{:S(2)}) collective-permute-start(bf16[128,2048]{1,0:T(8,128)(2,1)S(1)} %copy-done), channel_id=1, source_target_pairs={{0,2},{1,3},{2,0},{3,1},{4,6},{5,7},{6,4},{7,5},{8,10},{9,11},{10,... | collective-permute-start | bytes 1572872 | tf_op jit(solution)/shard_map/ppermute | solution.py:219
  9.4 0.7 copy-start.7
  9.4 0.7 copy-start.8
  9.4 0.7 copy-start.9
  9.4 0.7 copy-start.10
  9.4 0.7 copy-start.11
  10.3 10.9 %collective-permute-start.8 = (bf16[576,128]{1,0:T(8,128)(2,1)S(1)}, bf16[576,128]{1,0:T(8,128)(2,1)S(1)}, u32[]{:S(2)}, u32[]{:S(2)}) collective-permute-start(bf16[576,128]{1,0:T(8,128)(2,1)S(1)} %concatenate.3.a_ref.refs_0_), channel_id=1, source_target_pairs={{0,16},{1,17},{2,18},{3,19},{4,20},{5,21},{6,22},{7,23},{8,24},{9,... | collective-permute-start | bytes 442376 | tf_op jit(solution)/shard_map/ppermute | solution.py:219
  13.1 24.7 %collective-permute-start.13 = (bf16[2,128,1024]{2,1,0:T(8,128)(2,1)S(1)}, bf16[2,128,1024]{2,1,0:T(8,128)(2,1)S(1)}, u32[]{:S(2)}, u32[]{:S(2)}) collective-permute-start(bf16[2,128,1024]{2,1,0:T(8,128)(2,1)S(1)} %pad_maximum_fusion), channel_id=1, source_target_pairs={{0,8},{1,9},{2,10},{3,11},{4,12},{5,13},{6,14},{7,15},{8,0},{9,1},... | collective-permute-start | bytes 1572872 | tf_op jit(solution)/shard_map/ppermute | solution.py:219
  14.7 27.9 %collective-permute-start.4 = (bf16[128,2048]{1,0:T(8,128)(2,1)S(1)}, bf16[128,2048]{1,0:T(8,128)(2,1)S(1)}, u32[]{:S(2)}, u32[]{:S(2)}) collective-permute-start(bf16[128,2048]{1,0:T(8,128)(2,1)S(1)} %copy-done), channel_id=1, source_target_pairs={{0,16},{1,17},{2,18},{3,19},{4,20},{5,21},{6,22},{7,23},{8,24},{9,... | collective-permute-start | bytes 1572872 | tf_op jit(solution)/shard_map/ppermute | solution.py:219
  21.9 8.3 %collective-permute-start.10 = (bf16[1152,128]{1,0:T(8,128)(2,1)S(1)}, bf16[1152,128]{1,0:T(8,128)(2,1)S(1)}, u32[]{:S(2)}, u32[]{:S(2)}) collective-permute-start(bf16[1152,128]{1,0:T(8,128)(2,1)S(1)} %join.1), channel_id=1, source_target_pairs={{0,4},{1,5},{2,6},{3,7},{4,0},{5,1},{6,2},{7,3},{8,12},{9,13},{10,... | collective-permute-start | bytes 884744 | tf_op jit(solution)/shard_map/ppermute | solution.py:219
  22.3 9.5 %collective-permute-start.9 = (bf16[1152,128]{1,0:T(8,128)(2,1)S(1)}, bf16[1152,128]{1,0:T(8,128)(2,1)S(1)}, u32[]{:S(2)}, u32[]{:S(2)}) collective-permute-start(bf16[1152,128]{1,0:T(8,128)(2,1)S(1)} %join.1), channel_id=1, source_target_pairs={{0,2},{1,3},{2,0},{3,1},{4,6},{5,7},{6,4},{7,5},{8,10},{9,11},{10,... | collective-permute-start | bytes 884744 | tf_op jit(solution)/shard_map/ppermute | solution.py:219
  30.2 5.2 %collective-permute-start.11 = (bf16[576,128]{1,0:T(8,128)(2,1)S(1)}, bf16[576,128]{1,0:T(8,128)(2,1)S(1)}, u32[]{:S(2)}, u32[]{:S(2)}) collective-permute-start(bf16[576,128]{1,0:T(8,128)(2,1)S(1)} %slice.16), channel_id=1, source_target_pairs={{0,2},{1,3},{2,0},{3,1},{4,6},{5,7},{6,4},{7,5},{8,10},{9,11},{10,... | collective-permute-start | bytes 442376 | tf_op jit(solution)/shard_map/ppermute | solution.py:219
  31.8 5.2 %collective-permute-start.12 = (bf16[576,128]{1,0:T(8,128)(2,1)S(1)}, bf16[576,128]{1,0:T(8,128)(2,1)S(1)}, u32[]{:S(2)}, u32[]{:S(2)}) collective-permute-start(bf16[576,128]{1,0:T(8,128)(2,1)S(1)} %slice.17), channel_id=1, source_target_pairs={{0,4},{1,5},{2,6},{3,7},{4,0},{5,1},{6,2},{7,3},{8,12},{9,13},{10,... | collective-permute-start | bytes 442376 | tf_op jit(solution)/shard_map/ppermute | solution.py:219
  42.6 3.8 %copy-start.2 = (bf16[1,128,4096]{2,1,0:T(8,128)(2,1)S(1)}, bf16[1,128,4096]{2,1,0:T(8,128)(2,1)}, u32[]{:S(2)}) copy-start(bf16[1,128,4096]{2,1,0:T(8,128)(2,1)} %param.15) | copy-start | bytes 3145732
  44.7 1.7 %collective-permute-start.14 = (f32[128,640]{1,0:T(8,128)S(1)}, f32[128,640]{1,0:T(8,128)S(1)}, u32[]{:S(2)}, u32[]{:S(2)}) collective-permute-start(f32[128,640]{1,0:T(8,128)S(1)} %get-tuple-element.26), channel_id=1, source_target_pairs={{0,1},{1,0},{2,3},{3,2},{4,5},{5,4},{6,7},{7,6},{8,9},{9,8},{10,11... | collective-permute-start | bytes 983048 | tf_op jit(solution)/shard_map/ppermute | solution.py:219
  44.8 14.8 %collective-permute-start.5 = (bf16[128,2048]{1,0:T(8,128)(2,1)S(1)}, bf16[128,2048]{1,0:T(8,128)(2,1)S(1)}, u32[]{:S(2)}, u32[]{:S(2)}) collective-permute-start(bf16[128,2048]{1,0:T(8,128)(2,1)S(1)} %collective-permute-done.4.refs_9_.refs_4_), channel_id=1, source_target_pairs={{0,2},{1,3},{2,0},{3,1},{4,6},{5,7},{6,4},{7,5},{8,10},{9,11},{10,... | collective-permute-start | bytes 1572872 | tf_op jit(solution)/shard_map/ppermute | solution.py:219
  46.7 13.3 %collective-permute-start.17 = (bf16[2,128,1024]{2,1,0:T(8,128)(2,1)S(1)}, bf16[2,128,1024]{2,1,0:T(8,128)(2,1)S(1)}, u32[]{:S(2)}, u32[]{:S(2)}) collective-permute-start(bf16[2,128,1024]{2,1,0:T(8,128)(2,1)S(1)} %get-tuple-element.30), channel_id=1, source_target_pairs={{0,1},{1,0},{2,3},{3,2},{4,5},{5,4},{6,7},{7,6},{8,9},{9,8},{10,11... | collective-permute-start | bytes 1572872 | tf_op jit(solution)/shard_map/ppermute | solution.py:219
  46.9 14.0 %collective-permute-start.15 = (f32[128,640]{1,0:T(8,128)S(1)}, f32[128,640]{1,0:T(8,128)S(1)}, u32[]{:S(2)}, u32[]{:S(2)}) collective-permute-start(f32[128,640]{1,0:T(8,128)S(1)} %add.20.chip_ref), channel_id=1, source_target_pairs={{0,8},{1,9},{2,10},{3,11},{4,12},{5,13},{6,14},{7,15},{8,0},{9,1},... | collective-permute-start | bytes 983048 | tf_op jit(solution)/shard_map/ppermute | solution.py:219
  47.6 22.7 %collective-permute-start.2 = (bf16[128,2048]{1,0:T(8,128)(2,1)S(1)}, bf16[128,2048]{1,0:T(8,128)(2,1)S(1)}, u32[]{:S(2)}, u32[]{:S(2)}) collective-permute-start(bf16[128,2048]{1,0:T(8,128)(2,1)S(1)} %collective-permute-done.1.rest_1_.refs_2_), channel_id=1, source_target_pairs={{0,2},{1,3},{2,0},{3,1},{4,6},{5,7},{6,4},{7,5},{8,10},{9,11},{10,... | collective-permute-start | bytes 1572872 | tf_op jit(solution)/shard_map/ppermute | solution.py:219
  48.2 22.2 %collective-permute-start.6 = (bf16[128,2048]{1,0:T(8,128)(2,1)S(1)}, bf16[128,2048]{1,0:T(8,128)(2,1)S(1)}, u32[]{:S(2)}, u32[]{:S(2)}) collective-permute-start(bf16[128,2048]{1,0:T(8,128)(2,1)S(1)} %collective-permute-done.4.refs_9_.refs_4_), channel_id=1, source_target_pairs={{0,4},{1,5},{2,6},{3,7},{4,0},{5,1},{6,2},{7,3},{8,12},{9,13},{10,... | collective-permute-start | bytes 1572872 | tf_op jit(solution)/shard_map/ppermute | solution.py:219
  59.6 13.5 %collective-permute-start.7 = (bf16[128,2048]{1,0:T(8,128)(2,1)S(1)}, bf16[128,2048]{1,0:T(8,128)(2,1)S(1)}, u32[]{:S(2)}, u32[]{:S(2)}) collective-permute-start(bf16[128,2048]{1,0:T(8,128)(2,1)S(1)} %collective-permute-done.5.refs_5_), channel_id=1, source_target_pairs={{0,4},{1,5},{2,6},{3,7},{4,0},{5,1},{6,2},{7,3},{8,12},{9,13},{10,... | collective-permute-start | bytes 1572872 | tf_op jit(solution)/shard_map/ppermute | solution.py:219
  60.2 12.9 %collective-permute-start.18 = (bf16[2,128,1024]{2,1,0:T(8,128)(2,1)S(1)}, bf16[2,128,1024]{2,1,0:T(8,128)(2,1)S(1)}, u32[]{:S(2)}, u32[]{:S(2)}) collective-permute-start(bf16[2,128,1024]{2,1,0:T(8,128)(2,1)S(1)} %pad_maximum_fusion.1), channel_id=1, source_target_pairs={{0,8},{1,9},{2,10},{3,11},{4,12},{5,13},{6,14},{7,15},{8,0},{9,1},... | collective-permute-start | bytes 1572872 | tf_op jit(solution)/shard_map/ppermute | solution.py:219
  61.0 1.7 %collective-permute-start.16 = (f32[128,640]{1,0:T(8,128)S(1)}, f32[128,640]{1,0:T(8,128)S(1)}, u32[]{:S(2)}, u32[]{:S(2)}) collective-permute-start(f32[128,640]{1,0:T(8,128)S(1)} %combine.1.refs_6_), channel_id=1, source_target_pairs={{0,1},{1,0},{2,3},{3,2},{4,5},{5,4},{6,7},{7,6},{8,9},{9,8},{10,11... | collective-permute-start | bytes 983048 | tf_op jit(solution)/shard_map/ppermute | solution.py:219
  74.5 2.0 %collective-permute-start.19 = (bf16[128,2048]{1,0:T(8,128)(2,1)S(1)}, bf16[128,2048]{1,0:T(8,128)(2,1)S(1)}, u32[]{:S(2)}, u32[]{:S(2)}) collective-permute-start(bf16[128,2048]{1,0:T(8,128)(2,1)S(1)} %get-tuple-element.32), channel_id=1, source_target_pairs={{0,1},{1,0},{2,3},{3,2},{4,5},{5,4},{6,7},{7,6},{8,9},{9,8},{10,11... | collective-permute-start | bytes 1572872 | tf_op jit(solution)/shard_map/ppermute | solution.py:219
  76.6 14.0 %collective-permute-start.20 = (bf16[128,2048]{1,0:T(8,128)(2,1)S(1)}, bf16[128,2048]{1,0:T(8,128)(2,1)S(1)}, u32[]{:S(2)}, u32[]{:S(2)}) collective-permute-start(bf16[128,2048]{1,0:T(8,128)(2,1)S(1)} %add_convert_fusion.1.refs_9_), channel_id=1, source_target_pairs={{0,8},{1,9},{2,10},{3,11},{4,12},{5,13},{6,14},{7,15},{8,0},{9,1},... | collective-permute-start | bytes 1572872 | tf_op jit(solution)/shard_map/ppermute | solution.py:219
  90.6 1.9 %collective-permute-start.21 = (bf16[128,2048]{1,0:T(8,128)(2,1)S(1)}, bf16[128,2048]{1,0:T(8,128)(2,1)S(1)}, u32[]{:S(2)}, u32[]{:S(2)}) collective-permute-start(bf16[128,2048]{1,0:T(8,128)(2,1)S(1)} %get-tuple-element.36), channel_id=1, source_target_pairs={{0,1},{1,0},{2,3},{3,2},{4,5},{5,4},{6,7},{7,6},{8,9},{9,8},{10,11... | collective-permute-start | bytes 1572872 | tf_op jit(solution)/shard_map/ppermute | solution.py:219

commit v4 on v3

--- a/solution.py
+++ b/solution.py
@@ -211,7 +211,7 @@
 MEMBERS = (1, 8)
 SLOTS = (2, 4, 16)
 COST = {"attention": 5, "project": 0, "combine": 0, "scan": 8, "output": 0}
-WAITS = {"project": (4,), "add": (), "combine": (), "scan": ()}
+WAITS = {"project": (4,), "add": (), "combine": (6,), "scan": ()}
 XW, DT, AL, MISC, PACK_ROWS = 0, 288, 544, 560, 576
 
 
@@ -492,8 +492,8 @@
     )(query[0], key[0], value[0])
     mixed = spread(*made)
     pack_z = swap(pack, bit_z, count)
-    slot_x = swap(out_proj, bit_x, count)
-    slot_y = swap(out_proj, bit_y, count)
+    slot_x = swap(after(out_proj, pack), bit_x, count)
+    slot_y = swap(after(out_proj, pack), bit_y, count)
     pack_two = local_call(join_kernel, jax.ShapeDtypeStruct((2 * PACK_ROWS, HEAD), jnp.bfloat16), "join", waits=[slot_x, slot_y])(pack, pack_z)
     pack_x = swap(pack_two, bit_x, count)
     pack_y = swap(pack_two, bit_y, count)

time: 93.7 us -> 93.7 us (level)
  transfers between devices with their start and end apart: 22 -> 22, of which waited for: 15 -> 17; matrix products, arithmetic and copies ran while one was open for 0% -> 0% of each run, Pallas kernels for 17% -> 17%
where the time goes in v4:
time: 93.7 us; the launch traced here: 93.5 us
  waiting for transfers between devices  48.4 us (52%)
  Pallas kernels  21.5 us (23%)
  starting transfers between devices  18.1 us (19%)
  local copies, waits for them, and re-layouts  4.06 us (4%)
  other arithmetic  1.19 us (1%)
    ppermute x22, waiting for transfers between devices, swap(): return lax.ppermute(value, 'dp', [(i, i ^ distance) for i in range(count)])  48.4 us
    pallas_call x10, Pallas kernels, call(): pl.pallas_call(kernel, out_shape=out_shape, in_specs=[anywhere] * away +...  21.5 us
    ppermute x22, starting transfers between devices, swap(): return lax.ppermute(value, 'dp', [(i, i ^ distance) for i in range(count)])  18.1 us
    unnamed x24, local copies, waits for them, and re-layouts  3.81 us
  transfers between devices with their start and end apart: 22, of which 17 were waited for; matrix products, arithmetic and copies ran while one was open for 0% of the time, Pallas kernels for 17%

profile of v4, /device:TPU:0, one launch (start us, length us, event | category | flops | bytes accessed | tf_op | source)
XLA Modules:
  0.0 93.5 jit_solution(5644906389164351859)
XLA Ops:
  0.0 1.2 %copy-done.1 = bf16[1,128,4096]{2,1,0:T(8,128)(2,1)S(1)} copy-done((bf16[1,128,4096]{2,1,0:T(8,128)(2,1)S(1)}, bf16[1,128,4096]{2,1,0:T(8,128)(2,1)}, u32[]{:S(2)}) %copy-start.1) | copy-done | bytes 1048600
  1.2 0.9 %copy-done.3 = bf16[1,128,1024]{2,1,0:T(8,128)(2,1)S(1)} copy-done((bf16[1,128,1024]{2,1,0:T(8,128)(2,1)S(1)}, bf16[1,128,1024]{2,1,0:T(8,128)(2,1)}, u32[]{:S(2)}) %copy-start.3) | copy-done | bytes 262168
  2.2 0.9 %copy-done.4 = bf16[1,128,1024]{2,1,0:T(8,128)(2,1)S(1)} copy-done((bf16[1,128,1024]{2,1,0:T(8,128)(2,1)S(1)}, bf16[1,128,1024]{2,1,0:T(8,128)(2,1)}, u32[]{:S(2)}) %copy-start.4) | copy-done | bytes 262168
  3.1 1.6 %attention.1 = (bf16[128,1024]{1,0:T(8,128)(2,1)S(1)}, bf16[128,1024]{1,0:T(8,128)(2,1)S(1)}, bf16[2,128,1024]{2,1,0:T(8,128)(2,1)S(1)}) custom-call(bf16[128,4096]{1,0:T(8,128)(2,1)S(1)} %bitcast.12, bf16[128,1024]{1,0:T(8,128)(2,1)S(1)} %bitcast.14, bf16[128,1024]{1,0:T(8,128)(2,1)S(1)} %bitcast.15), custom_call_target="tpu_custom_call" | custom-call | flops 1 | bytes 18450000 | tf_op jit(solution)/shard_map/attention/pallas_call | solution.py:225
  4.8 0.5 collective-permute-start.3
  5.4 0.6 copy-done.7
  6.0 0.2 concatenate.3.a_ref.refs_0_
  6.2 2.6 %collective-permute-start.1 = (bf16[128,2048]{1,0:T(8,128)(2,1)S(1)}, bf16[128,2048]{1,0:T(8,128)(2,1)S(1)}, u32[]{:S(2)}, u32[]{:S(2)}) collective-permute-start(bf16[128,2048]{1,0:T(8,128)(2,1)S(1)} %copy-done), channel_id=1, source_target_pairs={{0,4},{1,5},{2,6},{3,7},{4,0},{5,1},{6,2},{7,3},{8,12},{9,13},{10,... | collective-permute-start | bytes 1572872 | tf_op jit(solution)/shard_map/ppermute | solution.py:219
  8.8 1.5 %collective-permute-start = (bf16[128,2048]{1,0:T(8,128)(2,1)S(1)}, bf16[128,2048]{1,0:T(8,128)(2,1)S(1)}, u32[]{:S(2)}, u32[]{:S(2)}) collective-permute-start(bf16[128,2048]{1,0:T(8,128)(2,1)S(1)} %copy-done), channel_id=1, source_target_pairs={{0,2},{1,3},{2,0},{3,1},{4,6},{5,7},{6,4},{7,5},{8,10},{9,11},{10,... | collective-permute-start | bytes 1572872 | tf_op jit(solution)/shard_map/ppermute | solution.py:219
  10.3 2.6 %collective-permute-start.8 = (bf16[576,128]{1,0:T(8,128)(2,1)S(1)}, bf16[576,128]{1,0:T(8,128)(2,1)S(1)}, u32[]{:S(2)}, u32[]{:S(2)}) collective-permute-start(bf16[576,128]{1,0:T(8,128)(2,1)S(1)} %concatenate.3.a_ref.refs_0_), channel_id=1, source_target_pairs={{0,16},{1,17},{2,18},{3,19},{4,20},{5,21},{6,22},{7,23},{8,24},{9,... | collective-permute-start | bytes 442376 | tf_op jit(solution)/shard_map/ppermute | solution.py:219
  13.0 1.6 %collective-permute-start.13 = (bf16[2,128,1024]{2,1,0:T(8,128)(2,1)S(1)}, bf16[2,128,1024]{2,1,0:T(8,128)(2,1)S(1)}, u32[]{:S(2)}, u32[]{:S(2)}) collective-permute-start(bf16[2,128,1024]{2,1,0:T(8,128)(2,1)S(1)} %pad_maximum_fusion), channel_id=1, source_target_pairs={{0,8},{1,9},{2,10},{3,11},{4,12},{5,13},{6,14},{7,15},{8,0},{9,1},... | collective-permute-start | bytes 1572872 | tf_op jit(solution)/shard_map/ppermute | solution.py:219
  14.6 0.3 collective-permute-start.4
  15.0 6.2 %collective-permute-done.8.b_ref.refs_1_ = bf16[576,128]{1,0:T(8,128)(2,1)S(1)} collective-permute-done((bf16[576,128]{1,0:T(8,128)(2,1)S(1)}, bf16[576,128]{1,0:T(8,128)(2,1)S(1)}, u32[]{:S(2)}, u32[]{:S(2)}) %collective-permute-start.8) | collective-permute-done | bytes 147488 | tf_op jit(solution)/shard_map/ppermute | solution.py:219
  21.2 0.2 collective-permute-done.1.rest_1_.refs_2_
  21.4 1.5 %collective-permute-done.rest_0_.refs_1_ = bf16[128,2048]{1,0:T(8,128)(2,1)S(1)} collective-permute-done((bf16[128,2048]{1,0:T(8,128)(2,1)S(1)}, bf16[128,2048]{1,0:T(8,128)(2,1)S(1)}, u32[]{:S(2)}, u32[]{:S(2)}) %collective-permute-start) | collective-permute-done | bytes 524320 | tf_op jit(solution)/shard_map/ppermute | solution.py:219
  22.9 0.4 collective-permute-start.10
  23.3 1.6 %collective-permute-start.9 = (bf16[1152,128]{1,0:T(8,128)(2,1)S(1)}, bf16[1152,128]{1,0:T(8,128)(2,1)S(1)}, u32[]{:S(2)}, u32[]{:S(2)}) collective-permute-start(bf16[1152,128]{1,0:T(8,128)(2,1)S(1)} %join.1), channel_id=1, source_target_pairs={{0,2},{1,3},{2,0},{3,1},{4,6},{5,7},{6,4},{7,5},{8,10},{9,11},{10,... | collective-permute-start | bytes 884744 | tf_op jit(solution)/shard_map/ppermute | solution.py:219
  25.0 6.3 %collective-permute-done.10.refs_3_ = bf16[1152,128]{1,0:T(8,128)(2,1)S(1)} collective-permute-done((bf16[1152,128]{1,0:T(8,128)(2,1)S(1)}, bf16[1152,128]{1,0:T(8,128)(2,1)S(1)}, u32[]{:S(2)}, u32[]{:S(2)}) %collective-permute-start.10) | collective-permute-done | bytes 294944 | tf_op jit(solution)/shard_map/ppermute | solution.py:219
  31.3 1.6 %collective-permute-start.11 = (bf16[576,128]{1,0:T(8,128)(2,1)S(1)}, bf16[576,128]{1,0:T(8,128)(2,1)S(1)}, u32[]{:S(2)}, u32[]{:S(2)}) collective-permute-start(bf16[576,128]{1,0:T(8,128)(2,1)S(1)} %slice.16), channel_id=1, source_target_pairs={{0,2},{1,3},{2,0},{3,1},{4,6},{5,7},{6,4},{7,5},{8,10},{9,11},{10,... | collective-permute-start | bytes 442376 | tf_op jit(solution)/shard_map/ppermute | solution.py:219
  32.9 0.7 collective-permute-start.12
  33.5 3.0 %collective-permute-done.11.refs_4_ = bf16[576,128]{1,0:T(8,128)(2,1)S(1)} collective-permute-done((bf16[576,128]{1,0:T(8,128)(2,1)S(1)}, bf16[576,128]{1,0:T(8,128)(2,1)S(1)}, u32[]{:S(2)}, u32[]{:S(2)}) %collective-permute-start.11) | collective-permute-done | bytes 147488 | tf_op jit(solution)/shard_map/ppermute | solution.py:219
  36.5 1.6 %collective-permute-done.12.refs_5_ = bf16[576,128]{1,0:T(8,128)(2,1)S(1)} collective-permute-done((bf16[576,128]{1,0:T(8,128)(2,1)S(1)}, bf16[576,128]{1,0:T(8,128)(2,1)S(1)}, u32[]{:S(2)}, u32[]{:S(2)}) %collective-permute-start.12) | collective-permute-done | bytes 147488 | tf_op jit(solution)/shard_map/ppermute | solution.py:219
  38.1 4.5 %collective-permute-done.4.refs_9_.refs_4_ = bf16[128,2048]{1,0:T(8,128)(2,1)S(1)} collective-permute-done((bf16[128,2048]{1,0:T(8,128)(2,1)S(1)}, bf16[128,2048]{1,0:T(8,128)(2,1)S(1)}, u32[]{:S(2)}, u32[]{:S(2)}) %collective-permute-start.4) | collective-permute-done | bytes 524320 | tf_op jit(solution)/shard_map/ppermute | solution.py:219
  42.6 2.1 %project.1 = (bf16[4,128,1024]{2,1,0:T(8,128)(2,1)S(1)}, f32[128,640]{1,0:T(8,128)S(1)}, f32[128,640]{1,0:T(8,128)S(1)}) custom-call(bf16[576,128]{1,0:T(8,128)(2,1)S(1)} %concatenate.3.a_ref.refs_0_, bf16[576,128]{1,0:T(8,128)(2,1)S(1)} %collective-permute-done.8.b_ref.refs_1_, bf16[1152,128]{1,0:T(8,128)(2,1)S(1)} %collective-permute-done.9.refs_2_, ...), custom_call_target="tpu_custom_call" | custom-call | flops 1 | tf_op jit(solution)/shard_map/project/pallas_call | solution.py:225
  44.8 0.6 collective-permute-start.5
  45.4 1.0 %collective-permute-done.14.b_ref = f32[128,640]{1,0:T(8,128)S(1)} collective-permute-done((f32[128,640]{1,0:T(8,128)S(1)}, f32[128,640]{1,0:T(8,128)S(1)}, u32[]{:S(2)}, u32[]{:S(2)}) %collective-permute-start.14) | collective-permute-done | bytes 327712 | tf_op jit(solution)/shard_map/ppermute | solution.py:219
  46.4 0.3 gates.1
  46.7 0.2 collective-permute-start.17
  46.9 0.5 collective-permute-start.6
  47.5 0.7 collective-permute-start.15
  48.1 0.5 collective-permute-start.2
  48.7 10.9 %collective-permute-done.5.refs_5_ = bf16[128,2048]{1,0:T(8,128)(2,1)S(1)} collective-permute-done((bf16[128,2048]{1,0:T(8,128)(2,1)S(1)}, bf16[128,2048]{1,0:T(8,128)(2,1)S(1)}, u32[]{:S(2)}, u32[]{:S(2)}) %collective-permute-start.5) | collective-permute-done | bytes 524320 | tf_op jit(solution)/shard_map/ppermute | solution.py:219
  59.6 0.5 collective-permute-start.7
  60.2 0.7 collective-permute-start.18
  60.9 0.2 collective-permute-done.6.rest_0_.refs_6_
  61.3 1.6 %collective-permute-done.16.refs_7_ = f32[128,640]{1,0:T(8,128)S(1)} collective-permute-done((f32[128,640]{1,0:T(8,128)S(1)}, f32[128,640]{1,0:T(8,128)S(1)}, u32[]{:S(2)}, u32[]{:S(2)}) %collective-permute-start.16) | collective-permute-done | bytes 327712 | tf_op jit(solution)/shard_map/ppermute | solution.py:219
  62.9 7.2 %scan.2.refs_8_ = f32[2,128,1024]{2,1,0:T(8,128)S(1)} custom-call(bf16[576,128]{1,0:T(8,128)(2,1)S(1)} %concatenate.3.a_ref.refs_0_, bf16[576,128]{1,0:T(8,128)(2,1)S(1)} %collective-permute-done.8.b_ref.refs_1_, bf16[1152,128]{1,0:T(8,128)(2,1)S(1)} %collective-permute-done.9.refs_2_, bf16[1152,128]{1,0:T(8,128)(2,1)S(1)} %collective-permute-done.10.refs_3_, ...), custom_call_target="tpu_custom_call" | custom-call | flops 1 | bytes 29520000 | tf_op jit(solution)/shard_map/scan/pallas_call | solution.py:225
  70.1 0.2 collective-permute-done.2.refs_3_
  70.3 2.3 %collective-permute-done.7.refs_7_ = bf16[128,2048]{1,0:T(8,128)(2,1)S(1)} collective-permute-done((bf16[128,2048]{1,0:T(8,128)(2,1)S(1)}, bf16[128,2048]{1,0:T(8,128)(2,1)S(1)}, u32[]{:S(2)}, u32[]{:S(2)}) %collective-permute-start.7) | collective-permute-done | bytes 524320 | tf_op jit(solution)/shard_map/ppermute | solution.py:219
  72.6 0.4 collective-permute-done.18.refs_9_.refs_10_
  73.0 1.5 %output.2 = (f32[128,2048]{1,0:T(8,128)S(1)}, bf16[128,2048]{1,0:T(8,128)(2,1)S(1)}) custom-call(bf16[128,2048]{1,0:T(8,128)(2,1)S(1)} %copy-done, bf16[128,2048]{1,0:T(8,128)(2,1)S(1)} %collective-permute-done.rest_0_.refs_1_, bf16[128,2048]{1,0:T(8,128)(2,1)S(1)} %collective-permute-done.1.rest_1_.refs_2_, ...), custom_call_target="tpu_custom_call" | custom-call | flops 1 | tf_op jit(solution)/shard_map/output/pallas_call | solution.py:225
  74.5 1.9 %collective-permute-done.19 = bf16[128,2048]{1,0:T(8,128)(2,1)S(1)} collective-permute-done((bf16[128,2048]{1,0:T(8,128)(2,1)S(1)}, bf16[128,2048]{1,0:T(8,128)(2,1)S(1)}, u32[]{:S(2)}, u32[]{:S(2)}) %collective-permute-start.19) | collective-permute-done | bytes 524320 | tf_op jit(solution)/shard_map/ppermute | solution.py:219
  76.5 0.7 collective-permute-start.20
  77.3 7.2 %scan.3.refs_8_ = f32[2,128,1024]{2,1,0:T(8,128)S(1)} custom-call(bf16[576,128]{1,0:T(8,128)(2,1)S(1)} %concatenate.3.a_ref.refs_0_, bf16[576,128]{1,0:T(8,128)(2,1)S(1)} %collective-permute-done.8.b_ref.refs_1_, bf16[1152,128]{1,0:T(8,128)(2,1)S(1)} %collective-permute-done.9.refs_2_, bf16[1152,128]{1,0:T(8,128)(2,1)S(1)} %collective-permute-done.10.refs_3_, ...), custom_call_target="tpu_custom_call" | custom-call | flops 1 | bytes 29520000 | tf_op jit(solution)/shard_map/scan/pallas_call | solution.py:225
  84.4 1.5 %output.3 = (f32[128,2048]{1,0:T(8,128)S(1)}, bf16[128,2048]{1,0:T(8,128)(2,1)S(1)}) custom-call(bf16[128,2048]{1,0:T(8,128)(2,1)S(1)} %copy-done, bf16[128,2048]{1,0:T(8,128)(2,1)S(1)} %collective-permute-done.rest_0_.refs_1_, bf16[128,2048]{1,0:T(8,128)(2,1)S(1)} %collective-permute-done.1.rest_1_.refs_2_, ...), custom_call_target="tpu_custom_call" | custom-call | flops 1 | tf_op jit(solution)/shard_map/output/pallas_call | solution.py:225
  85.9 4.6 %collective-permute-done.20 = bf16[128,2048]{1,0:T(8,128)(2,1)S(1)} collective-permute-done((bf16[128,2048]{1,0:T(8,128)(2,1)S(1)}, bf16[128,2048]{1,0:T(8,128)(2,1)S(1)}, u32[]{:S(2)}, u32[]{:S(2)}) %collective-permute-start.20) | collective-permute-done | bytes 524320 | tf_op jit(solution)/shard_map/ppermute | solution.py:219
  90.6 1.9 %collective-permute-done.21 = bf16[128,2048]{1,0:T(8,128)(2,1)S(1)} collective-permute-done((bf16[128,2048]{1,0:T(8,128)(2,1)S(1)}, bf16[128,2048]{1,0:T(8,128)(2,1)S(1)}, u32[]{:S(2)}, u32[]{:S(2)}) %collective-permute-start.21) | collective-permute-done | bytes 524320 | tf_op jit(solution)/shard_map/ppermute | solution.py:219
  92.5 1.0 %fusion = bf16[1,128,2048]{2,1,0:T(8,128)(2,1)} fusion(bf16[128,2048]{1,0:T(8,128)(2,1)S(1)} %collective-permute-done.20, f32[128,2048]{1,0:T(8,128)S(1)} %get-tuple-element.36, bf16[128,2048]{1,0:T(8,128)(2,1)S(1)} %collective-permute-done.21), kind=kLoop, calls=%fused_computation.2 | loop fusion | flops 1310720 | bytes 2621440 | tf_op jit(solution)/shard_map/broadcast_in_dim | solution.py:562
  (40 shorter events, 0.7 us)
Async XLA Ops:
  0.0 1.2 %copy-start.1 = (bf16[1,128,4096]{2,1,0:T(8,128)(2,1)S(1)}, bf16[1,128,4096]{2,1,0:T(8,128)(2,1)}, u32[]{:S(2)}) copy-start(bf16[1,128,4096]{2,1,0:T(8,128)(2,1)} %param.12) | copy-start | bytes 3145732
  1.2 0.9 %copy-start.3 = (bf16[1,128,1024]{2,1,0:T(8,128)(2,1)S(1)}, bf16[1,128,1024]{2,1,0:T(8,128)(2,1)}, u32[]{:S(2)}) copy-start(bf16[1,128,1024]{2,1,0:T(8,128)(2,1)} %param.13) | copy-start | bytes 786436
  2.2 0.9 %copy-start.4 = (bf16[1,128,1024]{2,1,0:T(8,128)(2,1)S(1)}, bf16[1,128,1024]{2,1,0:T(8,128)(2,1)}, u32[]{:S(2)}) copy-start(bf16[1,128,1024]{2,1,0:T(8,128)(2,1)} %param.14) | copy-start | bytes 786436
  3.1 2.2 %copy-start.5 = (bf16[128,288]{0,1:T(8,128)(2,1)S(1)}, bf16[128,288]{0,1:T(8,128)(2,1)}, u32[]{:S(2)}) copy-start(bf16[128,288]{0,1:T(8,128)(2,1)} %param.18) | copy-start | bytes 221188
  3.1 2.2 %copy-start.6 = (bf16[256,128]{1,0:T(8,128)(2,1)S(1)}, bf16[256,128]{1,0:T(8,128)(2,1)}, u32[]{:S(2)}) copy-start(bf16[256,128]{1,0:T(8,128)(2,1)} %param.19) | copy-start | bytes 196612
  3.1 3.1 %copy-start = (bf16[128,2048]{1,0:T(8,128)(2,1)S(1)}, bf16[128,2048]{1,0:T(8,128)(2,1)}, u32[]{:S(2)}) copy-start(bf16[128,2048]{1,0:T(8,128)(2,1)} %refs_0_.3) | copy-start | bytes 1572868
  4.8 8.1 %collective-permute-start.3 = (bf16[2,128,1024]{2,1,0:T(8,128)(2,1)S(1)}, bf16[2,128,1024]{2,1,0:T(8,128)(2,1)S(1)}, u32[]{:S(2)}, u32[]{:S(2)}) collective-permute-start(bf16[2,128,1024]{2,1,0:T(8,128)(2,1)S(1)} %get-tuple-element.23), channel_id=1, source_target_pairs={{0,1},{1,0},{2,3},{3,2},{4,5},{5,4},{6,7},{7,6},{8,9},{9,8},{10,11... | collective-permute-start | bytes 1572872 | tf_op jit(solution)/shard_map/ppermute | solution.py:219
  5.3 0.7 copy-start.7
  5.3 0.7 copy-start.8
  5.3 0.7 copy-start.9
  5.3 0.7 copy-start.10
  5.3 0.7 copy-start.11
  6.2 15.2 %collective-permute-start.1 = (bf16[128,2048]{1,0:T(8,128)(2,1)S(1)}, bf16[128,2048]{1,0:T(8,128)(2,1)S(1)}, u32[]{:S(2)}, u32[]{:S(2)}) collective-permute-start(bf16[128,2048]{1,0:T(8,128)(2,1)S(1)} %copy-done), channel_id=1, source_target_pairs={{0,4},{1,5},{2,6},{3,7},{4,0},{5,1},{6,2},{7,3},{8,12},{9,13},{10,... | collective-permute-start | bytes 1572872 | tf_op jit(solution)/shard_map/ppermute | solution.py:219
  8.8 14.0 %collective-permute-start = (bf16[128,2048]{1,0:T(8,128)(2,1)S(1)}, bf16[128,2048]{1,0:T(8,128)(2,1)S(1)}, u32[]{:S(2)}, u32[]{:S(2)}) collective-permute-start(bf16[128,2048]{1,0:T(8,128)(2,1)S(1)} %copy-done), channel_id=1, source_target_pairs={{0,2},{1,3},{2,0},{3,1},{4,6},{5,7},{6,4},{7,5},{8,10},{9,11},{10,... | collective-permute-start | bytes 1572872 | tf_op jit(solution)/shard_map/ppermute | solution.py:219
  10.3 10.9 %collective-permute-start.8 = (bf16[576,128]{1,0:T(8,128)(2,1)S(1)}, bf16[576,128]{1,0:T(8,128)(2,1)S(1)}, u32[]{:S(2)}, u32[]{:S(2)}) collective-permute-start(bf16[576,128]{1,0:T(8,128)(2,1)S(1)} %concatenate.3.a_ref.refs_0_), channel_id=1, source_target_pairs={{0,16},{1,17},{2,18},{3,19},{4,20},{5,21},{6,22},{7,23},{8,24},{9,... | collective-permute-start | bytes 442376 | tf_op jit(solution)/shard_map/ppermute | solution.py:219
  13.0 25.1 %collective-permute-start.13 = (bf16[2,128,1024]{2,1,0:T(8,128)(2,1)S(1)}, bf16[2,128,1024]{2,1,0:T(8,128)(2,1)S(1)}, u32[]{:S(2)}, u32[]{:S(2)}) collective-permute-start(bf16[2,128,1024]{2,1,0:T(8,128)(2,1)S(1)} %pad_maximum_fusion), channel_id=1, source_target_pairs={{0,8},{1,9},{2,10},{3,11},{4,12},{5,13},{6,14},{7,15},{8,0},{9,1},... | collective-permute-start | bytes 1572872 | tf_op jit(solution)/shard_map/ppermute | solution.py:219
  14.6 27.9 %collective-permute-start.4 = (bf16[128,2048]{1,0:T(8,128)(2,1)S(1)}, bf16[128,2048]{1,0:T(8,128)(2,1)S(1)}, u32[]{:S(2)}, u32[]{:S(2)}) collective-permute-start(bf16[128,2048]{1,0:T(8,128)(2,1)S(1)} %copy-done), channel_id=1, source_target_pairs={{0,16},{1,17},{2,18},{3,19},{4,20},{5,21},{6,22},{7,23},{8,24},{9,... | collective-permute-start | bytes 1572872 | tf_op jit(solution)/shard_map/ppermute | solution.py:219
  22.9 8.4 %collective-permute-start.10 = (bf16[1152,128]{1,0:T(8,128)(2,1)S(1)}, bf16[1152,128]{1,0:T(8,128)(2,1)S(1)}, u32[]{:S(2)}, u32[]{:S(2)}) collective-permute-start(bf16[1152,128]{1,0:T(8,128)(2,1)S(1)} %join.1), channel_id=1, source_target_pairs={{0,4},{1,5},{2,6},{3,7},{4,0},{5,1},{6,2},{7,3},{8,12},{9,13},{10,... | collective-permute-start | bytes 884744 | tf_op jit(solution)/shard_map/ppermute | solution.py:219
  23.3 9.5 %collective-permute-start.9 = (bf16[1152,128]{1,0:T(8,128)(2,1)S(1)}, bf16[1152,128]{1,0:T(8,128)(2,1)S(1)}, u32[]{:S(2)}, u32[]{:S(2)}) collective-permute-start(bf16[1152,128]{1,0:T(8,128)(2,1)S(1)} %join.1), channel_id=1, source_target_pairs={{0,2},{1,3},{2,0},{3,1},{4,6},{5,7},{6,4},{7,5},{8,10},{9,11},{10,... | collective-permute-start | bytes 884744 | tf_op jit(solution)/shard_map/ppermute | solution.py:219
  31.3 5.2 %collective-permute-start.11 = (bf16[576,128]{1,0:T(8,128)(2,1)S(1)}, bf16[576,128]{1,0:T(8,128)(2,1)S(1)}, u32[]{:S(2)}, u32[]{:S(2)}) collective-permute-start(bf16[576,128]{1,0:T(8,128)(2,1)S(1)} %slice.16), channel_id=1, source_target_pairs={{0,2},{1,3},{2,0},{3,1},{4,6},{5,7},{6,4},{7,5},{8,10},{9,11},{10,... | collective-permute-start | bytes 442376 | tf_op jit(solution)/shard_map/ppermute | solution.py:219
  32.9 5.2 %collective-permute-start.12 = (bf16[576,128]{1,0:T(8,128)(2,1)S(1)}, bf16[576,128]{1,0:T(8,128)(2,1)S(1)}, u32[]{:S(2)}, u32[]{:S(2)}) collective-permute-start(bf16[576,128]{1,0:T(8,128)(2,1)S(1)} %slice.17), channel_id=1, source_target_pairs={{0,4},{1,5},{2,6},{3,7},{4,0},{5,1},{6,2},{7,3},{8,12},{9,13},{10,... | collective-permute-start | bytes 442376 | tf_op jit(solution)/shard_map/ppermute | solution.py:219
  42.6 3.8 %copy-start.2 = (bf16[1,128,4096]{2,1,0:T(8,128)(2,1)S(1)}, bf16[1,128,4096]{2,1,0:T(8,128)(2,1)}, u32[]{:S(2)}) copy-start(bf16[1,128,4096]{2,1,0:T(8,128)(2,1)} %param.15) | copy-start | bytes 3145732
  44.7 1.7 %collective-permute-start.14 = (f32[128,640]{1,0:T(8,128)S(1)}, f32[128,640]{1,0:T(8,128)S(1)}, u32[]{:S(2)}, u32[]{:S(2)}) collective-permute-start(f32[128,640]{1,0:T(8,128)S(1)} %get-tuple-element.28), channel_id=1, source_target_pairs={{0,1},{1,0},{2,3},{3,2},{4,5},{5,4},{6,7},{7,6},{8,9},{9,8},{10,11... | collective-permute-start | bytes 983048 | tf_op jit(solution)/shard_map/ppermute | solution.py:219
  44.8 14.8 %collective-permute-start.5 = (bf16[128,2048]{1,0:T(8,128)(2,1)S(1)}, bf16[128,2048]{1,0:T(8,128)(2,1)S(1)}, u32[]{:S(2)}, u32[]{:S(2)}) collective-permute-start(bf16[128,2048]{1,0:T(8,128)(2,1)S(1)} %collective-permute-done.4.refs_9_.refs_4_), channel_id=1, source_target_pairs={{0,2},{1,3},{2,0},{3,1},{4,6},{5,7},{6,4},{7,5},{8,10},{9,11},{10,... | collective-permute-start | bytes 1572872 | tf_op jit(solution)/shard_map/ppermute | solution.py:219
  46.7 13.3 %collective-permute-start.17 = (bf16[2,128,1024]{2,1,0:T(8,128)(2,1)S(1)}, bf16[2,128,1024]{2,1,0:T(8,128)(2,1)S(1)}, u32[]{:S(2)}, u32[]{:S(2)}) collective-permute-start(bf16[2,128,1024]{2,1,0:T(8,128)(2,1)S(1)} %get-tuple-element.32), channel_id=1, source_target_pairs={{0,1},{1,0},{2,3},{3,2},{4,5},{5,4},{6,7},{7,6},{8,9},{9,8},{10,11... | collective-permute-start | bytes 1572872 | tf_op jit(solution)/shard_map/ppermute | solution.py:219
  46.9 14.2 %collective-permute-start.6 = (bf16[128,2048]{1,0:T(8,128)(2,1)S(1)}, bf16[128,2048]{1,0:T(8,128)(2,1)S(1)}, u32[]{:S(2)}, u32[]{:S(2)}) collective-permute-start(bf16[128,2048]{1,0:T(8,128)(2,1)S(1)} %collective-permute-done.4.refs_9_.refs_4_), channel_id=1, source_target_pairs={{0,4},{1,5},{2,6},{3,7},{4,0},{5,1},{6,2},{7,3},{8,12},{9,13},{10,... | collective-permute-start | bytes 1572872 | tf_op jit(solution)/shard_map/ppermute | solution.py:219
  47.5 13.7 %collective-permute-start.15 = (f32[128,640]{1,0:T(8,128)S(1)}, f32[128,640]{1,0:T(8,128)S(1)}, u32[]{:S(2)}, u32[]{:S(2)}) collective-permute-start(f32[128,640]{1,0:T(8,128)S(1)} %add.20.chip_ref), channel_id=1, source_target_pairs={{0,8},{1,9},{2,10},{3,11},{4,12},{5,13},{6,14},{7,15},{8,0},{9,1},... | collective-permute-start | bytes 983048 | tf_op jit(solution)/shard_map/ppermute | solution.py:219
  48.1 22.2 %collective-permute-start.2 = (bf16[128,2048]{1,0:T(8,128)(2,1)S(1)}, bf16[128,2048]{1,0:T(8,128)(2,1)S(1)}, u32[]{:S(2)}, u32[]{:S(2)}) collective-permute-start(bf16[128,2048]{1,0:T(8,128)(2,1)S(1)} %collective-permute-done.1.rest_1_.refs_2_), channel_id=1, source_target_pairs={{0,2},{1,3},{2,0},{3,1},{4,6},{5,7},{6,4},{7,5},{8,10},{9,11},{10,... | collective-permute-start | bytes 1572872 | tf_op jit(solution)/shard_map/ppermute | solution.py:219
  59.6 13.0 %collective-permute-start.7 = (bf16[128,2048]{1,0:T(8,128)(2,1)S(1)}, bf16[128,2048]{1,0:T(8,128)(2,1)S(1)}, u32[]{:S(2)}, u32[]{:S(2)}) collective-permute-start(bf16[128,2048]{1,0:T(8,128)(2,1)S(1)} %collective-permute-done.5.refs_5_), channel_id=1, source_target_pairs={{0,4},{1,5},{2,6},{3,7},{4,0},{5,1},{6,2},{7,3},{8,12},{9,13},{10,... | collective-permute-start | bytes 1572872 | tf_op jit(solution)/shard_map/ppermute | solution.py:219
  60.2 12.8 %collective-permute-start.18 = (bf16[2,128,1024]{2,1,0:T(8,128)(2,1)S(1)}, bf16[2,128,1024]{2,1,0:T(8,128)(2,1)S(1)}, u32[]{:S(2)}, u32[]{:S(2)}) collective-permute-start(bf16[2,128,1024]{2,1,0:T(8,128)(2,1)S(1)} %pad_maximum_fusion.1), channel_id=1, source_target_pairs={{0,8},{1,9},{2,10},{3,11},{4,12},{5,13},{6,14},{7,15},{8,0},{9,1},... | collective-permute-start | bytes 1572872 | tf_op jit(solution)/shard_map/ppermute | solution.py:219
  61.2 1.7 %collective-permute-start.16 = (f32[128,640]{1,0:T(8,128)S(1)}, f32[128,640]{1,0:T(8,128)S(1)}, u32[]{:S(2)}, u32[]{:S(2)}) collective-permute-start(f32[128,640]{1,0:T(8,128)S(1)} %combine.1.refs_6_), channel_id=1, source_target_pairs={{0,1},{1,0},{2,3},{3,2},{4,5},{5,4},{6,7},{7,6},{8,9},{9,8},{10,11... | collective-permute-start | bytes 983048 | tf_op jit(solution)/shard_map/ppermute | solution.py:219
  74.4 2.0 %collective-permute-start.19 = (bf16[128,2048]{1,0:T(8,128)(2,1)S(1)}, bf16[128,2048]{1,0:T(8,128)(2,1)S(1)}, u32[]{:S(2)}, u32[]{:S(2)}) collective-permute-start(bf16[128,2048]{1,0:T(8,128)(2,1)S(1)} %get-tuple-element.34), channel_id=1, source_target_pairs={{0,1},{1,0},{2,3},{3,2},{4,5},{5,4},{6,7},{7,6},{8,9},{9,8},{10,11... | collective-permute-start | bytes 1572872 | tf_op jit(solution)/shard_map/ppermute | solution.py:219
  76.5 14.0 %collective-permute-start.20 = (bf16[128,2048]{1,0:T(8,128)(2,1)S(1)}, bf16[128,2048]{1,0:T(8,128)(2,1)S(1)}, u32[]{:S(2)}, u32[]{:S(2)}) collective-permute-start(bf16[128,2048]{1,0:T(8,128)(2,1)S(1)} %add_convert_fusion.1.refs_9_), channel_id=1, source_target_pairs={{0,8},{1,9},{2,10},{3,11},{4,12},{5,13},{6,14},{7,15},{8,0},{9,1},... | collective-permute-start | bytes 1572872 | tf_op jit(solution)/shard_map/ppermute | solution.py:219
  90.6 1.9 %collective-permute-start.21 = (bf16[128,2048]{1,0:T(8,128)(2,1)S(1)}, bf16[128,2048]{1,0:T(8,128)(2,1)S(1)}, u32[]{:S(2)}, u32[]{:S(2)}) collective-permute-start(bf16[128,2048]{1,0:T(8,128)(2,1)S(1)} %get-tuple-element.38), channel_id=1, source_target_pairs={{0,1},{1,0},{2,3},{3,2},{4,5},{5,4},{6,7},{7,6},{8,9},{9,8},{10,11... | collective-permute-start | bytes 1572872 | tf_op jit(solution)/shard_map/ppermute | solution.py:219
